TPU v7x, 512 devices: a whole 4x4x16 slice. The times are simulated.
512 devices in a mesh: grp: 2 (over x_hi), seq: 32 (over x_lo, z), head: 8 (over y, core).
Axes of the slice: x: 4 (x_hi: 2, x_lo: 2; x = x_hi * 2 + x_lo), y: 4, z: 16, core: 2. Of those that a mesh axis runs over, the one named last changes fastest.
Arguments:
- features: bfloat16 [2, 32, 16, 32, 512], P('grp', 'seq', 'head'), may hold values from -6 to 6
- conv_weight: bfloat16 [3, 3, 3, 512, 16], replicated, may hold values from -0.0546875 to 0.0546875
- conv_bias: float32 [16], replicated, may hold values from -3 to 3
- token_order: int32 [4096], P('seq'), may hold values from 0 to 4095, each once
- embed_weight: bfloat16 [64, 3072], replicated, may hold values from -0.75 to 0.75
- norm_gain: float32 [3072], replicated, may hold values from 0.1 to 1.9
- qkv_weight: bfloat16 [3072, 3, 2048], P('seq', None, 'head'), may hold values from -0.109375 to 0.109375
- grad_out: bfloat16 [2, 4096, 2048], P('grp', 'seq', 'head'), may hold values from -6 to 6
Outputs:
- attended: bfloat16 [2, 4096, 2048], P('grp', 'seq', 'head')
- embed_grad: float32 [64, 3072], P(None, 'head')
All inputs are finite; a program needn't handle non-finite values.
Results may differ from a plain program's by a relative error of at most 0.0052.
Values may be sent and summed in bfloat16 or wider, within the bound.
No kernel may reach another device: no remote copies, remote signals or barrier semaphores. Data moves between devices by JAX's collectives and lax.ppermute only.
A program may use at most 64 MiB of HBM per device.

v0:
```python
import jax
import jax.numpy as jnp
from jax import lax
from jax.sharding import Mesh
from jax.sharding import PartitionSpec as P

D = 3072
HEAD_DIM = 64
SEQ = ("seq_0", "seq_1")
HEAD = ("head_0", "head_1")
GRP_SEQ = ("grp", "seq_0", "seq_1")


def shifted(value, axis, steps):
    count = lax.axis_size(axis)
    leading, last = (max(0, -steps), min(count, count - steps))
    return lax.ppermute(value, axis, [(source, source + steps) for source in range(leading, last)])


def extended(block, sides, width):
    for axis, dim in sides:
        count = lax.axis_size(axis)
        forward = [(i, i + 1) for i in range(count - 1)]
        backward = [(target, source) for source, target in forward]
        low = lax.ppermute(
            lax.slice_in_dim(block, block.shape[dim] - width, None, axis=dim), axis, forward
        )
        high = lax.ppermute(lax.slice_in_dim(block, 0, width, axis=dim), axis, backward)
        block = jnp.concatenate([low, block, high], axis=dim)
    return block


def from_everyone(array, axis):
    copies = jnp.broadcast_to(array, (lax.axis_size(axis), *array.shape))
    return lax.all_to_all(copies, axis, split_axis=0, concat_axis=0, tiled=True)


def joined_along(blocks, dim):
    lengths = list(blocks.shape[1:])
    lengths[dim] *= blocks.shape[0]
    return jnp.moveaxis(blocks, 0, dim).reshape(lengths)


def gather_axes(array, axes, dim):
    far, near = axes
    leading = from_everyone(array, far)
    blocks = jnp.swapaxes(from_everyone(leading, near), 0, 1)
    return joined_along(blocks.reshape(-1, *array.shape), dim)


def side_by_side(arrays, axis, dim, along):
    widths = [a.shape[along] for a in arrays]
    both = jnp.concatenate(arrays, axis=along)
    result = lax.all_gather(both, axis, axis=dim, tiled=True)
    return tuple(jnp.split(result, [sum(widths[:k]) for k in range(1, len(widths))], axis=along))


def split_up(array, dim, devices):
    before, after = (array.shape[:dim], array.shape[dim + 1 :])
    return jnp.moveaxis(array.reshape(*before, devices, -1, *after), dim, 0)


def sent_and_summed(array, axis, dim):
    devices = lax.axis_size(axis)
    blocks = lax.all_to_all(split_up(array, dim, devices), axis, 0, 0, tiled=True)
    return jnp.sum(blocks.astype(jnp.float32), axis=0)


def taken_together(array, axis):
    everything = from_everyone(array, axis)
    return jnp.sum(everything, axis=0)


def sent_and_summed_2(array, axis, dim):
    blocks = split_up(array, dim, lax.axis_size(axis))
    arrived = lax.all_to_all(blocks, axis, split_axis=0, concat_axis=0, tiled=True)
    return arrived.sum(axis=0)


def padded_to(lines, devices):
    spare = -lines.shape[0] % devices
    if not spare:
        return lines
    return jnp.concatenate([lines, jnp.zeros((spare, *lines.shape[1:]), lines.dtype)])


def gather_directly(array, axis, dim):
    return joined_along(from_everyone(array, axis), dim)


def nested_sum(array, axes):
    lines = array.reshape(-1, array.shape[-1])
    own = sent_and_summed_2(padded_to(lines, lax.axis_size(axes)), axes, 0)
    whole = gather_directly(own, axes, 0)
    return whole[: len(lines)].reshape(array.shape)


def patchify(latent):
    frames, rows, columns, channels = latent.shape
    blocks = latent.reshape(frames, rows // 2, 2, columns // 2, 2, channels)
    blocks = jnp.transpose(blocks, (0, 1, 3, 2, 4, 5))
    return blocks.reshape(frames * (rows // 2) * (columns // 2), 4 * channels)


def encode_tile(tile, conv_weight, conv_bias):
    frames, rows, columns, channels = tile.shape
    hops = (frames + 1) // frames
    earlier = []
    for hop in range(hops, 0, -1):
        earlier.append(shifted(tile, SEQ, hop))
    stacked = jnp.concatenate(earlier + [tile], axis=0)
    padded = extended(stacked, ((HEAD, 1),), 1)
    padded = jnp.pad(padded, ((0, 0), (0, 0), (1, 1), (0, 0)))
    total = jnp.zeros((frames * rows * columns, conv_weight.shape[-1]), jnp.float32) + conv_bias
    for a in range(3):
        for b in range(3):
            for e in range(3):
                piece = padded[a : a + frames, b : b + rows, e : e + columns].reshape(-1, channels)
                total = total + jnp.dot(
                    piece, conv_weight[a, b, e], preferred_element_type=jnp.float32
                )
    return total.astype(jnp.bfloat16).reshape(frames, rows, columns, conv_weight.shape[-1])


def head_major(matrix, head_local):
    count = matrix.shape[0]
    return jnp.transpose(matrix.reshape(count, head_local, HEAD_DIM), (1, 0, 2))


def row_major(stacked):
    heads_here, count, size = stacked.shape
    return jnp.transpose(stacked, (1, 0, 2)).reshape(count, heads_here * size)


def head_forward(operands):
    query, keys, values, cotan = operands
    factor = HEAD_DIM ** (-0.5)
    scores = jnp.dot(query, keys.T, preferred_element_type=jnp.float32) * factor
    top = jnp.max(scores, axis=-1, keepdims=True)
    lse = top + jnp.log(jnp.sum(jnp.exp(scores - top), axis=-1, keepdims=True))
    probs = jnp.exp(scores - lse)
    probs_low = probs.astype(jnp.bfloat16)
    output = jnp.dot(probs_low, values, preferred_element_type=jnp.float32).astype(jnp.bfloat16)
    delta = jnp.sum(cotan.astype(jnp.float32) * output.astype(jnp.float32), axis=-1, keepdims=True)
    dprob = jnp.dot(cotan, values.T, preferred_element_type=jnp.float32)
    dscore = (probs * (dprob - delta)).astype(jnp.bfloat16)
    grad_q = jnp.dot(dscore, keys, preferred_element_type=jnp.float32) * factor
    return (output, lse[:, 0], delta[:, 0], grad_q)


def head_backward(operands):
    query, cotan, lse_piece, delta_piece, own_keys, own_values = operands
    factor = HEAD_DIM ** (-0.5)
    scores = jnp.dot(query, own_keys.T, preferred_element_type=jnp.float32) * factor
    probs = jnp.exp(scores - lse_piece[:, None])
    value_add = jnp.dot(probs.astype(jnp.bfloat16).T, cotan, preferred_element_type=jnp.float32)
    dprob = jnp.dot(cotan, own_values.T, preferred_element_type=jnp.float32)
    dscore = (probs * (dprob - delta_piece[:, None])).astype(jnp.bfloat16)
    key_add = jnp.dot(dscore.T, query, preferred_element_type=jnp.float32)
    return (key_add, value_add)


def per_device(
    features, conv_weight, conv_bias, token_order, embed_weight, norm_gain, qkv_weight, grad_out
):
    tile = encode_tile(features[0], conv_weight, conv_bias)
    frames, rows, columns, channels = tile.shape
    every = gather_axes(tile[None], (("seq_0", "seq_1"), ("head_0", "head_1")), 0)
    seq_count = lax.axis_size(SEQ)
    head_count = lax.axis_size(HEAD)
    every = every.reshape(seq_count, head_count, frames, rows, columns, channels)
    every = jnp.transpose(every, (0, 2, 1, 3, 4, 5))
    whole = every.reshape(seq_count * frames, head_count * rows, columns, channels)
    patches = patchify(whole)
    tokens = jnp.take(patches, token_order, axis=0)
    local_rows = tokens.shape[0]
    mixed = jnp.dot(tokens, embed_weight, preferred_element_type=jnp.float32)
    inverse = lax.rsqrt(jnp.mean(mixed * mixed, axis=-1, keepdims=True) + 1e-06)
    normal = mixed * inverse
    hidden = (normal * norm_gain).astype(jnp.bfloat16)
    full_weight = lax.all_gather(qkv_weight, SEQ, axis=0, tiled=True)
    local_width = full_weight.shape[2]
    head_local = local_width // HEAD_DIM
    flat_weight = full_weight.reshape(D, 3 * local_width)
    proj = jnp.dot(hidden, flat_weight, preferred_element_type=jnp.float32).astype(jnp.bfloat16)
    proj = proj.reshape(local_rows, 3, local_width)
    query = proj[:, 0]
    keys_all, values_all = side_by_side((proj[:, 1], proj[:, 2]), SEQ, 0, 1)
    cotan = grad_out[0]
    output_h, lse_h, delta_h, grad_q_h = lax.map(
        head_forward,
        (
            head_major(query, head_local),
            head_major(keys_all, head_local),
            head_major(values_all, head_local),
            head_major(cotan, head_local),
        ),
    )
    output = row_major(output_h)
    grad_q = row_major(grad_q_h)
    lse_all, delta_all = side_by_side((jnp.transpose(lse_h), jnp.transpose(delta_h)), SEQ, 0, 1)
    own_keys = head_major(proj[:, 1], head_local)
    own_values = head_major(proj[:, 2], head_local)
    query_piece, cotan_piece = side_by_side((query, cotan), SEQ, 0, 1)
    lse_piece = jnp.transpose(lse_all)
    delta_piece = jnp.transpose(delta_all)
    key_add, value_add = lax.map(
        head_backward,
        (
            head_major(query_piece, head_local),
            head_major(cotan_piece, head_local),
            lse_piece,
            delta_piece,
            own_keys,
            own_values,
        ),
    )
    grad_k = row_major(key_add * HEAD_DIM ** (-0.5))
    grad_v = row_major(value_add)
    grads = (
        jnp.stack([grad_q, grad_k, grad_v], axis=1)
        .reshape(local_rows, 3 * local_width)
        .astype(jnp.bfloat16)
    )
    back_part = lax.dot_general(
        grads, flat_weight, (((1,), (1,)), ((), ())), preferred_element_type=jnp.float32
    )
    head_count_d = lax.axis_size(HEAD)
    width_dev = D // head_count_d
    start_col = lax.axis_index(HEAD) * width_dev
    normal_own = lax.dynamic_slice_in_dim(normal, start_col, width_dev, 1)
    gain_own = lax.dynamic_slice_in_dim(norm_gain, start_col, width_dev, 0)
    back_own = sent_and_summed(back_part.astype(jnp.bfloat16), HEAD, 1)
    scaled_own = back_own * gain_own
    inner_part = jnp.sum(scaled_own * normal_own, axis=-1, keepdims=True)
    inner = taken_together(inner_part, HEAD) / D
    dmixed_own = inverse * (scaled_own - normal_own * inner)
    embed_part = jnp.dot(
        tokens.astype(jnp.float32).T,
        dmixed_own,
        preferred_element_type=jnp.float32,
        precision=lax.Precision.HIGHEST,
    )
    embed_grad = nested_sum(embed_part, GRP_SEQ)
    attended = output.reshape(1, local_rows, local_width)
    return (attended, embed_grad)


def solution(mesh):
    torus = Mesh(
        mesh.devices.reshape(mesh.shape["grp"], 2, 16, 4, 2),
        ("grp", "seq_0", "seq_1", "head_0", "head_1"),
    )
    return jax.shard_map(
        per_device,
        mesh=torus,
        in_specs=(
            P("grp", SEQ, HEAD, None, None),
            P(),
            P(),
            P(SEQ),
            P(),
            P(),
            P(SEQ, None, HEAD),
            P("grp", SEQ, HEAD),
        ),
        out_specs=(P("grp", SEQ, HEAD), P(None, HEAD)),
        check_vma=False,
    )
```

profile of v0, /device:TPU:32, one launch (start us, length us, event | category | flops | bytes accessed | tf_op | source)
XLA Modules:
  0.0 568.4 jit_solution(3382214532136301586)
XLA Ops:
  7.2 5.3 collective-permute-start
  12.6 5.0 collective-permute-start.1
  32.4 28.4 %all_to_all.33 = bf16[32,2,512]{2,1,0:T(2,128)(2,1)S(1)} all-to-all(bf16[32,2,512]{2,1,0:T(2,128)(2,1)S(1)} %reshape.224), channel_id=1, replica_groups=mesh['grp'=2,'seq_0'=2,'seq_1'=16,'head_0'=4,'head_1'=2] {'seq_0','seq_1'}, dimensions={0} | all-to-all | bytes 131072 | tf_op jit(solution)/shard_map/all_to_all | solution.py:35
  64.6 7.4 %all-to-all-start.1 = ((bf16[8,2,16384]{2,1,0:T(2,128)(2,1)}), bf16[8,2,16384]{2,1,0:T(2,128)(2,1)S(1)}, u32[]{:S(2)}, u32[]{:S(2)}) async-start(bf16[8,2,16384]{2,1,0:T(2,128)(2,1)} %reshape.226), calls=%async_computation.1 | async-start | bytes 1048576 | tf_op jit(solution)/shard_map/all_to_all | solution.py:35
  72.1 10.3 %all-to-all-done.1 = bf16[8,2,16384]{2,1,0:T(2,128)(2,1)S(1)} async-done(((bf16[8,2,16384]{2,1,0:T(2,128)(2,1)}), bf16[8,2,16384]{2,1,0:T(2,128)(2,1)S(1)}, u32[]{:S(2)}, u32[]{:S(2)}) %all-to-all-start.1) | async-done | bytes 524320 | tf_op jit(solution)/shard_map/all_to_all | solution.py:35
  83.4 9.7 %copy.86 = bf16[32,8,16,2,2,16]{5,4,3,2,1,0:T(2,128)(2,1)} copy(bf16[32,8,16,2,2,16]{0,5,4,2,3,1:T(8,128)(2,1)S(1)} %bitcast.364) | data formatting | bytes 1048576 | tf_op jit(solution)/shard_map/reshape | solution.py:102
  93.1 8.0 %reshape.223 = bf16[4096,64]{1,0:T(8,128)(2,1)S(1)} reshape(bf16[32,8,16,2,2,16]{5,4,3,2,1,0:T(2,128)(2,1)} %copy.86) | data formatting | bytes 1048576 | tf_op jit(solution)/shard_map/reshape | solution.py:102
  102.5 63.6 %all-gather.4.cloned.1.call-done = bf16[3072,3,256]{2,0,1:T(8,128)(2,1)} async-done(((bf16[96,3,256]{2,0,1:T(8,128)(2,1)}), bf16[3072,3,256]{2,0,1:T(8,128)(2,1)}) %all-gather.4.cloned.1.call-update) | async-done | bytes 4718608 | tf_op jit(solution)/shard_map/all_gather | solution.py:181
  166.1 6.7 %copy.67 = bf16[3072,3,256]{0,2,1:T(8,128)(2,1)} copy(bf16[3072,3,256]{2,0,1:T(8,128)(2,1)} %all-gather.4.cloned.1.call-done) | data formatting | bytes 9437184 | tf_op jit(solution)/shard_map/all_gather | solution.py:181
  172.8 4.0 convolution_convert_fusion.1
  178.9 135.1 %all-gather.6.cloned.1.call-done = bf16[4096,512]{0,1:T(8,128)(2,1)} async-done(((bf16[128,512]{0,1:T(8,128)(2,1)}), bf16[4096,512]{0,1:T(8,128)(2,1)}) %all-gather.6.cloned.1.call-update) | async-done | bytes 4194320 | tf_op jit(solution)/shard_map/all_gather | solution.py:54
  314.0 4.6 fusion.160
  318.6 23.7 %while.30 = (s32[]{:T(128)}, bf16[4,128,64]{1,2,0:T(8,128)(2,1)S(1)}, f32[4,128]{1,0:T(4,128)S(1)}, f32[4,128]{1,0:T(4,128)S(1)}, bf16[4,128,64]{1,2,0:T(8,128)(...) while((s32[]{:T(128)}, ...), condition=%wide.region_5.6_spmd.clone, body=%wide.region_1.0_spmd.sunk.clone | while | flops 273727232 | bytes 10628201 | solution.py:190
  342.4 60.1 %all_gather.15 = f32[4096,8]{0,1:T(8,128)S(1)} all-gather(f32[128,8]{0,1:T(8,128)S(1)} %pad_maximum_fusion.13), channel_id=1, replica_groups=mesh['grp'=2,'seq_0'=2,'seq_1'=16,'head_0'=4,'head_1'=2] {'seq_0','seq_1'}, dimensions={0}, use_global_device_ids=true | all-gather | bytes 135168 | tf_op jit(solution)/shard_map/all_gather | solution.py:54
  402.5 52.2 %all-gather.8.cloned.1.call-done = bf16[4096,512]{0,1:T(8,128)(2,1)} async-done(((bf16[128,512]{0,1:T(8,128)(2,1)}), bf16[4096,512]{0,1:T(8,128)(2,1)}) %all-gather.8.cloned.1.call-update) | async-done | bytes 4194320 | tf_op jit(solution)/shard_map/all_gather | solution.py:54
  454.7 4.8 fusion.159
  459.5 22.7 %while.31 = (s32[]{:T(128)}, f32[4,128,64]{1,2,0:T(8,128)S(1)}, bf16[4,128,64]{1,2,0:T(8,128)(2,1)S(1)}, bf16[4,4096,64]{1,2,0:T(8,128)(2,1)}, bf16[4,128,64]{1,...) while((s32[]{:T(128)}, f32[4,128,64]{1,2,0:T(8,128)S(1)}, ...), condition=%wide.region_7.8_spmd.clone, body=%wide.region_6.7_spmd.sunk.clone | while | flops 271581184 | bytes 8589409 | solution.py:207
  482.5 4.0 fusion.61
  487.5 4.1 all-to-all-start.2
  491.6 13.1 %all-to-all-done.2 = bf16[8,128,384]{2,1,0:T(8,128)(2,1)S(1)} async-done(((bf16[8,128,384]{2,1,0:T(8,128)(2,1)}), bf16[8,128,384]{2,1,0:T(8,128)(2,1)S(1)}, u32[]{:S(2)}, u32[]{:S(2)}) %all-to-all-start.2) | async-done | bytes 786464 | tf_op jit(solution)/shard_map/all_to_all | solution.py:65
  505.9 7.6 %all_to_all.34 = f32[8,128,1]{1,2,0:T(1,128)S(1)} all-to-all(f32[8,128,1]{1,2,0:T(1,128)S(1)} %broadcast_in_dim.62), channel_id=1, replica_groups=mesh['grp'=2,'seq_0'=2,'seq_1'=16,'head_0'=4,'head_1'=2] {'head_0','head..., dimensions={0} | all-to-all | bytes 8192 | tf_op jit(solution)/shard_map/all_to_all | solution.py:35
  514.9 25.3 %all_to_all.35 = f32[64,1,384]{2,1,0:T(1,128)S(1)} all-to-all(f32[64,1,384]{2,1,0:T(1,128)S(1)} %copy.84), channel_id=1, replica_groups=mesh['grp'=2,'seq_0'=2,'seq_1'=16,'head_0'=4,'head_1'=2] {'grp','seq_0',..., dimensions={0} | all-to-all | bytes 196608 | tf_op jit(solution)/shard_map/all_to_all | solution.py:76
  541.0 5.8 %all-to-all-start.5 = ((f32[64,1,384]{2,1,0:T(1,128)}), f32[64,1,384]{2,1,0:T(1,128)S(1)}, u32[]{:S(2)}, u32[]{:S(2)}) async-start(f32[64,1,384]{2,1,0:T(1,128)} %broadcast_in_dim.63), calls=%async_computation.5 | async-start | bytes 196608 | tf_op jit(solution)/shard_map/all_to_all | solution.py:35
  547.5 13.7 %all-to-all-done.5 = f32[64,1,384]{2,1,0:T(1,128)S(1)} async-done(((f32[64,1,384]{2,1,0:T(1,128)}), f32[64,1,384]{2,1,0:T(1,128)S(1)}, u32[]{:S(2)}, u32[]{:S(2)}) %all-to-all-start.5) | async-done | bytes 98336 | tf_op jit(solution)/shard_map/all_to_all | solution.py:35
  (156 shorter events, 75.2 us)
Async XLA Ops:
  7.2 94.6 %copy-start = (bf16[64,3072]{1,0:T(8,128)(2,1)S(1)}, bf16[64,3072]{1,0:T(8,128)(2,1)}, u32[]{:S(2)}) copy-start(bf16[64,3072]{1,0:T(8,128)(2,1)} %param.16) | copy-start | bytes 1179652
  7.2 21.0 %copy-start.2 = (bf16[1,1,2,32,512]{4,3,2,1,0:T(8,128)(2,1)S(1)}, bf16[1,1,2,32,512]{4,3,2,1,0:T(8,128)(2,1)}, u32[]{:S(2)}) copy-start(bf16[1,1,2,32,512]{4,3,2,1,0:T(8,128)(2,1)} %param.12) | copy-start | bytes 196612
  7.2 158.9 %all-gather.4.cloned.1.call-start = ((), (), s32[]{:S(2)}) async-start(), calls=%async_computation.6 | async-start | bytes 4866048 | tf_op jit(solution)/shard_map/all_gather | solution.py:181
  7.2 10.4 %collective-permute-start = (bf16[1,2,32,512]{3,2,1,0:T(8,128)(2,1)}, bf16[1,2,32,512]{3,2,1,0:T(8,128)(2,1)S(1)}, u32[]{:S(2)}, u32[]{:S(2)}) collective-permute-start(bf16[1,2,32,512]{3,2,1,0:T(8,128)(2,1)} %bitcast.368), channel_id=1, source_target_pairs={{0,16},{8,24},{16,32},{24,40},{32,48},{40,56},{48,64},{56,72},{64,... | collective-permute-start | bytes 196616 | tf_op jit(solution)/shard_map/ppermute | solution.py:17
  12.6 7.2 %collective-permute-start.1 = (bf16[1,2,32,512]{3,2,1,0:T(8,128)(2,1)}, bf16[1,2,32,512]{3,2,1,0:T(8,128)(2,1)S(1)}, u32[]{:S(2)}, u32[]{:S(2)}) collective-permute-start(bf16[1,2,32,512]{3,2,1,0:T(8,128)(2,1)} %bitcast.369), channel_id=1, source_target_pairs={{0,8},{8,16},{16,24},{24,32},{32,40},{40,48},{48,56},{56,64},{64,7... | collective-permute-start | bytes 196616 | tf_op jit(solution)/shard_map/ppermute | solution.py:17
  20.7 2.8 collective-permute-start.2
  22.0 6.4 %copy-start.3 = (bf16[3,3,3,512,16]{3,4,2,1,0:T(8,128)(2,1)S(1)}, bf16[3,3,3,512,16]{3,4,2,1,0:T(8,128)(2,1)}, u32[]{:S(2)}) copy-start(bf16[3,3,3,512,16]{3,4,2,1,0:T(8,128)(2,1)} %param.13) | copy-start | bytes 1327108
  22.0 5.1 collective-permute-start.3
  24.3 5.2 copy-start.6
  61.9 10.2 %copy-start.7 = (s32[128]{0:T(128)S(1)}, s32[128]{0:T(128)}, u32[]{:S(2)}) copy-start(s32[128]{0:T(128)} %param.15) | copy-start | bytes 1540
  64.6 17.8 %all-to-all-start.1 = ((bf16[8,2,16384]{2,1,0:T(2,128)(2,1)}), bf16[8,2,16384]{2,1,0:T(2,128)(2,1)S(1)}, u32[]{:S(2)}, u32[]{:S(2)}) async-start(bf16[8,2,16384]{2,1,0:T(2,128)(2,1)} %reshape.226), calls=%async_computation.1 | async-start | bytes 1048576 | tf_op jit(solution)/shard_map/all_to_all | solution.py:35
  72.0 242.0 %all-gather.6.cloned.1.call-start = ((), (), s32[]{:S(2)}) async-start(), calls=%async_computation.7 | async-start | bytes 4325376 | tf_op jit(solution)/shard_map/all_gather | solution.py:54
  102.5 70.3 %copy-start.1 = (f32[128,3072]{1,0:T(8,128)}, f32[128,3072]{1,0:T(8,128)S(1)}, u32[]{:S(2)}) copy-start(f32[128,3072]{1,0:T(8,128)S(1)} %broadcast_multiply_fusion) | copy-start | bytes 4718596
  102.5 70.3 %copy-start.5 = (f32[3072]{0:T(1024)S(1)}, f32[3072]{0:T(1024)}, u32[]{:S(2)}) copy-start(f32[3072]{0:T(1024)} %param.17) | copy-start | bytes 36868
  172.8 5.2 copy-start.4
  177.8 276.9 %all-gather.8.cloned.1.call-start = ((), (), s32[]{:S(2)}) async-start(), calls=%async_computation.8 | async-start | bytes 4325376 | tf_op jit(solution)/shard_map/all_gather | solution.py:54
  487.5 17.3 %all-to-all-start.2 = ((bf16[8,128,384]{2,1,0:T(8,128)(2,1)}), bf16[8,128,384]{2,1,0:T(8,128)(2,1)S(1)}, u32[]{:S(2)}, u32[]{:S(2)}) async-start(bf16[8,128,384]{2,1,0:T(8,128)(2,1)} %bitcast.294), calls=%async_computation.2 | async-start | bytes 1572864 | tf_op jit(solution)/shard_map/all_to_all | solution.py:65
  541.0 20.2 %all-to-all-start.5 = ((f32[64,1,384]{2,1,0:T(1,128)}), f32[64,1,384]{2,1,0:T(1,128)S(1)}, u32[]{:S(2)}, u32[]{:S(2)}) async-start(f32[64,1,384]{2,1,0:T(1,128)} %broadcast_in_dim.63), calls=%async_computation.5 | async-start | bytes 196608 | tf_op jit(solution)/shard_map/all_to_all | solution.py:35
Sparse Core Ops, SparseCore 0:
  22.1 143.9 all-gather.3
  177.9 136.0 all-gather.5
  316.0 138.6 all-gather.7
where the time goes:
time: 570 us; the launch traced here: 568 us
  waiting for transfers between devices  293 us (51%)
  blocking collectives  121 us (21%)
  matrix products  57.2 us (10%)
  local copies, waits for them, and re-layouts  44.1 us (8%)
  starting transfers between devices  30.7 us (5%)
  between operations  14.2 us (2%)
  other arithmetic  7.52 us (1%)
    all_gather x2, waiting for transfers between devices, side_by_side(): result = lax.all_gather(both, axis, axis=dim, tiled=True)  187 us
    all_gather x1, waiting for transfers between devices, per_device(): full_weight = lax.all_gather(qkv_weight, SEQ, axis=0, tiled=True)  63.6 us
    all_gather x1, blocking collectives, side_by_side(): result = lax.all_gather(both, axis, axis=dim, tiled=True)  60.1 us
    all_to_all x2, blocking collectives, from_everyone(): return lax.all_to_all(copies, axis, split_axis=0, concat_axis=0, tiled=True)  36 us
    all_to_all x1, blocking collectives, sent_and_summed_2(): lax.all_to_all(blocks, axis, split_axis=0, concat_axis=0, tiled=True)  25.3 us
    all_to_all x2, waiting for transfers between devices, from_everyone(): return lax.all_to_all(copies, axis, split_axis=0, concat_axis=0, tiled=True)  23.9 us
    reshape x2, local copies, waits for them, and re-layouts, patchify(): return blocks.reshape(frames * (rows // 2) * (columns // 2), 4 * channels)  17.6 us
    all_to_all x2, starting transfers between devices, from_everyone(): return lax.all_to_all(copies, axis, split_axis=0, concat_axis=0, tiled=True)  13.2 us
  transfers between devices with their start and end apart: 10, of which 8 were waited for; matrix products, arithmetic and copies ran while one was open for 11% of the time, Pallas kernels for 0%

commit v1 on v0

v1 whole, which is shorter than its diff:
```python
import jax
import jax.numpy as jnp
from jax import lax
from jax.experimental import pallas as pl
from jax.experimental.pallas import tpu as pltpu
from jax.sharding import Mesh
from jax.sharding import PartitionSpec as P

D = 3072
HEAD_DIM = 64
FEAT = 64
SEQ = ("seq_0", "seq_1")
HEAD = ("head_0", "head_1")
PLANE = ("head_0", "head_1", "grp", "seq_0")
F32 = jnp.float32
BF16 = jnp.bfloat16
CHUNK = 512
HIGHEST = lax.Precision.HIGHEST


def shifted(value, axis, steps):
    count = lax.axis_size(axis)
    leading, last = (max(0, -steps), min(count, count - steps))
    return lax.ppermute(value, axis, [(source, source + steps) for source in range(leading, last)])


def extended(block, axis, dim, width):
    count = lax.axis_size(axis)
    forward = [(i, i + 1) for i in range(count - 1)]
    backward = [(target, source) for source, target in forward]
    low = lax.ppermute(
        lax.slice_in_dim(block, block.shape[dim] - width, None, axis=dim), axis, forward
    )
    high = lax.ppermute(lax.slice_in_dim(block, 0, width, axis=dim), axis, backward)
    return jnp.concatenate([low, block, high], axis=dim)


def from_everyone(array, axis):
    copies = jnp.broadcast_to(array, (lax.axis_size(axis), *array.shape))
    return lax.all_to_all(copies, axis, split_axis=0, concat_axis=0, tiled=True)


def encode_tile(tile, conv_weight, conv_bias):
    frames, rows, columns, channels = tile.shape
    earlier = [shifted(tile, SEQ, hop) for hop in (2, 1)]
    stacked = jnp.concatenate(earlier + [tile], axis=0)
    padded = extended(stacked, HEAD, 1, 1)
    padded = jnp.pad(padded, ((0, 0), (0, 0), (1, 1), (0, 0)))
    total = jnp.zeros((frames * rows * columns, conv_weight.shape[-1]), F32) + conv_bias
    for a in range(3):
        for b in range(3):
            for e in range(3):
                piece = padded[a : a + frames, b : b + rows, e : e + columns].reshape(-1, channels)
                total = total + jnp.dot(piece, conv_weight[a, b, e], preferred_element_type=F32)
    return total.astype(BF16).reshape(frames, rows, columns, conv_weight.shape[-1])


def two(x):
    high = x.astype(BF16)
    return high, (x - high.astype(F32)).astype(BF16)


def three(x):
    high, rest = x.astype(BF16), None
    rest = x - high.astype(F32)
    mid = rest.astype(BF16)
    return high, mid, (rest - mid.astype(F32)).astype(BF16)


def mm(a, b, dims=((1,), (0,)), precision=None):
    return lax.dot_general(a, b, (dims, ((), ())), preferred_element_type=F32, precision=precision)


NT = ((1,), (1,))
TN = ((0,), (0,))


def attention_kernel(
    x_ref, mt_ref, gram_ref, row_ref, half_ref, cot_ref,
    out_ref, at_ref, b_ref,
    both, keys, scores, probs, csum, query, qsum,
):
    head = pl.program_id(0)
    heads = pl.num_programs(0)
    pairs = x_ref.shape[0]
    factor = HEAD_DIM**-0.5
    zero = jnp.zeros((FEAT, FEAT), BF16)

    @pl.when(head == 0)
    def _():
        x = x_ref[...]
        pieces = [
            jnp.concatenate(
                [jnp.concatenate([g, zero], axis=1), jnp.concatenate([zero, g], axis=1)], axis=0
            )
            for g in three(gram_ref[...])
        ]
        y = (mm(x, pieces[2]) + mm(x, pieces[1])) + mm(x, pieces[0])
        lane_i = lax.broadcasted_iota(jnp.int32, (2 * FEAT, 2 * FEAT), 0) // FEAT
        lane_j = lax.broadcasted_iota(jnp.int32, (2 * FEAT, 2 * FEAT), 1) // FEAT
        ones = (lane_i == lane_j).astype(F32).astype(BF16)
        z = three(y * x.astype(F32))
        square = (mm(z[2], ones) + mm(z[1], ones)) + mm(z[0], ones)
        normed = x.astype(F32) * lax.rsqrt(jnp.maximum(square, 0.0) + 1e-06)
        high, low = two(normed)
        both[:, : 2 * FEAT] = high
        both[:, 2 * FEAT :] = low
        csum[...] = jnp.zeros_like(csum)
        qsum[...] = jnp.zeros_like(qsum)
        hot = lax.broadcasted_iota(jnp.int32, (row_ref.shape[0], pairs), 1) == row_ref[...]
        got = mm(hot.astype(F32).astype(BF16), both[...])
        second = half_ref[...] == 1
        for k in range(2):
            piece = got[:, 2 * FEAT * k : 2 * FEAT * (k + 1)]
            query[:, FEAT * k : FEAT * (k + 1)] = jnp.where(
                second, piece[:, FEAT:], piece[:, :FEAT]
            ).astype(BF16)

    pair, odd = head // 2, head % 2

    def weight(t):
        block = mt_ref[pl.ds(pl.multiple_of(t * 2 * FEAT + pair * FEAT, FEAT), FEAT), :]
        return jnp.where(odd == 1, block[:, FEAT:], block[:, :FEAT])

    w_q, w_k, w_v = weight(0), weight(1), weight(2)

    def stacked(pick):
        rows = []
        for w in (w_k, w_v):
            m = pick(w)
            rows.append(jnp.concatenate([m, zero], axis=1))
            rows.append(jnp.concatenate([zero, m], axis=1))
        return jnp.concatenate(rows, axis=0)

    main = stacked(lambda w: two(w)[0])
    rest = stacked(lambda w: two(w)[1])
    keys[...] = (
        mm(jnp.concatenate([main, main], axis=1), both[...], NT)
        + mm(rest, both[:, : 2 * FEAT], NT)
    ).astype(BF16)

    q_high, q_low = query[:, :FEAT], query[:, FEAT:]
    wq_high, wq_low = two(w_q)
    q = (mm(q_high, wq_high, NT) + (mm(q_high, wq_low, NT) + mm(q_low, wq_high, NT))).astype(BF16)
    q_scaled = (q.astype(F32) * factor).astype(BF16)
    cot = cot_ref[0]
    count = q.shape[0]

    top = jnp.full((count, 128), -jnp.inf, F32)
    for part in range(2):
        for c in range(0, pairs, CHUNK):
            s = mm(q_scaled, keys[part * FEAT : (part + 1) * FEAT, c : c + CHUNK])
            scores[:, part * pairs + c : part * pairs + c + CHUNK] = s
            for k in range(0, CHUNK, 128):
                top = jnp.maximum(top, s[:, k : k + 128])
    top = jnp.max(top, axis=1, keepdims=True)

    total = jnp.zeros((count, 128), F32)
    mixed = [jnp.zeros((count, 4 * FEAT), F32) for _ in range(2)]
    for part in range(2):
        for c in range(0, pairs, CHUNK):
            at = part * pairs + c
            p = jnp.exp(scores[:, at : at + CHUNK] - top)
            probs[:, at : at + CHUNK] = p
            for k in range(0, CHUNK, 128):
                total = total + p[:, k : k + 128]
            mixed[part] = mixed[part] + mm(p.astype(BF16), both[c : c + CHUNK, :])

    def folded(m):
        return (m[0][:, :FEAT] + m[0][:, 2 * FEAT : 3 * FEAT]) + (
            m[1][:, FEAT : 2 * FEAT] + m[1][:, 3 * FEAT :]
        )

    inverse = 1.0 / jnp.sum(total, axis=1, keepdims=True)
    value = folded(mixed) * inverse
    out = mm(value, w_v, NT, HIGHEST).astype(BF16)
    out_ref[0] = out
    delta = jnp.sum(cot.astype(F32) * out.astype(F32), axis=1, keepdims=True)

    mixed = [jnp.zeros((count, 4 * FEAT), F32) for _ in range(2)]
    for part in range(2):
        for c in range(0, pairs, CHUNK):
            at = part * pairs + c
            dp = mm(cot, keys[(2 + part) * FEAT : (3 + part) * FEAT, c : c + CHUNK])
            p = probs[:, at : at + CHUNK] * inverse
            ds = p * (dp - delta)
            mixed[part] = mixed[part] + mm(ds.astype(BF16), both[c : c + CHUNK, :])
            both_sides = ds * scores[:, at : at + CHUNK] + p * dp
            csum[:, at : at + CHUNK] += jnp.sum(both_sides.reshape(count // 8, 8, CHUNK), axis=0)
    grad = folded(mixed)
    dq = mm(grad, w_k, NT, HIGHEST) * factor
    q32 = q.astype(F32)
    qsum[...] += jnp.broadcast_to(jnp.sum(dq * q32, axis=1, keepdims=True), qsum.shape)
    own = q_high.astype(F32) + q_low.astype(F32)
    a_q = mm(dq, own, TN, HIGHEST)
    a_k = mm(q_scaled.astype(F32), grad, TN, HIGHEST)
    a_v = mm(cot.astype(F32), value, TN, HIGHEST)
    for t, a in enumerate((a_q, a_k, a_v)):
        rows = pl.ds(pl.multiple_of(t * 2 * FEAT + pair * FEAT, FEAT), FEAT)

        @pl.when(odd == 0)
        def _():
            at_ref[rows, :FEAT] = a

        @pl.when(odd == 1)
        def _():
            at_ref[rows, FEAT:] = a

    @pl.when(head == heads - 1)
    def _():
        eye_i = lax.broadcasted_iota(jnp.int32, (2 * FEAT, 2 * FEAT), 0)
        eye_j = lax.broadcasted_iota(jnp.int32, (2 * FEAT, 2 * FEAT), 1)
        eye = (eye_i == eye_j).astype(F32).astype(BF16)
        high = both[:, : 2 * FEAT]
        turned = mm(eye, high, NT)
        c_all = jnp.sum(csum[...], axis=0, keepdims=True)
        weighted = jnp.concatenate(
            [turned[:FEAT] * c_all[:, :pairs], turned[FEAT:] * c_all[:, pairs:]], axis=0
        )
        full = mm(weighted.astype(BF16), high)
        own_part = mm(own * qsum[:, :FEAT], own, TN, HIGHEST)
        b_ref[...] = ((full[:FEAT, :FEAT] + full[FEAT:, FEAT:]) + own_part) * (1.0 / D)


def attention(x, mt, gram, row, half, cot):
    heads, count, _ = cot.shape
    pairs = x.shape[0]
    whole = lambda *shape: pl.BlockSpec(shape, lambda i: (0,) * len(shape))
    per_head = pl.BlockSpec((1, count, HEAD_DIM), lambda i: (i, 0, 0))
    return pl.pallas_call(
        attention_kernel,
        grid=(heads,),
        in_specs=[
            whole(*x.shape), whole(*mt.shape), whole(*gram.shape),
            whole(*row.shape), whole(*half.shape), per_head,
        ],
        out_specs=[per_head, whole(*mt.shape), whole(*gram.shape)],
        out_shape=[
            jax.ShapeDtypeStruct(cot.shape, BF16),
            jax.ShapeDtypeStruct(mt.shape, F32),
            jax.ShapeDtypeStruct(gram.shape, F32),
        ],
        scratch_shapes=[
            pltpu.VMEM((pairs, 4 * FEAT), BF16),
            pltpu.VMEM((4 * FEAT, pairs), BF16),
            pltpu.VMEM((count, 2 * pairs), F32),
            pltpu.VMEM((count, 2 * pairs), F32),
            pltpu.VMEM((8, 2 * pairs), F32),
            pltpu.VMEM((count, 2 * FEAT), BF16),
            pltpu.VMEM((count, 128), F32),
        ],
        compiler_params=pltpu.CompilerParams(
            dimension_semantics=("arbitrary",), vmem_limit_bytes=48 * 1024 * 1024
        ),
        name="attention",
    )(x, mt, gram, row, half, cot)


def per_device(
    features, conv_weight, conv_bias, token_order, embed_weight, norm_gain, qkv_weight, grad_out
):
    seq_count = lax.axis_size(SEQ)
    depth, _, width = qkv_weight.shape
    heads = width // HEAD_DIM
    rows = 3 * (heads // 2) * HEAD_DIM
    rows_each = rows // seq_count

    w = qkv_weight.reshape(depth, 3, heads // 2, 2, HEAD_DIM)
    w = jnp.transpose(w, (1, 2, 4, 3, 0)).reshape(seq_count, rows_each * 2, depth)
    w_slice = lax.all_to_all(w, SEQ, 0, 0, tiled=True)
    embed32 = embed_weight.astype(F32)
    gained = jnp.concatenate(two(embed32 * norm_gain), axis=0).reshape(2 * FEAT, seq_count, depth)
    m_slice = lax.dot_general(
        w_slice, gained, (((0, 2), (1, 2)), ((), ())), preferred_element_type=F32
    )
    m_slice = (m_slice[:, :FEAT] + m_slice[:, FEAT:]).reshape(rows_each, 2 * FEAT)
    mt = from_everyone(m_slice, SEQ).reshape(rows, 2 * FEAT)
    gram = lax.dot_general(
        embed_weight, embed_weight, (((1,), (1,)), ((), ())), preferred_element_type=F32
    ) * (1.0 / D)

    tile = encode_tile(features[0], conv_weight, conv_bias)
    _, _, columns, channels = tile.shape
    patch = jnp.transpose(tile.reshape(2, columns // 2, 2, channels), (1, 0, 2, 3))
    patch = patch.reshape(2, columns // 4, FEAT)
    patch = jnp.transpose(patch, (1, 0, 2)).reshape(columns // 4, 2 * FEAT)
    every = from_everyone(from_everyone(patch, SEQ), HEAD)
    every = every.reshape(-1, 2 * FEAT)

    per_patch_row = columns // 4
    head_count = lax.axis_size(HEAD)
    j = token_order % (2 * per_patch_row)
    i = (token_order // (2 * per_patch_row)) % head_count
    f = token_order // (2 * per_patch_row * head_count)
    row = (i * seq_count + f) * per_patch_row + j % per_patch_row
    half = j // per_patch_row

    cot = jnp.transpose(grad_out[0].reshape(-1, heads, HEAD_DIM), (1, 0, 2))
    out, at, b = attention(every, mt, gram, row[:, None], half[:, None], cot)
    attended = jnp.transpose(out, (1, 0, 2)).reshape(1, -1, width)

    at = lax.all_to_all(at.reshape(seq_count, rows_each, 2 * FEAT), SEQ, 0, 0, tiled=True)
    a_slice = jnp.sum(at, axis=0).reshape(rows_each * 2, FEAT)
    a_both = jnp.concatenate(two(a_slice), axis=1)
    t = lax.dot_general(
        a_both, w_slice, (((0,), (1,)), ((), ())), preferred_element_type=F32
    )
    t = t[:FEAT] + t[FEAT:]
    second = jnp.dot(b, embed32, preferred_element_type=F32, precision=HIGHEST)
    t = t * norm_gain.reshape(seq_count, depth) - second.reshape(FEAT, seq_count, depth)
    t = jnp.transpose(t, (1, 0, 2)).astype(BF16)
    t = lax.all_to_all(t, PLANE, 0, 0, tiled=True)
    t = jnp.sum(t.astype(F32), axis=0)
    t = jnp.sum(from_everyone(t, "seq_1"), axis=0)
    t = from_everyone(t, ("grp", "seq_0"))
    embed_grad = jnp.transpose(t, (1, 0, 2)).reshape(FEAT, -1)
    return (attended, embed_grad)


def solution(mesh):
    torus = Mesh(
        mesh.devices.reshape(mesh.shape["grp"], 2, 16, 4, 2),
        ("grp", "seq_0", "seq_1", "head_0", "head_1"),
    )
    return jax.shard_map(
        per_device,
        mesh=torus,
        in_specs=(
            P("grp", SEQ, HEAD, None, None),
            P(),
            P(),
            P(SEQ),
            P(),
            P(),
            P(SEQ, None, HEAD),
            P("grp", SEQ, HEAD),
        ),
        out_specs=(P("grp", SEQ, HEAD), P(None, HEAD)),
        check_vma=False,
    )
```

time: 570 us -> 219 us (0.38)
  waiting for transfers between devices: 293 us -> 78.4 us
  blocking collectives: 121 us -> 50.2 us
  matrix products: 57.2 us -> 5.46 us
  local copies, waits for them, and re-layouts: 44.1 us -> 9.24 us
  starting transfers between devices: 30.7 us -> 52.7 us
  Pallas kernels: 0 us -> 18.4 us
  between operations: 14.2 us -> 1.01 us
    all_gather x3 -> x0, waiting for transfers between devices: 251 us -> none  [the longest x2 187 us: side_by_side(): result = lax.all_gather(both, axis, axis=dim, tiled=True)]
    all_gather x1 -> x0, blocking collectives: 60.1 us -> none  [side_by_side(): result = lax.all_gather(both, axis, axis=dim, tiled=True)]
    dot_general x55 -> x31, matrix products: 57.2 us -> 5.46 us  [the longest x27 3.55 us: encode_tile(): jnp.dot(piece, conv_weight[a, b, e], preferred_element_type=F32)]
    all_to_all x2 -> x4, waiting for transfers between devices: 23.9 us -> 49 us  [from_everyone(): return lax.all_to_all(copies, axis, split_axis=0, concat_axis=0, tiled=True)]
    pallas_call x0 -> x1, Pallas kernels: none -> 18.4 us  [attention(): pl.pallas_call(attention_kernel, grid=(heads,), in_specs=[whole(*x.shape)...]
    reshape x4 -> x7, local copies, waits for them, and re-layouts: 18.7 us -> 1.82 us  [the longest x1 0.76 us: per_device(): embed_grad = jnp.transpose(t, (1, 0, 2)).reshape(FEAT, -1)]
    all_to_all x1 -> x2, starting transfers between devices: 4.09 us -> 17.5 us  [the longest x1 12.4 us: per_device(): w_slice = lax.all_to_all(w, SEQ, 0, 0, tiled=True)]
    all_to_all x1 -> x2, waiting for transfers between devices: 13.1 us -> 26.2 us  [the longest x1 20.2 us: per_device(): lax.all_to_all(at.reshape(seq_count, rows_each, 2 * FEAT), SEQ, 0, 0, til...]
  transfers between devices with their start and end apart: 10 -> 10, of which waited for: 8 -> 7; matrix products, arithmetic and copies ran while one was open for 11% -> 5% of each run, Pallas kernels for 0% -> 0%
where the time goes in v1:
time: 219 us; the launch traced here: 218 us
  waiting for transfers between devices  78.4 us (36%)
  starting transfers between devices  52.7 us (24%)
  blocking collectives  50.2 us (23%)
  Pallas kernels  18.4 us (8%)
  local copies, waits for them, and re-layouts  9.24 us (4%)
  matrix products  5.46 us (2%)
  other arithmetic  2.68 us (1%)
    all_to_all x4, waiting for transfers between devices, from_everyone(): return lax.all_to_all(copies, axis, split_axis=0, concat_axis=0, tiled=True)  49 us
    all_to_all x1, blocking collectives, from_everyone(): return lax.all_to_all(copies, axis, split_axis=0, concat_axis=0, tiled=True)  33.6 us
    all_to_all x4, starting transfers between devices, from_everyone(): return lax.all_to_all(copies, axis, split_axis=0, concat_axis=0, tiled=True)  22.2 us
    all_to_all x1, waiting for transfers between devices, per_device(): lax.all_to_all(at.reshape(seq_count, rows_each, 2 * FEAT), SEQ, 0, 0, til...  20.2 us
    pallas_call x1, Pallas kernels, attention(): pl.pallas_call(attention_kernel, grid=(heads,), in_specs=[whole(*x.shape)...  18.4 us
    all_to_all x1, blocking collectives, per_device(): t = lax.all_to_all(t, PLANE, 0, 0, tiled=True)  16.5 us
    all_to_all x1, starting transfers between devices, per_device(): w_slice = lax.all_to_all(w, SEQ, 0, 0, tiled=True)  12.4 us
    ppermute x2, starting transfers between devices, shifted(): lax.ppermute(value, axis, [(source, source + steps) for source in range(l...  10.3 us
  transfers between devices with their start and end apart: 10, of which 7 were waited for; matrix products, arithmetic and copies ran while one was open for 5% of the time, Pallas kernels for 0%

profile of v1, /device:TPU:32, one launch (start us, length us, event | category | flops | bytes accessed | tf_op | source)
XLA Modules:
  0.0 218.1 jit_solution(8699058440493456453)
XLA Ops:
  0.6 4.0 %collective-permute-start.1 = (bf16[1,2,32,512]{3,2,1,0:T(8,128)(2,1)}, bf16[1,2,32,512]{3,2,1,0:T(8,128)(2,1)S(1)}, u32[]{:S(2)}, u32[]{:S(2)}) collective-permute-start(bf16[1,2,32,512]{3,2,1,0:T(8,128)(2,1)} %bitcast.178), channel_id=1, source_target_pairs={{0,8},{8,16},{16,24},{24,32},{32,40},{40,48},{48,56},{56,64},{64,7... | collective-permute-start | bytes 196616 | tf_op jit(solution)/shard_map/ppermute | solution.py:24
  4.6 6.4 %collective-permute-start = (bf16[1,2,32,512]{3,2,1,0:T(8,128)(2,1)}, bf16[1,2,32,512]{3,2,1,0:T(8,128)(2,1)S(1)}, u32[]{:S(2)}, u32[]{:S(2)}) collective-permute-start(bf16[1,2,32,512]{3,2,1,0:T(8,128)(2,1)} %bitcast.179), channel_id=1, source_target_pairs={{0,16},{8,24},{16,32},{24,40},{32,48},{40,56},{48,64},{56,72},{64,... | collective-permute-start | bytes 196616 | tf_op jit(solution)/shard_map/ppermute | solution.py:24
  11.0 1.1 copy.77
  12.1 0.9 copy.78
  13.0 12.4 %all-to-all-start.2 = ((bf16[32,24,96]{2,1,0:T(8,128)(2,1)}), bf16[32,24,96]{2,1,0:T(8,128)(2,1)S(1)}, u32[]{:S(2)}, u32[]{:S(2)}) async-start(bf16[32,24,96]{2,1,0:T(8,128)(2,1)} %bitcast.2), calls=%async_computation.2 | async-start | bytes 393216 | tf_op jit(solution)/shard_map/all_to_all | solution.py:270
  25.3 1.1 fusion.14
  26.6 1.3 collective-permute-start.2
  27.9 1.3 collective-permute-start.3
  29.6 3.2 %collective-permute-done.3 = bf16[3,1,32,512]{3,2,1,0:T(8,128)(2,1)S(1)} collective-permute-done((bf16[3,1,32,512]{3,2,1,0:T(8,128)(2,1)S(1)}, bf16[3,1,32,512]{3,2,1,0:T(8,128)(2,1)S(1)}, u32[]{:S(2)}, u32[]{:S(2)}) %collective-permute-start.3) | collective-permute-done | bytes 98336 | tf_op jit(solution)/shard_map/ppermute | solution.py:34
  37.3 6.0 %all-to-all-done.2 = bf16[32,24,96]{2,1,0:T(8,128)(2,1)S(1)} async-done(((bf16[32,24,96]{2,1,0:T(8,128)(2,1)}), bf16[32,24,96]{2,1,0:T(8,128)(2,1)S(1)}, u32[]{:S(2)}, u32[]{:S(2)}) %all-to-all-start.2) | async-done | bytes 147488 | tf_op jit(solution)/shard_map/all_to_all | solution.py:270
  43.9 7.1 %all-to-all-start = ((bf16[32,8,128]{2,1,0:T(8,128)(2,1)}), bf16[32,8,128]{2,1,0:T(8,128)(2,1)S(1)}, u32[]{:S(2)}, u32[]{:S(2)}) async-start(bf16[32,8,128]{2,1,0:T(8,128)(2,1)} %broadcast_in_dim.23), calls=%async_computation | async-start | bytes 131072 | tf_op jit(solution)/shard_map/all_to_all | solution.py:40
  51.5 12.7 %all-to-all-done = bf16[32,8,128]{2,1,0:T(8,128)(2,1)S(1)} async-done(((bf16[32,8,128]{2,1,0:T(8,128)(2,1)}), bf16[32,8,128]{2,1,0:T(8,128)(2,1)S(1)}, u32[]{:S(2)}, u32[]{:S(2)}) %all-to-all-start) | async-done | bytes 65568 | tf_op jit(solution)/shard_map/all_to_all | solution.py:40
  64.9 5.0 %all-to-all-start.3 = ((f32[32,12,128]{2,1,0:T(8,128)}), f32[32,12,128]{2,1,0:T(8,128)S(1)}, u32[]{:S(2)}, u32[]{:S(2)}) async-start(f32[32,12,128]{2,1,0:T(8,128)} %broadcast_in_dim.25), calls=%async_computation.3 | async-start | bytes 524288 | tf_op jit(solution)/shard_map/all_to_all | solution.py:40
  70.0 21.6 %all-to-all-done.3 = f32[32,12,128]{2,1,0:T(8,128)S(1)} async-done(((f32[32,12,128]{2,1,0:T(8,128)}), f32[32,12,128]{2,1,0:T(8,128)S(1)}, u32[]{:S(2)}, u32[]{:S(2)}) %all-to-all-start.3) | async-done | bytes 196640 | tf_op jit(solution)/shard_map/all_to_all | solution.py:40
  92.5 6.8 %all-to-all-start.1 = ((bf16[8,32,8,128]{3,2,1,0:T(8,128)(2,1)}), bf16[8,32,8,128]{3,2,1,0:T(8,128)(2,1)S(1)}, u32[]{:S(2)}, u32[]{:S(2)}) async-start(bf16[8,32,8,128]{3,2,1,0:T(8,128)(2,1)} %broadcast_in_dim.24), calls=%async_computation.1 | async-start | bytes 1048576 | tf_op jit(solution)/shard_map/all_to_all | solution.py:40
  100.1 9.5 %all-to-all-done.1 = bf16[8,32,8,128]{3,2,1,0:T(8,128)(2,1)S(1)} async-done(((bf16[8,32,8,128]{3,2,1,0:T(8,128)(2,1)}), bf16[8,32,8,128]{3,2,1,0:T(8,128)(2,1)S(1)}, u32[]{:S(2)}, u32[]{:S(2)}) %all-to-all-start.1) | async-done | bytes 524320 | tf_op jit(solution)/shard_map/all_to_all | solution.py:40
  109.6 18.4 %attention.1 = (bf16[4,128,64]{2,1,0:T(8,128)(2,1)S(1)}, f32[384,128]{1,0:T(8,128)S(1)}, f32[64,64]{1,0:T(8,128)S(1)}) custom-call(bf16[2048,128]{1,0:T(8,128)(2,1)S(1)} %bitcast.173, f32[384,128]{1,0:T(8,128)S(1)} %reshape.162.mt_ref, f32[64,64]{1,0:T(8,128)S(1)} %convolution_multiply_fusion.gram_ref, s32[128,1]{1,0:T(8,128)S(1)} %copy.81.row_ref, ...), custom_call_target="tpu_custom_call" | custom-call | tf_op jit(solution)/shard_map/attention/pallas_call | solution.py:230
  128.8 5.1 %all-to-all-start.4 = ((f32[32,12,128]{2,1,0:T(8,128)}), f32[32,12,128]{2,1,0:T(8,128)S(1)}, u32[]{:S(2)}, u32[]{:S(2)}) async-start(f32[32,12,128]{2,1,0:T(8,128)} %reshape.164), calls=%async_computation.4 | async-start | bytes 524288 | tf_op jit(solution)/shard_map/all_to_all | solution.py:302
  134.0 0.9 fusion.94
  134.9 20.2 %all-to-all-done.4 = f32[32,12,128]{2,1,0:T(8,128)S(1)} async-done(((f32[32,12,128]{2,1,0:T(8,128)}), f32[32,12,128]{2,1,0:T(8,128)S(1)}, u32[]{:S(2)}, u32[]{:S(2)}) %all-to-all-start.4) | async-done | bytes 196640 | tf_op jit(solution)/shard_map/all_to_all | solution.py:302
  156.9 16.5 %all_to_all.40 = bf16[32,64,96]{2,1,0:T(8,128)(2,1)S(1)} all-to-all(bf16[32,64,96]{2,1,0:T(8,128)(2,1)S(1)} %copy.85), channel_id=1, replica_groups=mesh['grp'=2,'seq_0'=2,'seq_1'=16,'head_0'=4,'head_1'=2] {'head_0','head..., dimensions={0} | all-to-all | bytes 786432 | tf_op jit(solution)/shard_map/all_to_all | solution.py:312
  173.6 33.6 %all_to_all.41 = f32[16,64,96]{2,1,0:T(8,128)S(1)} all-to-all(f32[16,64,96]{2,1,0:T(8,128)S(1)} %broadcast_in_dim.28), channel_id=1, replica_groups=mesh['grp'=2,'seq_0'=2,'seq_1'=16,'head_0'=4,'head_1'=2] {'seq_1'}, dimensions={0} | all-to-all | bytes 786432 | tf_op jit(solution)/shard_map/all_to_all | solution.py:40
  207.9 3.3 %all-to-all-start.7 = ((f32[4,64,96]{2,1,0:T(8,128)}), f32[4,64,96]{2,1,0:T(8,128)S(1)}, u32[]{:S(2)}, u32[]{:S(2)}) async-start(f32[4,64,96]{2,1,0:T(8,128)} %broadcast_in_dim.29), calls=%async_computation.7 | async-start | bytes 262144 | tf_op jit(solution)/shard_map/all_to_all | solution.py:40
  212.1 5.1 %all-to-all-done.7 = f32[4,64,96]{2,1,0:T(8,128)S(1)} async-done(((f32[4,64,96]{2,1,0:T(8,128)}), f32[4,64,96]{2,1,0:T(8,128)S(1)}, u32[]{:S(2)}, u32[]{:S(2)}) %all-to-all-start.7) | async-done | bytes 98336 | tf_op jit(solution)/shard_map/all_to_all | solution.py:40
  (87 shorter events, 13.4 us)
Async XLA Ops:
  0.6 25.9 %copy-start.1 = (bf16[1,1,2,32,512]{4,3,2,1,0:T(8,128)(2,1)S(1)}, bf16[1,1,2,32,512]{4,3,2,1,0:T(8,128)(2,1)}, u32[]{:S(2)}) copy-start(bf16[1,1,2,32,512]{4,3,2,1,0:T(8,128)(2,1)} %param.8) | copy-start | bytes 196612
  0.6 25.8 %collective-permute-start.1 = (bf16[1,2,32,512]{3,2,1,0:T(8,128)(2,1)}, bf16[1,2,32,512]{3,2,1,0:T(8,128)(2,1)S(1)}, u32[]{:S(2)}, u32[]{:S(2)}) collective-permute-start(bf16[1,2,32,512]{3,2,1,0:T(8,128)(2,1)} %bitcast.178), channel_id=1, source_target_pairs={{0,8},{8,16},{16,24},{24,32},{32,40},{40,48},{48,56},{56,64},{64,7... | collective-permute-start | bytes 196616 | tf_op jit(solution)/shard_map/ppermute | solution.py:24
  4.6 21.9 %collective-permute-start = (bf16[1,2,32,512]{3,2,1,0:T(8,128)(2,1)}, bf16[1,2,32,512]{3,2,1,0:T(8,128)(2,1)S(1)}, u32[]{:S(2)}, u32[]{:S(2)}) collective-permute-start(bf16[1,2,32,512]{3,2,1,0:T(8,128)(2,1)} %bitcast.179), channel_id=1, source_target_pairs={{0,16},{8,24},{16,32},{24,40},{32,48},{40,56},{48,64},{56,72},{64,... | collective-permute-start | bytes 196616 | tf_op jit(solution)/shard_map/ppermute | solution.py:24
  13.0 30.3 %all-to-all-start.2 = ((bf16[32,24,96]{2,1,0:T(8,128)(2,1)}), bf16[32,24,96]{2,1,0:T(8,128)(2,1)S(1)}, u32[]{:S(2)}, u32[]{:S(2)}) async-start(bf16[32,24,96]{2,1,0:T(8,128)(2,1)} %bitcast.2), calls=%async_computation.2 | async-start | bytes 393216 | tf_op jit(solution)/shard_map/all_to_all | solution.py:270
  26.6 3.1 %collective-permute-start.2 = (bf16[3,1,32,512]{3,2,1,0:T(8,128)(2,1)S(1)}, bf16[3,1,32,512]{3,2,1,0:T(8,128)(2,1)S(1)}, u32[]{:S(2)}, u32[]{:S(2)}) collective-permute-start(bf16[3,1,32,512]{3,2,1,0:T(8,128)(2,1)S(1)} %get-tuple-element.49), channel_id=1, source_target_pairs={{0,1},{1,2},{2,3},{3,4},{4,5},{5,6},{6,7},{8,9},{9,10},{10,11},{11... | collective-permute-start | bytes 294920 | tf_op jit(solution)/shard_map/ppermute | solution.py:31
  27.9 5.0 %collective-permute-start.3 = (bf16[3,1,32,512]{3,2,1,0:T(8,128)(2,1)S(1)}, bf16[3,1,32,512]{3,2,1,0:T(8,128)(2,1)S(1)}, u32[]{:S(2)}, u32[]{:S(2)}) collective-permute-start(bf16[3,1,32,512]{3,2,1,0:T(8,128)(2,1)S(1)} %get-tuple-element.50), channel_id=1, source_target_pairs={{1,0},{2,1},{3,2},{4,3},{5,4},{6,5},{7,6},{9,8},{10,9},{11,10},{12... | collective-permute-start | bytes 294920 | tf_op jit(solution)/shard_map/ppermute | solution.py:34
  29.6 3.6 %copy-start.2 = (bf16[3,3,3,512,16]{3,4,2,1,0:T(8,128)(2,1)S(1)}, bf16[3,3,3,512,16]{3,4,2,1,0:T(8,128)(2,1)}, u32[]{:S(2)}) copy-start(bf16[3,3,3,512,16]{3,4,2,1,0:T(8,128)(2,1)} %param.9) | copy-start | bytes 1327108
  33.0 1.1 copy-start.6
  35.6 34.4 %copy-start.5 = (s32[128]{0:T(128)S(1)}, s32[128]{0:T(128)}, u32[]{:S(2)}) copy-start(s32[128]{0:T(128)} %param.11) | copy-start | bytes 1540
  43.9 20.3 %all-to-all-start = ((bf16[32,8,128]{2,1,0:T(8,128)(2,1)}), bf16[32,8,128]{2,1,0:T(8,128)(2,1)S(1)}, u32[]{:S(2)}, u32[]{:S(2)}) async-start(bf16[32,8,128]{2,1,0:T(8,128)(2,1)} %broadcast_in_dim.23), calls=%async_computation | async-start | bytes 131072 | tf_op jit(solution)/shard_map/all_to_all | solution.py:40
  51.0 48.5 %copy-start.3 = (bf16[1,128,256]{2,1,0:T(8,128)(2,1)S(1)}, bf16[1,128,256]{2,1,0:T(8,128)(2,1)}, u32[]{:S(2)}) copy-start(bf16[1,128,256]{2,1,0:T(8,128)(2,1)} %param.15) | copy-start | bytes 196612
  51.3 48.5 %copy-start = (bf16[64,3072]{1,0:T(8,128)(2,1)S(1)}, bf16[64,3072]{1,0:T(8,128)(2,1)}, u32[]{:S(2)}) copy-start(bf16[64,3072]{1,0:T(8,128)(2,1)} %param.12) | copy-start | bytes 1179652
  64.9 26.7 %all-to-all-start.3 = ((f32[32,12,128]{2,1,0:T(8,128)}), f32[32,12,128]{2,1,0:T(8,128)S(1)}, u32[]{:S(2)}, u32[]{:S(2)}) async-start(f32[32,12,128]{2,1,0:T(8,128)} %broadcast_in_dim.25), calls=%async_computation.3 | async-start | bytes 524288 | tf_op jit(solution)/shard_map/all_to_all | solution.py:40
  92.5 17.1 %all-to-all-start.1 = ((bf16[8,32,8,128]{3,2,1,0:T(8,128)(2,1)}), bf16[8,32,8,128]{3,2,1,0:T(8,128)(2,1)S(1)}, u32[]{:S(2)}, u32[]{:S(2)}) async-start(bf16[8,32,8,128]{3,2,1,0:T(8,128)(2,1)} %broadcast_in_dim.24), calls=%async_computation.1 | async-start | bytes 1048576 | tf_op jit(solution)/shard_map/all_to_all | solution.py:40
  99.8 34.1 %copy-start.4 = (f32[3072]{0:T(1024)S(1)}, f32[3072]{0:T(1024)}, u32[]{:S(2)}) copy-start(f32[3072]{0:T(1024)} %param.13) | copy-start | bytes 36868
  128.8 26.3 %all-to-all-start.4 = ((f32[32,12,128]{2,1,0:T(8,128)}), f32[32,12,128]{2,1,0:T(8,128)S(1)}, u32[]{:S(2)}, u32[]{:S(2)}) async-start(f32[32,12,128]{2,1,0:T(8,128)} %reshape.164), calls=%async_computation.4 | async-start | bytes 524288 | tf_op jit(solution)/shard_map/all_to_all | solution.py:302
  207.9 9.3 %all-to-all-start.7 = ((f32[4,64,96]{2,1,0:T(8,128)}), f32[4,64,96]{2,1,0:T(8,128)S(1)}, u32[]{:S(2)}, u32[]{:S(2)}) async-start(f32[4,64,96]{2,1,0:T(8,128)} %broadcast_in_dim.29), calls=%async_computation.7 | async-start | bytes 262144 | tf_op jit(solution)/shard_map/all_to_all | solution.py:40

commit v2 on v1

--- a/solution.py
+++ b/solution.py
@@ -76,7 +76,7 @@
 
 
 def attention_kernel(
-    x_ref, mt_ref, gram_ref, row_ref, half_ref, cot_ref,
+    x_ref, high_ref, low_ref, gram_ref, row_ref, half_ref, cot_ref,
     out_ref, at_ref, b_ref,
     both, keys, scores, probs, csum, query, qsum,
 ):
@@ -118,29 +118,31 @@
 
     pair, odd = head // 2, head % 2
 
-    def weight(t):
-        block = mt_ref[pl.ds(pl.multiple_of(t * 2 * FEAT + pair * FEAT, FEAT), FEAT), :]
+    def weight(t, ref):
+        block = ref[pl.ds(pl.multiple_of(t * 2 * FEAT + pair * FEAT, FEAT), FEAT), :]
+        block = block.astype(F32)
         return jnp.where(odd == 1, block[:, FEAT:], block[:, :FEAT])
 
-    w_q, w_k, w_v = weight(0), weight(1), weight(2)
-
-    def stacked(pick):
+    w_high = [weight(t, high_ref) for t in range(3)]
+    w_low = [weight(t, low_ref) for t in range(3)]
+    w_k, w_v = w_high[1] + w_low[1], w_high[2] + w_low[2]
+
+    def stacked(parts):
         rows = []
-        for w in (w_k, w_v):
-            m = pick(w)
+        for m in parts:
             rows.append(jnp.concatenate([m, zero], axis=1))
             rows.append(jnp.concatenate([zero, m], axis=1))
         return jnp.concatenate(rows, axis=0)
 
-    main = stacked(lambda w: two(w)[0])
-    rest = stacked(lambda w: two(w)[1])
+    main = stacked([w.astype(BF16) for w in w_high[1:]])
+    rest = stacked([w.astype(BF16) for w in w_low[1:]])
     keys[...] = (
         mm(jnp.concatenate([main, main], axis=1), both[...], NT)
         + mm(rest, both[:, : 2 * FEAT], NT)
     ).astype(BF16)
 
     q_high, q_low = query[:, :FEAT], query[:, FEAT:]
-    wq_high, wq_low = two(w_q)
+    wq_high, wq_low = w_high[0].astype(BF16), w_low[0].astype(BF16)
     q = (mm(q_high, wq_high, NT) + (mm(q_high, wq_low, NT) + mm(q_low, wq_high, NT))).astype(BF16)
     q_scaled = (q.astype(F32) * factor).astype(BF16)
     cot = cot_ref[0]
@@ -222,7 +224,7 @@
         b_ref[...] = ((full[:FEAT, :FEAT] + full[FEAT:, FEAT:]) + own_part) * (1.0 / D)
 
 
-def attention(x, mt, gram, row, half, cot):
+def attention(x, high, low, gram, row, half, cot):
     heads, count, _ = cot.shape
     pairs = x.shape[0]
     whole = lambda *shape: pl.BlockSpec(shape, lambda i: (0,) * len(shape))
@@ -231,13 +233,13 @@
         attention_kernel,
         grid=(heads,),
         in_specs=[
-            whole(*x.shape), whole(*mt.shape), whole(*gram.shape),
+            whole(*x.shape), whole(*high.shape), whole(*low.shape), whole(*gram.shape),
             whole(*row.shape), whole(*half.shape), per_head,
         ],
-        out_specs=[per_head, whole(*mt.shape), whole(*gram.shape)],
+        out_specs=[per_head, whole(*high.shape), whole(*gram.shape)],
         out_shape=[
             jax.ShapeDtypeStruct(cot.shape, BF16),
-            jax.ShapeDtypeStruct(mt.shape, F32),
+            jax.ShapeDtypeStruct(high.shape, F32),
             jax.ShapeDtypeStruct(gram.shape, F32),
         ],
         scratch_shapes=[
@@ -253,7 +255,7 @@
             dimension_semantics=("arbitrary",), vmem_limit_bytes=48 * 1024 * 1024
         ),
         name="attention",
-    )(x, mt, gram, row, half, cot)
+    )(x, high, low, gram, row, half, cot)
 
 
 def per_device(
@@ -268,13 +270,11 @@
     w = qkv_weight.reshape(depth, 3, heads // 2, 2, HEAD_DIM)
     w = jnp.transpose(w, (1, 2, 4, 3, 0)).reshape(seq_count, rows_each * 2, depth)
     w_slice = lax.all_to_all(w, SEQ, 0, 0, tiled=True)
+    w_slice = jnp.transpose(w_slice, (1, 0, 2)).reshape(rows_each * 2, D)
     embed32 = embed_weight.astype(F32)
-    gained = jnp.concatenate(two(embed32 * norm_gain), axis=0).reshape(2 * FEAT, seq_count, depth)
-    m_slice = lax.dot_general(
-        w_slice, gained, (((0, 2), (1, 2)), ((), ())), preferred_element_type=F32
-    )
+    gained = jnp.concatenate(two(embed32 * norm_gain), axis=0)
+    m_slice = mm(w_slice, gained, NT)
     m_slice = (m_slice[:, :FEAT] + m_slice[:, FEAT:]).reshape(rows_each, 2 * FEAT)
-    mt = from_everyone(m_slice, SEQ).reshape(rows, 2 * FEAT)
     gram = lax.dot_general(
         embed_weight, embed_weight, (((1,), (1,)), ((), ())), preferred_element_type=F32
     ) * (1.0 / D)
@@ -284,8 +284,11 @@
     patch = jnp.transpose(tile.reshape(2, columns // 2, 2, channels), (1, 0, 2, 3))
     patch = patch.reshape(2, columns // 4, FEAT)
     patch = jnp.transpose(patch, (1, 0, 2)).reshape(columns // 4, 2 * FEAT)
-    every = from_everyone(from_everyone(patch, SEQ), HEAD)
-    every = every.reshape(-1, 2 * FEAT)
+    own_rows = columns // 4
+    arrived = from_everyone(jnp.concatenate([patch, *two(m_slice)], axis=0), SEQ)
+    every = from_everyone(arrived[:, :own_rows], HEAD).reshape(-1, 2 * FEAT)
+    m_high = arrived[:, own_rows : own_rows + rows_each].reshape(rows, 2 * FEAT)
+    m_low = arrived[:, own_rows + rows_each :].reshape(rows, 2 * FEAT)
 
     per_patch_row = columns // 4
     head_count = lax.axis_size(HEAD)
@@ -296,24 +299,22 @@
     half = j // per_patch_row
 
     cot = jnp.transpose(grad_out[0].reshape(-1, heads, HEAD_DIM), (1, 0, 2))
-    out, at, b = attention(every, mt, gram, row[:, None], half[:, None], cot)
+    out, at, b = attention(every, m_high, m_low, gram, row[:, None], half[:, None], cot)
     attended = jnp.transpose(out, (1, 0, 2)).reshape(1, -1, width)
 
     at = lax.all_to_all(at.reshape(seq_count, rows_each, 2 * FEAT), SEQ, 0, 0, tiled=True)
     a_slice = jnp.sum(at, axis=0).reshape(rows_each * 2, FEAT)
     a_both = jnp.concatenate(two(a_slice), axis=1)
-    t = lax.dot_general(
-        a_both, w_slice, (((0,), (1,)), ((), ())), preferred_element_type=F32
-    )
+    t = mm(a_both, w_slice, TN)
     t = t[:FEAT] + t[FEAT:]
-    second = jnp.dot(b, embed32, preferred_element_type=F32, precision=HIGHEST)
-    t = t * norm_gain.reshape(seq_count, depth) - second.reshape(FEAT, seq_count, depth)
-    t = jnp.transpose(t, (1, 0, 2)).astype(BF16)
+    t = t * norm_gain - mm(b, embed32, precision=HIGHEST)
+    parts = lax.axis_size(("grp", "seq_0"))
+    t = jnp.transpose(t.reshape(parts, FEAT // parts, head_count, -1), (2, 0, 1, 3))
+    t = t.astype(BF16).reshape(parts * head_count, FEAT // parts, -1)
     t = lax.all_to_all(t, PLANE, 0, 0, tiled=True)
-    t = jnp.sum(t.astype(F32), axis=0)
-    t = jnp.sum(from_everyone(t, "seq_1"), axis=0)
-    t = from_everyone(t, ("grp", "seq_0"))
-    embed_grad = jnp.transpose(t, (1, 0, 2)).reshape(FEAT, -1)
+    t = jnp.sum(t.astype(F32), axis=0).astype(BF16)
+    t = jnp.sum(from_everyone(t, "seq_1").astype(F32), axis=0)
+    embed_grad = from_everyone(t, ("grp", "seq_0")).reshape(FEAT, -1)
     return (attended, embed_grad)
 
 

time: 219 us -> 183 us (0.84)
  waiting for transfers between devices: 78.4 us -> 44.5 us
  blocking collectives: 50.2 us -> 60.9 us
  starting transfers between devices: 52.7 us -> 43.1 us
    all_to_all x0 -> x1, blocking collectives: none -> 25.2 us  [per_device(): lax.all_to_all(at.reshape(seq_count, rows_each, 2 * FEAT), SEQ, 0, 0, til...]
    all_to_all x1 -> x0, waiting for transfers between devices: 20.2 us -> none  [per_device(): lax.all_to_all(at.reshape(seq_count, rows_each, 2 * FEAT), SEQ, 0, 0, til...]
    all_to_all x4 -> x3, waiting for transfers between devices: 49 us -> 34.6 us  [from_everyone(): return lax.all_to_all(copies, axis, split_axis=0, concat_axis=0, tiled=True)]
    all_to_all x1, blocking collectives: 33.6 us -> 20.6 us  [from_everyone(): return lax.all_to_all(copies, axis, split_axis=0, concat_axis=0, tiled=True)]
    all_to_all x1 -> x0, starting transfers between devices: 5.1 us -> none  [per_device(): lax.all_to_all(at.reshape(seq_count, rows_each, 2 * FEAT), SEQ, 0, 0, til...]
    all_to_all x4 -> x3, starting transfers between devices: 22.2 us -> 17.8 us  [from_everyone(): return lax.all_to_all(copies, axis, split_axis=0, concat_axis=0, tiled=True)]
  transfers between devices with their start and end apart: 10 -> 8, of which waited for: 7 -> 5; matrix products, arithmetic and copies ran while one was open for 5% -> 5% of each run, Pallas kernels for 0% -> 0%
where the time goes in v2:
time: 183 us; the launch traced here: 182 us
  blocking collectives  60.9 us (33%)
  waiting for transfers between devices  44.5 us (24%)
  starting transfers between devices  43.1 us (24%)
  Pallas kernels  18.3 us (10%)
  local copies, waits for them, and re-layouts  7.35 us (4%)
  matrix products  5.04 us (3%)
    all_to_all x3, waiting for transfers between devices, from_everyone(): return lax.all_to_all(copies, axis, split_axis=0, concat_axis=0, tiled=True)  34.6 us
    all_to_all x1, blocking collectives, per_device(): lax.all_to_all(at.reshape(seq_count, rows_each, 2 * FEAT), SEQ, 0, 0, til...  25.2 us
    all_to_all x1, blocking collectives, from_everyone(): return lax.all_to_all(copies, axis, split_axis=0, concat_axis=0, tiled=True)  20.6 us
    pallas_call x1, Pallas kernels, attention(): pl.pallas_call(attention_kernel, grid=(heads,), in_specs=[whole(*x.shape)...  18.3 us
    all_to_all x3, starting transfers between devices, from_everyone(): return lax.all_to_all(copies, axis, split_axis=0, concat_axis=0, tiled=True)  17.8 us
    all_to_all x1, blocking collectives, per_device(): t = lax.all_to_all(t, PLANE, 0, 0, tiled=True)  15.1 us
    all_to_all x1, starting transfers between devices, per_device(): w_slice = lax.all_to_all(w, SEQ, 0, 0, tiled=True)  12.4 us
    ppermute x2, starting transfers between devices, shifted(): lax.ppermute(value, axis, [(source, source + steps) for source in range(l...  10.4 us
  transfers between devices with their start and end apart: 8, of which 5 were waited for; matrix products, arithmetic and copies ran while one was open for 5% of the time, Pallas kernels for 0%

profile of v2, /device:TPU:32, one launch (start us, length us, event | category | flops | bytes accessed | tf_op | source)
XLA Modules:
  0.0 181.8 jit_solution(15424609438851436332)
XLA Ops:
  0.7 5.3 %collective-permute-start = (bf16[1,2,32,512]{3,2,1,0:T(8,128)(2,1)}, bf16[1,2,32,512]{3,2,1,0:T(8,128)(2,1)S(1)}, u32[]{:S(2)}, u32[]{:S(2)}) collective-permute-start(bf16[1,2,32,512]{3,2,1,0:T(8,128)(2,1)} %bitcast.172), channel_id=1, source_target_pairs={{0,16},{8,24},{16,32},{24,40},{32,48},{40,56},{48,64},{56,72},{64,... | collective-permute-start | bytes 196616 | tf_op jit(solution)/shard_map/ppermute | solution.py:24
  6.0 5.0 %collective-permute-start.1 = (bf16[1,2,32,512]{3,2,1,0:T(8,128)(2,1)}, bf16[1,2,32,512]{3,2,1,0:T(8,128)(2,1)S(1)}, u32[]{:S(2)}, u32[]{:S(2)}) collective-permute-start(bf16[1,2,32,512]{3,2,1,0:T(8,128)(2,1)} %bitcast.173), channel_id=1, source_target_pairs={{0,8},{8,16},{16,24},{24,32},{32,40},{40,48},{48,56},{56,64},{64,7... | collective-permute-start | bytes 196616 | tf_op jit(solution)/shard_map/ppermute | solution.py:24
  11.0 1.1 copy.40
  12.1 0.9 copy.41
  13.0 12.4 %all-to-all-start = ((bf16[32,24,96]{2,1,0:T(8,128)(2,1)}), bf16[32,24,96]{2,1,0:T(8,128)(2,1)S(1)}, u32[]{:S(2)}, u32[]{:S(2)}) async-start(bf16[32,24,96]{2,1,0:T(8,128)(2,1)} %bitcast.60), calls=%async_computation | async-start | bytes 393216 | tf_op jit(solution)/shard_map/all_to_all | solution.py:272
  25.4 0.9 pad_maximum_fusion
  26.3 1.3 collective-permute-start.2
  27.6 1.3 collective-permute-start.3
  29.1 3.5 %collective-permute-done.3 = bf16[3,1,32,512]{3,2,1,0:T(8,128)(2,1)S(1)} collective-permute-done((bf16[3,1,32,512]{3,2,1,0:T(8,128)(2,1)S(1)}, bf16[3,1,32,512]{3,2,1,0:T(8,128)(2,1)S(1)}, u32[]{:S(2)}, u32[]{:S(2)}) %collective-permute-start.3) | collective-permute-done | bytes 98336 | tf_op jit(solution)/shard_map/ppermute | solution.py:34
  37.0 6.3 %all-to-all-done = bf16[32,24,96]{2,1,0:T(8,128)(2,1)S(1)} async-done(((bf16[32,24,96]{2,1,0:T(8,128)(2,1)}), bf16[32,24,96]{2,1,0:T(8,128)(2,1)S(1)}, u32[]{:S(2)}, u32[]{:S(2)}) %all-to-all-start) | async-done | bytes 147488 | tf_op jit(solution)/shard_map/all_to_all | solution.py:272
  44.1 0.7 broadcast_in_dim.21
  44.8 6.8 %all-to-all-start.1 = ((bf16[32,32,128]{2,1,0:T(8,128)(2,1)}), bf16[32,32,128]{2,1,0:T(8,128)(2,1)S(1)}, u32[]{:S(2)}, u32[]{:S(2)}) async-start(bf16[32,32,128]{2,1,0:T(8,128)(2,1)} %broadcast_in_dim.21), calls=%async_computation.1 | async-start | bytes 524288 | tf_op jit(solution)/shard_map/all_to_all | solution.py:40
  52.2 19.8 %all-to-all-done.1 = bf16[32,32,128]{2,1,0:T(8,128)(2,1)S(1)} async-done(((bf16[32,32,128]{2,1,0:T(8,128)(2,1)}), bf16[32,32,128]{2,1,0:T(8,128)(2,1)S(1)}, u32[]{:S(2)}, u32[]{:S(2)}) %all-to-all-start.1) | async-done | bytes 262176 | tf_op jit(solution)/shard_map/all_to_all | solution.py:40
  71.9 0.9 broadcast_in_dim.22
  72.8 7.7 %all-to-all-start.2 = ((bf16[8,32,8,128]{3,2,1,0:T(8,128)(2,1)}), bf16[8,32,8,128]{3,2,1,0:T(8,128)(2,1)S(1)}, u32[]{:S(2)}, u32[]{:S(2)}) async-start(bf16[8,32,8,128]{3,2,1,0:T(8,128)(2,1)} %broadcast_in_dim.22), calls=%async_computation.2 | async-start | bytes 1048576 | tf_op jit(solution)/shard_map/all_to_all | solution.py:40
  80.9 10.0 %all-to-all-done.2 = bf16[8,32,8,128]{3,2,1,0:T(8,128)(2,1)S(1)} async-done(((bf16[8,32,8,128]{3,2,1,0:T(8,128)(2,1)}), bf16[8,32,8,128]{3,2,1,0:T(8,128)(2,1)S(1)}, u32[]{:S(2)}, u32[]{:S(2)}) %all-to-all-start.2) | async-done | bytes 524320 | tf_op jit(solution)/shard_map/all_to_all | solution.py:40
  90.9 18.3 %attention.1 = (bf16[4,128,64]{2,1,0:T(8,128)(2,1)S(1)}, f32[384,128]{1,0:T(8,128)S(1)}, f32[64,64]{1,0:T(8,128)S(1)}) custom-call(bf16[2048,128]{1,0:T(8,128)(2,1)S(1)} %bitcast.169, bf16[384,128]{1,0:T(8,128)(2,1)S(1)} %reshape.166.high_ref, bf16[384,128]{1,0:T(8,128)(2,1)S(1)} %reshape.167.low_ref, f32[64,64]{1,0:T(8,128)S(1)} %convolution_multiply_fusion.gram_ref, ...), custom_call_target="tpu_custom_call" | custom-call | tf_op jit(solution)/shard_map/attention/pallas_call | solution.py:232
  109.2 25.2 %all_to_all.35 = f32[32,12,128]{2,1,0:T(8,128)S(1)} all-to-all(f32[32,12,128]{2,1,0:T(8,128)S(1)} %reshape.169), channel_id=1, replica_groups=mesh['grp'=2,'seq_0'=2,'seq_1'=16,'head_0'=4,'head_1'=2] {'seq_0','seq_1'}, dimensions={0} | all-to-all | bytes 393216 | tf_op jit(solution)/shard_map/all_to_all | solution.py:305
  135.6 15.1 %all_to_all.36 = bf16[32,16,384]{2,1,0:T(8,128)(2,1)S(1)} all-to-all(bf16[32,16,384]{2,1,0:T(8,128)(2,1)S(1)} %bitcast.182), channel_id=1, replica_groups=mesh['grp'=2,'seq_0'=2,'seq_1'=16,'head_0'=4,'head_1'=2] {'head_0','head..., dimensions={0} | all-to-all | bytes 786432 | tf_op jit(solution)/shard_map/all_to_all | solution.py:314
  150.8 20.6 %all_to_all.37 = bf16[16,16,384]{2,1,0:T(8,128)(2,1)S(1)} all-to-all(bf16[16,16,384]{2,1,0:T(8,128)(2,1)S(1)} %broadcast_in_dim.25), channel_id=1, replica_groups=mesh['grp'=2,'seq_0'=2,'seq_1'=16,'head_0'=4,'head_1'=2] {'seq_1'}, dimensions={0} | all-to-all | bytes 393216 | tf_op jit(solution)/shard_map/all_to_all | solution.py:40
  171.4 0.6 broadcast_in_dim.26
  172.1 3.3 %all-to-all-start.6 = ((f32[4,16,384]{2,1,0:T(8,128)}), f32[4,16,384]{2,1,0:T(8,128)S(1)}, u32[]{:S(2)}, u32[]{:S(2)}) async-start(f32[4,16,384]{2,1,0:T(8,128)} %broadcast_in_dim.26), calls=%async_computation.6 | async-start | bytes 196608 | tf_op jit(solution)/shard_map/all_to_all | solution.py:40
  175.5 0.7 copy.49
  176.3 4.9 %all-to-all-done.6 = f32[4,16,384]{2,1,0:T(8,128)S(1)} async-done(((f32[4,16,384]{2,1,0:T(8,128)}), f32[4,16,384]{2,1,0:T(8,128)S(1)}, u32[]{:S(2)}, u32[]{:S(2)}) %all-to-all-start.6) | async-done | bytes 98336 | tf_op jit(solution)/shard_map/all_to_all | solution.py:40
  (86 shorter events, 8.2 us)
Async XLA Ops:
  0.6 32.0 %copy-start.1 = (bf16[1,1,2,32,512]{4,3,2,1,0:T(8,128)(2,1)S(1)}, bf16[1,1,2,32,512]{4,3,2,1,0:T(8,128)(2,1)}, u32[]{:S(2)}) copy-start(bf16[1,1,2,32,512]{4,3,2,1,0:T(8,128)(2,1)} %param.8) | copy-start | bytes 196612
  0.6 28.2 %copy-start = (bf16[64,3072]{1,0:T(8,128)(2,1)S(1)}, bf16[64,3072]{1,0:T(8,128)(2,1)}, u32[]{:S(2)}) copy-start(bf16[64,3072]{1,0:T(8,128)(2,1)} %param.12) | copy-start | bytes 1179652
  0.7 28.2 %copy-start.4 = (f32[3072]{0:T(1024)S(1)}, f32[3072]{0:T(1024)}, u32[]{:S(2)}) copy-start(f32[3072]{0:T(1024)} %param.13) | copy-start | bytes 36868
  0.7 24.7 %collective-permute-start = (bf16[1,2,32,512]{3,2,1,0:T(8,128)(2,1)}, bf16[1,2,32,512]{3,2,1,0:T(8,128)(2,1)S(1)}, u32[]{:S(2)}, u32[]{:S(2)}) collective-permute-start(bf16[1,2,32,512]{3,2,1,0:T(8,128)(2,1)} %bitcast.172), channel_id=1, source_target_pairs={{0,16},{8,24},{16,32},{24,40},{32,48},{40,56},{48,64},{56,72},{64,... | collective-permute-start | bytes 196616 | tf_op jit(solution)/shard_map/ppermute | solution.py:24
  6.0 19.4 %collective-permute-start.1 = (bf16[1,2,32,512]{3,2,1,0:T(8,128)(2,1)}, bf16[1,2,32,512]{3,2,1,0:T(8,128)(2,1)S(1)}, u32[]{:S(2)}, u32[]{:S(2)}) collective-permute-start(bf16[1,2,32,512]{3,2,1,0:T(8,128)(2,1)} %bitcast.173), channel_id=1, source_target_pairs={{0,8},{8,16},{16,24},{24,32},{32,40},{40,48},{48,56},{56,64},{64,7... | collective-permute-start | bytes 196616 | tf_op jit(solution)/shard_map/ppermute | solution.py:24
  13.0 30.3 %all-to-all-start = ((bf16[32,24,96]{2,1,0:T(8,128)(2,1)}), bf16[32,24,96]{2,1,0:T(8,128)(2,1)S(1)}, u32[]{:S(2)}, u32[]{:S(2)}) async-start(bf16[32,24,96]{2,1,0:T(8,128)(2,1)} %bitcast.60), calls=%async_computation | async-start | bytes 393216 | tf_op jit(solution)/shard_map/all_to_all | solution.py:272
  26.3 2.8 %collective-permute-start.2 = (bf16[3,1,32,512]{3,2,1,0:T(8,128)(2,1)S(1)}, bf16[3,1,32,512]{3,2,1,0:T(8,128)(2,1)S(1)}, u32[]{:S(2)}, u32[]{:S(2)}) collective-permute-start(bf16[3,1,32,512]{3,2,1,0:T(8,128)(2,1)S(1)} %get-tuple-element.49), channel_id=1, source_target_pairs={{0,1},{1,2},{2,3},{3,4},{4,5},{5,6},{6,7},{8,9},{9,10},{10,11},{11... | collective-permute-start | bytes 294920 | tf_op jit(solution)/shard_map/ppermute | solution.py:31
  27.6 5.0 %collective-permute-start.3 = (bf16[3,1,32,512]{3,2,1,0:T(8,128)(2,1)S(1)}, bf16[3,1,32,512]{3,2,1,0:T(8,128)(2,1)S(1)}, u32[]{:S(2)}, u32[]{:S(2)}) collective-permute-start(bf16[3,1,32,512]{3,2,1,0:T(8,128)(2,1)S(1)} %get-tuple-element.50), channel_id=1, source_target_pairs={{1,0},{2,1},{3,2},{4,3},{5,4},{6,5},{7,6},{9,8},{10,9},{11,10},{12... | collective-permute-start | bytes 294920 | tf_op jit(solution)/shard_map/ppermute | solution.py:34
  29.0 3.9 %copy-start.2 = (bf16[3,3,3,512,16]{3,4,2,1,0:T(8,128)(2,1)S(1)}, bf16[3,3,3,512,16]{3,4,2,1,0:T(8,128)(2,1)}, u32[]{:S(2)}) copy-start(bf16[3,3,3,512,16]{3,4,2,1,0:T(8,128)(2,1)} %param.9) | copy-start | bytes 1327108
  32.7 1.1 copy-start.6
  36.8 14.9 %copy-start.5 = (s32[128]{0:T(128)S(1)}, s32[128]{0:T(128)}, u32[]{:S(2)}) copy-start(s32[128]{0:T(128)} %param.11) | copy-start | bytes 1540
  43.3 8.6 %copy-start.3 = (bf16[1,128,256]{2,1,0:T(8,128)(2,1)S(1)}, bf16[1,128,256]{2,1,0:T(8,128)(2,1)}, u32[]{:S(2)}) copy-start(bf16[1,128,256]{2,1,0:T(8,128)(2,1)} %param.15) | copy-start | bytes 196612
  44.8 27.1 %all-to-all-start.1 = ((bf16[32,32,128]{2,1,0:T(8,128)(2,1)}), bf16[32,32,128]{2,1,0:T(8,128)(2,1)S(1)}, u32[]{:S(2)}, u32[]{:S(2)}) async-start(bf16[32,32,128]{2,1,0:T(8,128)(2,1)} %broadcast_in_dim.21), calls=%async_computation.1 | async-start | bytes 524288 | tf_op jit(solution)/shard_map/all_to_all | solution.py:40
  72.8 18.1 %all-to-all-start.2 = ((bf16[8,32,8,128]{3,2,1,0:T(8,128)(2,1)}), bf16[8,32,8,128]{3,2,1,0:T(8,128)(2,1)S(1)}, u32[]{:S(2)}, u32[]{:S(2)}) async-start(bf16[8,32,8,128]{3,2,1,0:T(8,128)(2,1)} %broadcast_in_dim.22), calls=%async_computation.2 | async-start | bytes 1048576 | tf_op jit(solution)/shard_map/all_to_all | solution.py:40
  172.1 9.1 %all-to-all-start.6 = ((f32[4,16,384]{2,1,0:T(8,128)}), f32[4,16,384]{2,1,0:T(8,128)S(1)}, u32[]{:S(2)}, u32[]{:S(2)}) async-start(f32[4,16,384]{2,1,0:T(8,128)} %broadcast_in_dim.26), calls=%async_computation.6 | async-start | bytes 196608 | tf_op jit(solution)/shard_map/all_to_all | solution.py:40

commit v3 on v2

--- a/solution.py
+++ b/solution.py
@@ -116,10 +116,10 @@
                 second, piece[:, FEAT:], piece[:, :FEAT]
             ).astype(BF16)
 
-    pair, odd = head // 2, head % 2
+    odd = head % 2
 
     def weight(t, ref):
-        block = ref[pl.ds(pl.multiple_of(t * 2 * FEAT + pair * FEAT, FEAT), FEAT), :]
+        block = ref[t * FEAT : (t + 1) * FEAT, :]
         block = block.astype(F32)
         return jnp.where(odd == 1, block[:, FEAT:], block[:, :FEAT])
 
@@ -198,15 +198,7 @@
     a_k = mm(q_scaled.astype(F32), grad, TN, HIGHEST)
     a_v = mm(cot.astype(F32), value, TN, HIGHEST)
     for t, a in enumerate((a_q, a_k, a_v)):
-        rows = pl.ds(pl.multiple_of(t * 2 * FEAT + pair * FEAT, FEAT), FEAT)
-
-        @pl.when(odd == 0)
-        def _():
-            at_ref[rows, :FEAT] = a
-
-        @pl.when(odd == 1)
-        def _():
-            at_ref[rows, FEAT:] = a
+        at_ref[pl.ds(pl.multiple_of(t * 2 * FEAT + odd * FEAT, FEAT), FEAT), :] = a
 
     @pl.when(head == heads - 1)
     def _():
@@ -236,10 +228,10 @@
             whole(*x.shape), whole(*high.shape), whole(*low.shape), whole(*gram.shape),
             whole(*row.shape), whole(*half.shape), per_head,
         ],
-        out_specs=[per_head, whole(*high.shape), whole(*gram.shape)],
+        out_specs=[per_head, whole(2 * high.shape[0], FEAT), whole(*gram.shape)],
         out_shape=[
             jax.ShapeDtypeStruct(cot.shape, BF16),
-            jax.ShapeDtypeStruct(high.shape, F32),
+            jax.ShapeDtypeStruct((2 * high.shape[0], FEAT), F32),
             jax.ShapeDtypeStruct(gram.shape, F32),
         ],
         scratch_shapes=[
@@ -261,20 +253,39 @@
 def per_device(
     features, conv_weight, conv_bias, token_order, embed_weight, norm_gain, qkv_weight, grad_out
 ):
-    seq_count = lax.axis_size(SEQ)
+    far = lax.axis_index("seq_0")
+    near_count = lax.axis_size("seq_1")
     depth, _, width = qkv_weight.shape
-    heads = width // HEAD_DIM
-    rows = 3 * (heads // 2) * HEAD_DIM
-    rows_each = rows // seq_count
-
-    w = qkv_weight.reshape(depth, 3, heads // 2, 2, HEAD_DIM)
-    w = jnp.transpose(w, (1, 2, 4, 3, 0)).reshape(seq_count, rows_each * 2, depth)
-    w_slice = lax.all_to_all(w, SEQ, 0, 0, tiled=True)
-    w_slice = jnp.transpose(w_slice, (1, 0, 2)).reshape(rows_each * 2, D)
+    pair = 2 * HEAD_DIM
+    rows = 3 * HEAD_DIM
+    rows_each = rows // near_count
+
+    def swapped(array, axis):
+        first, second = jnp.split(array, 2, axis=axis)
+        mine = jnp.where(far == 0, first, second)
+        given = jnp.where(far == 0, second, first)
+        return mine, lax.ppermute(given, "seq_0", [(0, 1), (1, 0)])
+
+    def in_order(mine, other):
+        return jnp.where(far == 0, jnp.stack([mine, other]), jnp.stack([other, mine]))
+
+    w = in_order(*swapped(qkv_weight, 2)).reshape(2, depth, 3 * pair)
     embed32 = embed_weight.astype(F32)
-    gained = jnp.concatenate(two(embed32 * norm_gain), axis=0)
-    m_slice = mm(w_slice, gained, NT)
-    m_slice = (m_slice[:, :FEAT] + m_slice[:, FEAT:]).reshape(rows_each, 2 * FEAT)
+    start = lax.axis_index("seq_1") * depth
+    m_part = 0.0
+    for k in range(2):
+        at = start + k * (D // 2)
+        gained = lax.dynamic_slice_in_dim(embed_weight, at, depth, 1).astype(F32)
+        gained = jnp.concatenate(
+            two(gained * lax.dynamic_slice_in_dim(norm_gain, at, depth, 0)), axis=0
+        )
+        m_part = m_part + lax.dot_general(
+            w[k], gained, (((0,), (1,)), ((), ())), preferred_element_type=F32
+        )
+    m_part = (m_part[:, :FEAT] + m_part[:, FEAT:]).reshape(3, 2, HEAD_DIM, FEAT)
+    m_part = jnp.transpose(m_part, (0, 2, 1, 3)).reshape(near_count, rows_each, 2 * FEAT)
+    m_slice = jnp.sum(lax.all_to_all(m_part, "seq_1", 0, 0, tiled=True), axis=0)
+    w_full = lax.all_gather(w, "seq_1", axis=0)
     gram = lax.dot_general(
         embed_weight, embed_weight, (((1,), (1,)), ((), ())), preferred_element_type=F32
     ) * (1.0 / D)
@@ -285,27 +296,38 @@
     patch = patch.reshape(2, columns // 4, FEAT)
     patch = jnp.transpose(patch, (1, 0, 2)).reshape(columns // 4, 2 * FEAT)
     own_rows = columns // 4
-    arrived = from_everyone(jnp.concatenate([patch, *two(m_slice)], axis=0), SEQ)
-    every = from_everyone(arrived[:, :own_rows], HEAD).reshape(-1, 2 * FEAT)
+    arrived = from_everyone(jnp.concatenate([patch, *two(m_slice)], axis=0), "seq_1")
+    every = from_everyone(arrived[:, :own_rows], ("seq_0", *HEAD)).reshape(-1, 2 * FEAT)
     m_high = arrived[:, own_rows : own_rows + rows_each].reshape(rows, 2 * FEAT)
     m_low = arrived[:, own_rows + rows_each :].reshape(rows, 2 * FEAT)
 
     per_patch_row = columns // 4
     head_count = lax.axis_size(HEAD)
-    j = token_order % (2 * per_patch_row)
-    i = (token_order // (2 * per_patch_row)) % head_count
-    f = token_order // (2 * per_patch_row * head_count)
-    row = (i * seq_count + f) * per_patch_row + j % per_patch_row
+    order = in_order(token_order, lax.ppermute(token_order, "seq_0", [(0, 1), (1, 0)]))
+    order = order.reshape(-1, 1)
+    j = order % (2 * per_patch_row)
+    i = (order // (2 * per_patch_row)) % head_count
+    f = order // (2 * per_patch_row * head_count)
+    plane = (f // near_count) * head_count + i
+    row = (plane * near_count + f % near_count) * per_patch_row + j % per_patch_row
     half = j // per_patch_row
 
-    cot = jnp.transpose(grad_out[0].reshape(-1, heads, HEAD_DIM), (1, 0, 2))
-    out, at, b = attention(every, m_high, m_low, gram, row[:, None], half[:, None], cot)
-    attended = jnp.transpose(out, (1, 0, 2)).reshape(1, -1, width)
-
-    at = lax.all_to_all(at.reshape(seq_count, rows_each, 2 * FEAT), SEQ, 0, 0, tiled=True)
-    a_slice = jnp.sum(at, axis=0).reshape(rows_each * 2, FEAT)
-    a_both = jnp.concatenate(two(a_slice), axis=1)
-    t = mm(a_both, w_slice, TN)
+    cot = in_order(*swapped(grad_out[0], 1)).reshape(-1, 2, HEAD_DIM)
+    out, at, b = attention(
+        every, m_high, m_low, gram, row, half, jnp.transpose(cot, (1, 0, 2))
+    )
+    out = jnp.transpose(out, (1, 0, 2)).reshape(2, -1, pair)
+    mine = jnp.where(far == 0, out[0], out[1])
+    other = lax.ppermute(jnp.where(far == 0, out[1], out[0]), "seq_0", [(0, 1), (1, 0)])
+    attended = jnp.where(
+        far == 0,
+        jnp.concatenate([mine, other], axis=1),
+        jnp.concatenate([other, mine], axis=1),
+    )[None]
+
+    a_both = jnp.concatenate(two(at), axis=1)
+    w_full = jnp.transpose(w_full, (1, 0, 2, 3)).reshape(D, 3 * pair)
+    t = mm(a_both, w_full, ((0,), (1,)))
     t = t[:FEAT] + t[FEAT:]
     t = t * norm_gain - mm(b, embed32, precision=HIGHEST)
     parts = lax.axis_size(("grp", "seq_0"))

time: 183 us -> 190 us (1.038)
  blocking collectives: 60.9 us -> 17.4 us
  waiting for transfers between devices: 44.5 us -> 64.5 us
  starting transfers between devices: 43.1 us -> 59.3 us
  between operations: 1.01 us -> 14.6 us
  Pallas kernels: 18.3 us -> 13.6 us
  other arithmetic: 1.57 us -> 4.42 us
  local copies, waits for them, and re-layouts: 7.35 us -> 9.66 us
    all_to_all x2 -> x0, blocking collectives: 45.8 us -> none  [the longest x1 25.2 us: per_device(): lax.all_to_all(at.reshape(seq_count, rows_each, 2 * FEAT), SEQ, 0, 0, til...]
    all_gather x0 -> x1, waiting for transfers between devices: none -> 15.6 us  [per_device(): w_full = lax.all_gather(w, 'seq_1', axis=0)]
    ppermute x0 -> x4, starting transfers between devices: none -> 11.2 us  [the longest x2 6.8 us: swapped(): return (mine, lax.ppermute(given, 'seq_0', [(0, 1), (1, 0)]))]
    all_to_all x3 -> x4, waiting for transfers between devices: 34.6 us -> 39.7 us  [from_everyone(): return lax.all_to_all(copies, axis, split_axis=0, concat_axis=0, tiled=True)]
    pallas_call x1, Pallas kernels: 18.3 us -> 13.6 us  [attention(): pl.pallas_call(attention_kernel, grid=(heads,), in_specs=[whole(*x.shape)...]
    all_to_all x3 -> x4, starting transfers between devices: 17.8 us -> 22.3 us  [from_everyone(): return lax.all_to_all(copies, axis, split_axis=0, concat_axis=0, tiled=True)]
    ppermute x1, waiting for transfers between devices: 3.53 us -> 0.01 us  [extended(): lax.ppermute(lax.slice_in_dim(block, 0, width, axis=dim), axis, backward)]
    all_to_all x1, waiting for transfers between devices: 6.33 us -> 9.16 us  [per_device(): m_slice = jnp.sum(lax.all_to_all(m_part, 'seq_1', 0, 0, tiled=True), axis=0)]
  transfers between devices with their start and end apart: 8 -> 14, of which waited for: 5 -> 6; matrix products, arithmetic and copies ran while one was open for 5% -> 8% of each run, Pallas kernels for 0% -> 7%
where the time goes in v3:
time: 190 us; the launch traced here: 189 us
  waiting for transfers between devices  64.5 us (34%)
  starting transfers between devices  59.3 us (31%)
  blocking collectives  17.4 us (9%)
  between operations  14.6 us (8%)
  Pallas kernels  13.6 us (7%)
  local copies, waits for them, and re-layouts  9.66 us (5%)
  matrix products  5.58 us (3%)
  other arithmetic  4.42 us (2%)
    all_to_all x4, waiting for transfers between devices, from_everyone(): return lax.all_to_all(copies, axis, split_axis=0, concat_axis=0, tiled=True)  39.7 us
    all_to_all x4, starting transfers between devices, from_everyone(): return lax.all_to_all(copies, axis, split_axis=0, concat_axis=0, tiled=True)  22.3 us
    all_to_all x1, blocking collectives, per_device(): t = lax.all_to_all(t, PLANE, 0, 0, tiled=True)  17.4 us
    all_gather x1, waiting for transfers between devices, per_device(): w_full = lax.all_gather(w, 'seq_1', axis=0)  15.6 us
    pallas_call x1, Pallas kernels, attention(): pl.pallas_call(attention_kernel, grid=(heads,), in_specs=[whole(*x.shape)...  13.6 us
    all_to_all x1, starting transfers between devices, per_device(): m_slice = jnp.sum(lax.all_to_all(m_part, 'seq_1', 0, 0, tiled=True), axis=0)  11.2 us
    ppermute x2, starting transfers between devices, shifted(): lax.ppermute(value, axis, [(source, source + steps) for source in range(l...  10.2 us
    all_to_all x1, waiting for transfers between devices, per_device(): m_slice = jnp.sum(lax.all_to_all(m_part, 'seq_1', 0, 0, tiled=True), axis=0)  9.16 us
  transfers between devices with their start and end apart: 14, of which 6 were waited for; matrix products, arithmetic and copies ran while one was open for 8% of the time, Pallas kernels for 7%

profile of v3, /device:TPU:32, one launch (start us, length us, event | category | flops | bytes accessed | tf_op | source)
XLA Modules:
  0.0 189.0 jit_solution(10115552040042883297)
XLA Ops:
  7.2 3.8 %collective-permute-start.1 = (bf16[1,2,32,512]{3,2,1,0:T(8,128)(2,1)}, bf16[1,2,32,512]{3,2,1,0:T(8,128)(2,1)S(1)}, u32[]{:S(2)}, u32[]{:S(2)}) collective-permute-start(bf16[1,2,32,512]{3,2,1,0:T(8,128)(2,1)} %bitcast.189), channel_id=1, source_target_pairs={{0,8},{8,16},{16,24},{24,32},{32,40},{40,48},{48,56},{56,64},{64,7... | collective-permute-start | bytes 196616 | tf_op jit(solution)/shard_map/ppermute | solution.py:24
  11.0 6.4 %collective-permute-start = (bf16[1,2,32,512]{3,2,1,0:T(8,128)(2,1)}, bf16[1,2,32,512]{3,2,1,0:T(8,128)(2,1)S(1)}, u32[]{:S(2)}, u32[]{:S(2)}) collective-permute-start(bf16[1,2,32,512]{3,2,1,0:T(8,128)(2,1)} %bitcast.190), channel_id=1, source_target_pairs={{0,16},{8,24},{16,32},{24,40},{32,48},{40,56},{48,64},{56,72},{64,... | collective-permute-start | bytes 196616 | tf_op jit(solution)/shard_map/ppermute | solution.py:24
  17.4 0.9 broadcast_select_fusion.1
  18.3 3.4 %collective-permute-start.4 = (bf16[96,3,128]{2,0,1:T(8,128)(2,1)S(1)}, bf16[96,3,128]{2,0,1:T(8,128)(2,1)S(1)}, u32[]{:S(2)}, u32[]{:S(2)}) collective-permute-start(bf16[96,3,128]{2,0,1:T(8,128)(2,1)S(1)} %get-tuple-element.55), channel_id=1, source_target_pairs={{0,128},{128,0},{1,129},{129,1},{2,130},{130,2},{3,131},{131,3},{4... | collective-permute-start | bytes 221192 | tf_op jit(solution)/shard_map/ppermute | solution.py:267
  21.8 2.4 %collective-permute-start.5 = (s32[128]{0:T(128)}, s32[128]{0:T(128)S(1)}, u32[]{:S(2)}, u32[]{:S(2)}) collective-permute-start(s32[128]{0:T(128)} %param.11), channel_id=1, source_target_pairs={{0,128},{128,0},{1,129},{129,1},{2,130},{130,2},{3,131},{131,3},{4... | collective-permute-start | bytes 1544 | tf_op jit(solution)/shard_map/ppermute | solution.py:306
  27.0 1.3 collective-permute-start.3
  28.3 3.0 %collective-permute-start.2 = (bf16[3,1,32,512]{3,2,1,0:T(8,128)(2,1)S(1)}, bf16[3,1,32,512]{3,2,1,0:T(8,128)(2,1)S(1)}, u32[]{:S(2)}, u32[]{:S(2)}) collective-permute-start(bf16[3,1,32,512]{3,2,1,0:T(8,128)(2,1)S(1)} %get-tuple-element.50), channel_id=1, source_target_pairs={{0,1},{1,2},{2,3},{3,4},{4,5},{5,6},{6,7},{8,9},{9,10},{10,11},{11... | collective-permute-start | bytes 294920 | tf_op jit(solution)/shard_map/ppermute | solution.py:31
  33.1 11.2 %all-to-all-start = ((f32[16,12,128]{2,1,0:T(8,128)}), f32[16,12,128]{2,1,0:T(8,128)S(1)}, u32[]{:S(2)}, u32[]{:S(2)}) async-start(f32[16,12,128]{2,1,0:T(8,128)} %reshape.762), calls=%async_computation | async-start | bytes 262144 | tf_op jit(solution)/shard_map/all_to_all | solution.py:287
  49.7 9.2 %all-to-all-done = f32[16,12,128]{2,1,0:T(8,128)S(1)} async-done(((f32[16,12,128]{2,1,0:T(8,128)}), f32[16,12,128]{2,1,0:T(8,128)S(1)}, u32[]{:S(2)}, u32[]{:S(2)}) %all-to-all-start) | async-done | bytes 98336 | tf_op jit(solution)/shard_map/all_to_all | solution.py:287
  59.5 5.4 %all-to-all-start.1 = ((bf16[16,32,128]{2,1,0:T(8,128)(2,1)}), bf16[16,32,128]{2,1,0:T(8,128)(2,1)S(1)}, u32[]{:S(2)}, u32[]{:S(2)}) async-start(bf16[16,32,128]{2,1,0:T(8,128)(2,1)} %broadcast_in_dim.8), calls=%async_computation.1 | async-start | bytes 262144 | tf_op jit(solution)/shard_map/all_to_all | solution.py:40
  64.9 3.4 %collective-permute-start.6 = (bf16[128,128]{1,0:T(8,128)(2,1)S(1)}, bf16[128,128]{1,0:T(8,128)(2,1)S(1)}, u32[]{:S(2)}, u32[]{:S(2)}) collective-permute-start(bf16[128,128]{1,0:T(8,128)(2,1)S(1)} %get-tuple-element.63), channel_id=1, source_target_pairs={{0,128},{128,0},{1,129},{129,1},{2,130},{130,2},{3,131},{131,3},{4... | collective-permute-start | bytes 98312 | tf_op jit(solution)/shard_map/ppermute | solution.py:267
  68.8 10.5 %all-to-all-done.1 = bf16[16,32,128]{2,1,0:T(8,128)(2,1)S(1)} async-done(((bf16[16,32,128]{2,1,0:T(8,128)(2,1)}), bf16[16,32,128]{2,1,0:T(8,128)(2,1)S(1)}, u32[]{:S(2)}, u32[]{:S(2)}) %all-to-all-start.1) | async-done | bytes 131104 | tf_op jit(solution)/shard_map/all_to_all | solution.py:40
  80.2 5.4 %all-to-all-start.2 = ((bf16[16,16,8,128]{3,2,1,0:T(8,128)(2,1)}), bf16[16,16,8,128]{3,2,1,0:T(8,128)(2,1)S(1)}, u32[]{:S(2)}, u32[]{:S(2)}) async-start(bf16[16,16,8,128]{3,2,1,0:T(8,128)(2,1)} %broadcast_in_dim.18), calls=%async_computation.2 | async-start | bytes 1048576 | tf_op jit(solution)/shard_map/all_to_all | solution.py:40
  86.3 10.2 %all-to-all-done.2 = bf16[16,16,8,128]{3,2,1,0:T(8,128)(2,1)S(1)} async-done(((bf16[16,16,8,128]{3,2,1,0:T(8,128)(2,1)}), bf16[16,16,8,128]{3,2,1,0:T(8,128)(2,1)S(1)}, u32[]{:S(2)}, u32[]{:S(2)}) %all-to-all-start.2) | async-done | bytes 524320 | tf_op jit(solution)/shard_map/all_to_all | solution.py:40
  96.4 13.6 %attention.1 = (bf16[2,256,64]{2,1,0:T(8,128)(2,1)S(1)}, f32[384,64]{1,0:T(8,128)S(1)}, f32[64,64]{1,0:T(8,128)S(1)}) custom-call(bf16[2048,128]{1,0:T(8,128)(2,1)S(1)} %bitcast.185, bf16[192,128]{1,0:T(8,128)(2,1)S(1)} %reshape.764.high_ref, bf16[192,128]{1,0:T(8,128)(2,1)S(1)} %reshape.765.low_ref, f32[64,64]{1,0:T(8,128)S(1)} %convolution_multiply_fusion.gram_ref, ...), custom_call_target="tpu_custom_call" | custom-call | tf_op jit(solution)/shard_map/attention/pallas_call | solution.py:224
  110.1 15.6 %all-gather.2.cloned.1.call-done = bf16[16,2,96,384]{3,2,1,0:T(8,128)(2,1)} async-done(((bf16[1,2,96,384]{3,2,1,0:T(8,128)(2,1)}), bf16[16,2,96,384]{3,2,1,0:T(8,128)(2,1)}) %all-gather.2.cloned.1.call-update) | async-done | bytes 2359312 | tf_op jit(solution)/shard_map/all_gather | solution.py:288
  125.7 1.9 %copy.82 = bf16[16,2,96,384]{3,2,0,1:T(8,128)(2,1)S(1)} copy(bf16[16,2,96,384]{3,2,1,0:T(8,128)(2,1)} %all-gather.2.cloned.1.call-done) | data formatting | bytes 4718592 | tf_op jit(solution)/shard_map/all_gather | solution.py:288
  127.6 0.9 fusion.31
  129.2 17.4 %all_to_all.30 = bf16[32,16,384]{2,1,0:T(8,128)(2,1)S(1)} all-to-all(bf16[32,16,384]{2,1,0:T(8,128)(2,1)S(1)} %bitcast.199), channel_id=1, replica_groups=mesh['grp'=2,'seq_0'=2,'seq_1'=16,'head_0'=4,'head_1'=2] {'head_0','head..., dimensions={0} | all-to-all | bytes 786432 | tf_op jit(solution)/shard_map/all_to_all | solution.py:336
  147.3 8.3 %all-to-all-start.4 = ((bf16[16,16,384]{2,1,0:T(8,128)(2,1)}), bf16[16,16,384]{2,1,0:T(8,128)(2,1)S(1)}, u32[]{:S(2)}, u32[]{:S(2)}) async-start(bf16[16,16,384]{2,1,0:T(8,128)(2,1)} %broadcast_in_dim.19), calls=%async_computation.4 | async-start | bytes 393216 | tf_op jit(solution)/shard_map/all_to_all | solution.py:40
  155.7 1.9 %collective-permute-start.7 = (bf16[128,128]{0,1:T(8,128)(2,1)S(1)}, bf16[128,128]{0,1:T(8,128)(2,1)S(1)}, u32[]{:S(2)}, u32[]{:S(2)}) collective-permute-start(bf16[128,128]{0,1:T(8,128)(2,1)S(1)} %bitcast.234), channel_id=1, source_target_pairs={{0,128},{128,0},{1,129},{129,1},{2,130},{130,2},{3,131},{131,3},{4... | collective-permute-start | bytes 98312 | tf_op jit(solution)/shard_map/ppermute | solution.py:321
  157.7 14.0 %all-to-all-done.4 = bf16[16,16,384]{2,1,0:T(8,128)(2,1)S(1)} async-done(((bf16[16,16,384]{2,1,0:T(8,128)(2,1)}), bf16[16,16,384]{2,1,0:T(8,128)(2,1)S(1)}, u32[]{:S(2)}, u32[]{:S(2)}) %all-to-all-start.4) | async-done | bytes 196640 | tf_op jit(solution)/shard_map/all_to_all | solution.py:40
  172.5 3.3 %all-to-all-start.5 = ((f32[4,16,384]{2,1,0:T(8,128)}), f32[4,16,384]{2,1,0:T(8,128)S(1)}, u32[]{:S(2)}, u32[]{:S(2)}) async-start(f32[4,16,384]{2,1,0:T(8,128)} %broadcast_in_dim.20), calls=%async_computation.5 | async-start | bytes 196608 | tf_op jit(solution)/shard_map/all_to_all | solution.py:40
  176.6 5.0 %all-to-all-done.5 = f32[4,16,384]{2,1,0:T(8,128)S(1)} async-done(((f32[4,16,384]{2,1,0:T(8,128)}), f32[4,16,384]{2,1,0:T(8,128)S(1)}, u32[]{:S(2)}, u32[]{:S(2)}) %all-to-all-start.5) | async-done | bytes 98336 | tf_op jit(solution)/shard_map/all_to_all | solution.py:40
  (110 shorter events, 16.0 us)
Async XLA Ops:
  7.2 18.9 %collective-permute-start.1 = (bf16[1,2,32,512]{3,2,1,0:T(8,128)(2,1)}, bf16[1,2,32,512]{3,2,1,0:T(8,128)(2,1)S(1)}, u32[]{:S(2)}, u32[]{:S(2)}) collective-permute-start(bf16[1,2,32,512]{3,2,1,0:T(8,128)(2,1)} %bitcast.189), channel_id=1, source_target_pairs={{0,8},{8,16},{16,24},{24,32},{32,40},{40,48},{48,56},{56,64},{64,7... | collective-permute-start | bytes 196616 | tf_op jit(solution)/shard_map/ppermute | solution.py:24
  11.0 15.1 %collective-permute-start = (bf16[1,2,32,512]{3,2,1,0:T(8,128)(2,1)}, bf16[1,2,32,512]{3,2,1,0:T(8,128)(2,1)S(1)}, u32[]{:S(2)}, u32[]{:S(2)}) collective-permute-start(bf16[1,2,32,512]{3,2,1,0:T(8,128)(2,1)} %bitcast.190), channel_id=1, source_target_pairs={{0,16},{8,24},{16,32},{24,40},{32,48},{40,56},{48,64},{56,72},{64,... | collective-permute-start | bytes 196616 | tf_op jit(solution)/shard_map/ppermute | solution.py:24
  18.3 13.0 %collective-permute-start.4 = (bf16[96,3,128]{2,0,1:T(8,128)(2,1)S(1)}, bf16[96,3,128]{2,0,1:T(8,128)(2,1)S(1)}, u32[]{:S(2)}, u32[]{:S(2)}) collective-permute-start(bf16[96,3,128]{2,0,1:T(8,128)(2,1)S(1)} %get-tuple-element.55), channel_id=1, source_target_pairs={{0,128},{128,0},{1,129},{129,1},{2,130},{130,2},{3,131},{131,3},{4... | collective-permute-start | bytes 221192 | tf_op jit(solution)/shard_map/ppermute | solution.py:267
  21.8 46.9 %collective-permute-start.5 = (s32[128]{0:T(128)}, s32[128]{0:T(128)S(1)}, u32[]{:S(2)}, u32[]{:S(2)}) collective-permute-start(s32[128]{0:T(128)} %param.11), channel_id=1, source_target_pairs={{0,128},{128,0},{1,129},{129,1},{2,130},{130,2},{3,131},{131,3},{4... | collective-permute-start | bytes 1544 | tf_op jit(solution)/shard_map/ppermute | solution.py:306
  26.1 19.2 %copy-start.1 = (bf16[1,1,2,32,512]{4,3,2,1,0:T(8,128)(2,1)S(1)}, bf16[1,1,2,32,512]{4,3,2,1,0:T(8,128)(2,1)}, u32[]{:S(2)}) copy-start(bf16[1,1,2,32,512]{4,3,2,1,0:T(8,128)(2,1)} %param.8) | copy-start | bytes 196612
  27.0 18.2 %collective-permute-start.3 = (bf16[3,1,32,512]{3,2,1,0:T(8,128)(2,1)S(1)}, bf16[3,1,32,512]{3,2,1,0:T(8,128)(2,1)S(1)}, u32[]{:S(2)}, u32[]{:S(2)}) collective-permute-start(bf16[3,1,32,512]{3,2,1,0:T(8,128)(2,1)S(1)} %get-tuple-element.51), channel_id=1, source_target_pairs={{1,0},{2,1},{3,2},{4,3},{5,4},{6,5},{7,6},{9,8},{10,9},{11,10},{12... | collective-permute-start | bytes 294920 | tf_op jit(solution)/shard_map/ppermute | solution.py:34
  28.3 16.9 %collective-permute-start.2 = (bf16[3,1,32,512]{3,2,1,0:T(8,128)(2,1)S(1)}, bf16[3,1,32,512]{3,2,1,0:T(8,128)(2,1)S(1)}, u32[]{:S(2)}, u32[]{:S(2)}) collective-permute-start(bf16[3,1,32,512]{3,2,1,0:T(8,128)(2,1)S(1)} %get-tuple-element.50), channel_id=1, source_target_pairs={{0,1},{1,2},{2,3},{3,4},{4,5},{5,6},{6,7},{8,9},{9,10},{10,11},{11... | collective-permute-start | bytes 294920 | tf_op jit(solution)/shard_map/ppermute | solution.py:31
  32.2 13.4 %copy-start.2 = (bf16[3,3,3,512,16]{3,4,2,1,0:T(8,128)(2,1)S(1)}, bf16[3,3,3,512,16]{3,4,2,1,0:T(8,128)(2,1)}, u32[]{:S(2)}) copy-start(bf16[3,3,3,512,16]{3,4,2,1,0:T(8,128)(2,1)} %param.9) | copy-start | bytes 1327108
  33.1 25.8 %all-to-all-start = ((f32[16,12,128]{2,1,0:T(8,128)}), f32[16,12,128]{2,1,0:T(8,128)S(1)}, u32[]{:S(2)}, u32[]{:S(2)}) async-start(f32[16,12,128]{2,1,0:T(8,128)} %reshape.762), calls=%async_computation | async-start | bytes 262144 | tf_op jit(solution)/shard_map/all_to_all | solution.py:287
  44.3 2.1 %copy-start.6 = (f32[16]{0:T(128)S(1)}, f32[16]{0:T(128)}, u32[]{:S(2)}) copy-start(f32[16]{0:T(128)} %param.10) | copy-start | bytes 196
  44.3 81.3 %all-gather.2.cloned.1.call-start = ((), (), s32[]{:S(2)}) async-start(), calls=%async_computation.6 | async-start | bytes 2506752 | tf_op jit(solution)/shard_map/all_gather | solution.py:288
  45.6 19.3 %copy-start.3 = (bf16[1,128,256]{2,1,0:T(8,128)(2,1)S(1)}, bf16[1,128,256]{2,1,0:T(8,128)(2,1)}, u32[]{:S(2)}) copy-start(bf16[1,128,256]{2,1,0:T(8,128)(2,1)} %param.15) | copy-start | bytes 196612
  45.6 22.7 %copy-start = (bf16[64,3072]{1,0:T(8,128)(2,1)S(1)}, bf16[64,3072]{1,0:T(8,128)(2,1)}, u32[]{:S(2)}) copy-start(bf16[64,3072]{1,0:T(8,128)(2,1)} %param.12) | copy-start | bytes 1179652
  46.5 22.1 %copy-start.5 = (s32[128]{0:T(128)S(1)}, s32[128]{0:T(128)}, u32[]{:S(2)}) copy-start(s32[128]{0:T(128)} %param.11) | copy-start | bytes 1540
  59.5 19.8 %all-to-all-start.1 = ((bf16[16,32,128]{2,1,0:T(8,128)(2,1)}), bf16[16,32,128]{2,1,0:T(8,128)(2,1)S(1)}, u32[]{:S(2)}, u32[]{:S(2)}) async-start(bf16[16,32,128]{2,1,0:T(8,128)(2,1)} %broadcast_in_dim.8), calls=%async_computation.1 | async-start | bytes 262144 | tf_op jit(solution)/shard_map/all_to_all | solution.py:40
  64.9 21.1 %collective-permute-start.6 = (bf16[128,128]{1,0:T(8,128)(2,1)S(1)}, bf16[128,128]{1,0:T(8,128)(2,1)S(1)}, u32[]{:S(2)}, u32[]{:S(2)}) collective-permute-start(bf16[128,128]{1,0:T(8,128)(2,1)S(1)} %get-tuple-element.63), channel_id=1, source_target_pairs={{0,128},{128,0},{1,129},{129,1},{2,130},{130,2},{3,131},{131,3},{4... | collective-permute-start | bytes 98312 | tf_op jit(solution)/shard_map/ppermute | solution.py:267
  80.2 16.2 %all-to-all-start.2 = ((bf16[16,16,8,128]{3,2,1,0:T(8,128)(2,1)}), bf16[16,16,8,128]{3,2,1,0:T(8,128)(2,1)S(1)}, u32[]{:S(2)}, u32[]{:S(2)}) async-start(bf16[16,16,8,128]{3,2,1,0:T(8,128)(2,1)} %broadcast_in_dim.18), calls=%async_computation.2 | async-start | bytes 1048576 | tf_op jit(solution)/shard_map/all_to_all | solution.py:40
  127.6 1.0 copy-start.4
  147.3 24.5 %all-to-all-start.4 = ((bf16[16,16,384]{2,1,0:T(8,128)(2,1)}), bf16[16,16,384]{2,1,0:T(8,128)(2,1)S(1)}, u32[]{:S(2)}, u32[]{:S(2)}) async-start(bf16[16,16,384]{2,1,0:T(8,128)(2,1)} %broadcast_in_dim.19), calls=%async_computation.4 | async-start | bytes 393216 | tf_op jit(solution)/shard_map/all_to_all | solution.py:40
  155.7 20.1 %collective-permute-start.7 = (bf16[128,128]{0,1:T(8,128)(2,1)S(1)}, bf16[128,128]{0,1:T(8,128)(2,1)S(1)}, u32[]{:S(2)}, u32[]{:S(2)}) collective-permute-start(bf16[128,128]{0,1:T(8,128)(2,1)S(1)} %bitcast.234), channel_id=1, source_target_pairs={{0,128},{128,0},{1,129},{129,1},{2,130},{130,2},{3,131},{131,3},{4... | collective-permute-start | bytes 98312 | tf_op jit(solution)/shard_map/ppermute | solution.py:321
  172.5 9.1 %all-to-all-start.5 = ((f32[4,16,384]{2,1,0:T(8,128)}), f32[4,16,384]{2,1,0:T(8,128)S(1)}, u32[]{:S(2)}, u32[]{:S(2)}) async-start(f32[4,16,384]{2,1,0:T(8,128)} %broadcast_in_dim.20), calls=%async_computation.5 | async-start | bytes 196608 | tf_op jit(solution)/shard_map/all_to_all | solution.py:40
Sparse Core Ops, SparseCore 0:
  47.2 78.3 all-gather.1

commit v4 on v3

--- a/solution.py
+++ b/solution.py
@@ -24,35 +24,9 @@
     return lax.ppermute(value, axis, [(source, source + steps) for source in range(leading, last)])
 
 
-def extended(block, axis, dim, width):
-    count = lax.axis_size(axis)
-    forward = [(i, i + 1) for i in range(count - 1)]
-    backward = [(target, source) for source, target in forward]
-    low = lax.ppermute(
-        lax.slice_in_dim(block, block.shape[dim] - width, None, axis=dim), axis, forward
-    )
-    high = lax.ppermute(lax.slice_in_dim(block, 0, width, axis=dim), axis, backward)
-    return jnp.concatenate([low, block, high], axis=dim)
-
-
 def from_everyone(array, axis):
     copies = jnp.broadcast_to(array, (lax.axis_size(axis), *array.shape))
     return lax.all_to_all(copies, axis, split_axis=0, concat_axis=0, tiled=True)
-
-
-def encode_tile(tile, conv_weight, conv_bias):
-    frames, rows, columns, channels = tile.shape
-    earlier = [shifted(tile, SEQ, hop) for hop in (2, 1)]
-    stacked = jnp.concatenate(earlier + [tile], axis=0)
-    padded = extended(stacked, HEAD, 1, 1)
-    padded = jnp.pad(padded, ((0, 0), (0, 0), (1, 1), (0, 0)))
-    total = jnp.zeros((frames * rows * columns, conv_weight.shape[-1]), F32) + conv_bias
-    for a in range(3):
-        for b in range(3):
-            for e in range(3):
-                piece = padded[a : a + frames, b : b + rows, e : e + columns].reshape(-1, channels)
-                total = total + jnp.dot(piece, conv_weight[a, b, e], preferred_element_type=F32)
-    return total.astype(BF16).reshape(frames, rows, columns, conv_weight.shape[-1])
 
 
 def two(x):
@@ -73,6 +47,63 @@
 
 NT = ((1,), (1,))
 TN = ((0,), (0,))
+
+
+def conv_kernel(f_ref, w_ref, out_ref):
+    tile = f_ref[...]
+    spots, channels = tile.shape
+    half = spots // 2
+    cols = half // 2
+    lat = w_ref.shape[0] // 27
+    to = lax.broadcasted_iota(jnp.int32, (spots, spots), 0)
+    source = (to // cols % 2) * half + (to % cols) * 2 + to // half
+    pick = lax.broadcasted_iota(jnp.int32, (spots, spots), 1) == source
+    tile = mm(pick.astype(F32).astype(BF16), tile).astype(BF16)
+    zero = jnp.zeros((lat, channels), BF16)
+
+    def block(a, taps):
+        rows = []
+        for b in (2, 1, 0):
+            for e in taps:
+                at = ((a * 3 + b) * 3 + e) * lat if e is not None else 0
+                rows.append(zero if e is None else w_ref[at : at + lat, :])
+        return rows + [zero, zero]
+
+    row = lax.broadcasted_iota(jnp.int32, (cols, 128), 0)
+    sums = [0.0] * 3
+    for parity, here, there, shift in ((0, (1, 0), (None, 2), cols - 1), (1, (2, 1), (0, None), 1)):
+        weights = jnp.concatenate(
+            [w for taps in (here, there) for a in range(3) for w in block(a, taps)], axis=0
+        )
+        got = mm(tile[parity * half : (parity + 1) * half], weights, NT)
+        edge = cols - 1 if parity == 0 else 0
+        for a in range(3):
+            near = got[:, a * 128 : (a + 1) * 128]
+            far = got[:, (a + 3) * 128 : (a + 4) * 128]
+            for r in range(2):
+                moved = pltpu.roll(far[r * cols : (r + 1) * cols], shift, 0)
+                both = near[r * cols : (r + 1) * cols] + jnp.where(row == edge, 0.0, moved)
+                sums[a] = sums[a] + (both if r == 0 else pltpu.roll(both, 32, 1))
+    for a in range(3):
+        out_ref[a] = sums[a]
+
+
+def encode_tile(tile, conv_weight, conv_bias):
+    rows, columns, channels = tile.shape
+    lat = conv_weight.shape[-1]
+    weight = jnp.moveaxis(conv_weight, 4, 3).reshape(27 * lat, channels)
+    parts = pl.pallas_call(
+        conv_kernel,
+        out_shape=jax.ShapeDtypeStruct((3, columns // 2, 8 * lat), F32),
+        name="taps",
+    )(tile.reshape(rows * columns, channels), weight)
+    total = (parts[2] + shifted(parts[1], SEQ, 1)) + shifted(parts[0], SEQ, 2)
+    above, below = shifted(total, HEAD, 1), shifted(total, HEAD, -1)
+    own = total[:, 2 * lat : 6 * lat]
+    own = own + jnp.concatenate([above[:, 6 * lat :], below[:, : 2 * lat]], axis=1)
+    patch = (own + jnp.tile(conv_bias, 4)).astype(BF16)
+    first, second = jnp.split(patch, 2, axis=0)
+    return jnp.concatenate([first, second], axis=1)
 
 
 def attention_kernel(
@@ -198,7 +229,11 @@
     a_k = mm(q_scaled.astype(F32), grad, TN, HIGHEST)
     a_v = mm(cot.astype(F32), value, TN, HIGHEST)
     for t, a in enumerate((a_q, a_k, a_v)):
-        at_ref[pl.ds(pl.multiple_of(t * 2 * FEAT + odd * FEAT, FEAT), FEAT), :] = a
+        for side in range(2):
+
+            @pl.when(odd == side)
+            def _():
+                at_ref[t * FEAT : (t + 1) * FEAT, side * FEAT : (side + 1) * FEAT] = a
 
     @pl.when(head == heads - 1)
     def _():
@@ -228,10 +263,10 @@
             whole(*x.shape), whole(*high.shape), whole(*low.shape), whole(*gram.shape),
             whole(*row.shape), whole(*half.shape), per_head,
         ],
-        out_specs=[per_head, whole(2 * high.shape[0], FEAT), whole(*gram.shape)],
+        out_specs=[per_head, whole(*high.shape), whole(*gram.shape)],
         out_shape=[
             jax.ShapeDtypeStruct(cot.shape, BF16),
-            jax.ShapeDtypeStruct((2 * high.shape[0], FEAT), F32),
+            jax.ShapeDtypeStruct(high.shape, F32),
             jax.ShapeDtypeStruct(gram.shape, F32),
         ],
         scratch_shapes=[
@@ -269,39 +304,27 @@
     def in_order(mine, other):
         return jnp.where(far == 0, jnp.stack([mine, other]), jnp.stack([other, mine]))
 
-    w = in_order(*swapped(qkv_weight, 2)).reshape(2, depth, 3 * pair)
+    w = qkv_weight.reshape(depth, 3, 2, 2, HEAD_DIM)
+    w = jnp.transpose(w, (2, 1, 4, 3, 0)).reshape(2 * near_count, rows_each * 2, depth)
+    w_slice = lax.all_to_all(w, SEQ, 0, 0, tiled=True)
+    w_slice = jnp.transpose(w_slice, (1, 0, 2)).reshape(rows_each * 2, D)
     embed32 = embed_weight.astype(F32)
-    start = lax.axis_index("seq_1") * depth
-    m_part = 0.0
-    for k in range(2):
-        at = start + k * (D // 2)
-        gained = lax.dynamic_slice_in_dim(embed_weight, at, depth, 1).astype(F32)
-        gained = jnp.concatenate(
-            two(gained * lax.dynamic_slice_in_dim(norm_gain, at, depth, 0)), axis=0
-        )
-        m_part = m_part + lax.dot_general(
-            w[k], gained, (((0,), (1,)), ((), ())), preferred_element_type=F32
-        )
-    m_part = (m_part[:, :FEAT] + m_part[:, FEAT:]).reshape(3, 2, HEAD_DIM, FEAT)
-    m_part = jnp.transpose(m_part, (0, 2, 1, 3)).reshape(near_count, rows_each, 2 * FEAT)
-    m_slice = jnp.sum(lax.all_to_all(m_part, "seq_1", 0, 0, tiled=True), axis=0)
-    w_full = lax.all_gather(w, "seq_1", axis=0)
+    gained = jnp.concatenate(two(embed32 * norm_gain), axis=0)
+    m_slice = mm(w_slice, gained, NT)
+    m_slice = (m_slice[:, :FEAT] + m_slice[:, FEAT:]).reshape(rows_each, 2 * FEAT)
     gram = lax.dot_general(
         embed_weight, embed_weight, (((1,), (1,)), ((), ())), preferred_element_type=F32
     ) * (1.0 / D)
 
-    tile = encode_tile(features[0], conv_weight, conv_bias)
-    _, _, columns, channels = tile.shape
-    patch = jnp.transpose(tile.reshape(2, columns // 2, 2, channels), (1, 0, 2, 3))
-    patch = patch.reshape(2, columns // 4, FEAT)
-    patch = jnp.transpose(patch, (1, 0, 2)).reshape(columns // 4, 2 * FEAT)
-    own_rows = columns // 4
+    patch = encode_tile(features[0, 0], conv_weight, conv_bias)
+    token_order, grad_out, patch = lax.optimization_barrier((token_order, grad_out, patch))
+    own_rows = patch.shape[0]
     arrived = from_everyone(jnp.concatenate([patch, *two(m_slice)], axis=0), "seq_1")
     every = from_everyone(arrived[:, :own_rows], ("seq_0", *HEAD)).reshape(-1, 2 * FEAT)
     m_high = arrived[:, own_rows : own_rows + rows_each].reshape(rows, 2 * FEAT)
     m_low = arrived[:, own_rows + rows_each :].reshape(rows, 2 * FEAT)
 
-    per_patch_row = columns // 4
+    per_patch_row = own_rows
     head_count = lax.axis_size(HEAD)
     order = in_order(token_order, lax.ppermute(token_order, "seq_0", [(0, 1), (1, 0)]))
     order = order.reshape(-1, 1)
@@ -325,9 +348,10 @@
         jnp.concatenate([other, mine], axis=1),
     )[None]
 
-    a_both = jnp.concatenate(two(at), axis=1)
-    w_full = jnp.transpose(w_full, (1, 0, 2, 3)).reshape(D, 3 * pair)
-    t = mm(a_both, w_full, ((0,), (1,)))
+    at = lax.all_to_all(at.reshape(near_count, rows_each, 2 * FEAT), "seq_1", 0, 0, tiled=True)
+    a_slice = jnp.sum(at, axis=0).reshape(rows_each * 2, FEAT)
+    a_both = jnp.concatenate(two(a_slice), axis=1)
+    t = mm(a_both, w_slice, TN)
     t = t[:FEAT] + t[FEAT:]
     t = t * norm_gain - mm(b, embed32, precision=HIGHEST)
     parts = lax.axis_size(("grp", "seq_0"))

time: 190 us -> 164 us (0.86)
  blocking collectives: 17.4 us -> 34.5 us
  waiting for transfers between devices: 64.5 us -> 47.9 us
  between operations: 14.6 us -> 1.04 us
  starting transfers between devices: 59.3 us -> 52.3 us
  matrix products: 5.58 us -> 1.49 us
  other arithmetic: 4.42 us -> 1.75 us
  Pallas kernels: 13.6 us -> 16.2 us
    all_to_all x0 -> x1, blocking collectives: none -> 19.2 us  [per_device(): lax.all_to_all(at.reshape(near_count, rows_each, 2 * FEAT), 'seq_1', 0, 0...]
    all_gather x1 -> x0, waiting for transfers between devices: 15.6 us -> none  [per_device(): w_full = lax.all_gather(w, 'seq_1', axis=0)]
    all_to_all x4, starting transfers between devices: 22.3 us -> 17.7 us  [from_everyone(): return lax.all_to_all(copies, axis, split_axis=0, concat_axis=0, tiled=True)]
    ppermute x2 -> x0, starting transfers between devices: 4.33 us -> none  [the longest x1 3.04 us: extended(): lax.ppermute(lax.slice_in_dim(block, block.shape[dim] - width, None, axis...]
    ppermute x2 -> x4, starting transfers between devices: 10.2 us -> 14.5 us  [shifted(): lax.ppermute(value, axis, [(source, source + steps) for source in range(l...]
    all_to_all x4, waiting for transfers between devices: 39.7 us -> 35.5 us  [from_everyone(): return lax.all_to_all(copies, axis, split_axis=0, concat_axis=0, tiled=True)]
    dot_general x29 -> x0, matrix products: 3.88 us -> none  [the longest x27 3.55 us: encode_tile(): jnp.dot(piece, conv_weight[a, b, e], preferred_element_type=F32)]
    ppermute x2 -> x1, starting transfers between devices: 6.8 us -> 3.48 us  [swapped(): return (mine, lax.ppermute(given, 'seq_0', [(0, 1), (1, 0)]))]
  transfers between devices with their start and end apart: 14 -> 12, of which waited for: 6 -> 6; matrix products, arithmetic and copies ran while one was open for 8% -> 4% of each run, Pallas kernels for 7% -> 0%
where the time goes in v4:
time: 164 us; the launch traced here: 163 us
  starting transfers between devices  52.3 us (32%)
  waiting for transfers between devices  47.9 us (29%)
  blocking collectives  34.5 us (21%)
  Pallas kernels  16.2 us (10%)
  local copies, waits for them, and re-layouts  8.19 us (5%)
  other arithmetic  1.75 us (1%)
    all_to_all x4, waiting for transfers between devices, from_everyone(): return lax.all_to_all(copies, axis, split_axis=0, concat_axis=0, tiled=True)  35.5 us
    all_to_all x1, blocking collectives, per_device(): lax.all_to_all(at.reshape(near_count, rows_each, 2 * FEAT), 'seq_1', 0, 0...  19.2 us
    all_to_all x4, starting transfers between devices, from_everyone(): return lax.all_to_all(copies, axis, split_axis=0, concat_axis=0, tiled=True)  17.7 us
    all_to_all x1, blocking collectives, per_device(): t = lax.all_to_all(t, PLANE, 0, 0, tiled=True)  15.3 us
    ppermute x4, starting transfers between devices, shifted(): lax.ppermute(value, axis, [(source, source + steps) for source in range(l...  14.5 us
    pallas_call x1, Pallas kernels, attention(): pl.pallas_call(attention_kernel, grid=(heads,), in_specs=[whole(*x.shape)...  13.8 us
    all_to_all x1, starting transfers between devices, per_device(): w_slice = lax.all_to_all(w, SEQ, 0, 0, tiled=True)  12.4 us
    all_to_all x1, waiting for transfers between devices, per_device(): w_slice = lax.all_to_all(w, SEQ, 0, 0, tiled=True)  11.8 us
  transfers between devices with their start and end apart: 12, of which 6 were waited for; matrix products, arithmetic and copies ran while one was open for 4% of the time, Pallas kernels for 0%

profile of v4, /device:TPU:32, one launch (start us, length us, event | category | flops | bytes accessed | tf_op | source)
XLA Modules:
  0.0 163.3 jit_solution(3204229169165739441)
XLA Ops:
  0.7 2.3 %taps.1 = f32[3,16,128]{2,1,0:T(8,128)} custom-call(bf16[64,512]{1,0:T(8,128)(2,1)} %bitcast.62, bf16[432,512]{1,0:T(8,128)(2,1)} %bitcast.58), custom_call_target="tpu_custom_call" | custom-call | tf_op jit(solution)/shard_map/taps/pallas_call | solution.py:95
  3.7 3.8 %collective-permute-start = (f32[16,128]{1,0:T(8,128)S(1)}, f32[16,128]{1,0:T(8,128)S(1)}, u32[]{:S(2)}, u32[]{:S(2)}) collective-permute-start(f32[16,128]{1,0:T(8,128)S(1)} %get-tuple-element.32), channel_id=1, source_target_pairs={{0,8},{8,16},{16,24},{24,32},{32,40},{40,48},{48,56},{56,64},{64,7... | collective-permute-start | bytes 24584 | tf_op jit(solution)/shard_map/ppermute | solution.py:24
  7.5 6.4 %collective-permute-start.1 = (f32[16,128]{1,0:T(8,128)S(1)}, f32[16,128]{1,0:T(8,128)S(1)}, u32[]{:S(2)}, u32[]{:S(2)}) collective-permute-start(f32[16,128]{1,0:T(8,128)S(1)} %get-tuple-element.33), channel_id=1, source_target_pairs={{0,16},{8,24},{16,32},{24,40},{32,48},{40,56},{48,64},{56,72},{64,... | collective-permute-start | bytes 24584 | tf_op jit(solution)/shard_map/ppermute | solution.py:24
  13.9 1.1 copy.23
  15.0 0.9 copy.24
  15.9 12.4 %all-to-all-start = ((bf16[32,24,96]{2,1,0:T(8,128)(2,1)}), bf16[32,24,96]{2,1,0:T(8,128)(2,1)S(1)}, u32[]{:S(2)}, u32[]{:S(2)}) async-start(bf16[32,24,96]{2,1,0:T(8,128)(2,1)} %bitcast.8), calls=%async_computation | async-start | bytes 393216 | tf_op jit(solution)/shard_map/all_to_all | solution.py:309
  29.0 1.3 collective-permute-start.3
  30.3 3.0 %collective-permute-start.2 = (f32[16,128]{1,0:T(8,128)S(1)}, f32[16,128]{1,0:T(8,128)S(1)}, u32[]{:S(2)}, u32[]{:S(2)}) collective-permute-start(f32[16,128]{1,0:T(8,128)S(1)} %fusion.25), channel_id=1, source_target_pairs={{0,1},{1,2},{2,3},{3,4},{4,5},{5,6},{6,7},{8,9},{9,10},{10,11},{11... | collective-permute-start | bytes 24584 | tf_op jit(solution)/shard_map/ppermute | solution.py:24
  34.4 11.8 %all-to-all-done = bf16[32,24,96]{2,1,0:T(8,128)(2,1)S(1)} async-done(((bf16[32,24,96]{2,1,0:T(8,128)(2,1)}), bf16[32,24,96]{2,1,0:T(8,128)(2,1)S(1)}, u32[]{:S(2)}, u32[]{:S(2)}) %all-to-all-start) | async-done | bytes 147488 | tf_op jit(solution)/shard_map/all_to_all | solution.py:309
  47.7 4.7 %all-to-all-start.1 = ((bf16[16,32,128]{2,1,0:T(8,128)(2,1)}), bf16[16,32,128]{2,1,0:T(8,128)(2,1)S(1)}, u32[]{:S(2)}, u32[]{:S(2)}) async-start(bf16[16,32,128]{2,1,0:T(8,128)(2,1)} %broadcast_in_dim.15), calls=%async_computation.1 | async-start | bytes 262144 | tf_op jit(solution)/shard_map/all_to_all | solution.py:29
  52.7 2.4 %collective-permute-start.4 = (s32[128]{0:T(128)S(1)}, s32[128]{0:T(128)S(1)}, u32[]{:S(2)}, u32[]{:S(2)}) collective-permute-start(s32[128]{0:T(128)S(1)} %copy-done.4), channel_id=1, source_target_pairs={{0,128},{128,0},{1,129},{129,1},{2,130},{130,2},{3,131},{131,3},{4... | collective-permute-start | bytes 1544 | tf_op jit(solution)/shard_map/ppermute | solution.py:329
  55.1 3.5 %collective-permute-start.5 = (bf16[128,128]{1,0:T(8,128)(2,1)S(1)}, bf16[128,128]{1,0:T(8,128)(2,1)S(1)}, u32[]{:S(2)}, u32[]{:S(2)}) collective-permute-start(bf16[128,128]{1,0:T(8,128)(2,1)S(1)} %get-tuple-element.31), channel_id=1, source_target_pairs={{0,128},{128,0},{1,129},{129,1},{2,130},{130,2},{3,131},{131,3},{4... | collective-permute-start | bytes 98312 | tf_op jit(solution)/shard_map/ppermute | solution.py:302
  58.8 6.3 %all-to-all-done.1 = bf16[16,32,128]{2,1,0:T(8,128)(2,1)S(1)} async-done(((bf16[16,32,128]{2,1,0:T(8,128)(2,1)}), bf16[16,32,128]{2,1,0:T(8,128)(2,1)S(1)}, u32[]{:S(2)}, u32[]{:S(2)}) %all-to-all-start.1) | async-done | bytes 131104 | tf_op jit(solution)/shard_map/all_to_all | solution.py:29
  65.1 0.9 broadcast_in_dim.16
  66.0 4.5 %all-to-all-start.2 = ((bf16[16,16,8,128]{3,2,1,0:T(8,128)(2,1)}), bf16[16,16,8,128]{3,2,1,0:T(8,128)(2,1)S(1)}, u32[]{:S(2)}, u32[]{:S(2)}) async-start(bf16[16,16,8,128]{3,2,1,0:T(8,128)(2,1)} %broadcast_in_dim.16), calls=%async_computation.2 | async-start | bytes 1048576 | tf_op jit(solution)/shard_map/all_to_all | solution.py:29
  71.2 10.2 %all-to-all-done.2 = bf16[16,16,8,128]{3,2,1,0:T(8,128)(2,1)S(1)} async-done(((bf16[16,16,8,128]{3,2,1,0:T(8,128)(2,1)}), bf16[16,16,8,128]{3,2,1,0:T(8,128)(2,1)S(1)}, u32[]{:S(2)}, u32[]{:S(2)}) %all-to-all-start.2) | async-done | bytes 524320 | tf_op jit(solution)/shard_map/all_to_all | solution.py:29
  81.4 13.8 %attention.1 = (bf16[2,256,64]{2,1,0:T(8,128)(2,1)S(1)}, f32[192,128]{1,0:T(8,128)S(1)}, f32[64,64]{1,0:T(8,128)S(1)}) custom-call(bf16[2048,128]{1,0:T(8,128)(2,1)S(1)} %bitcast.50, bf16[192,128]{1,0:T(8,128)(2,1)S(1)} %reshape.597.high_ref, bf16[192,128]{1,0:T(8,128)(2,1)S(1)} %reshape.598.low_ref, f32[64,64]{1,0:T(8,128)S(1)} %convolution_multiply_fusion.gram_ref, ...), custom_call_target="tpu_custom_call" | custom-call | tf_op jit(solution)/shard_map/attention/pallas_call | solution.py:259
  95.3 19.2 %all_to_all.35 = f32[16,12,128]{2,1,0:T(8,128)S(1)} all-to-all(f32[16,12,128]{2,1,0:T(8,128)S(1)} %reshape.599), channel_id=1, replica_groups=mesh['grp'=2,'seq_0'=2,'seq_1'=16,'head_0'=4,'head_1'=2] {'seq_1'}, dimensions={0} | all-to-all | bytes 196608 | tf_op jit(solution)/shard_map/all_to_all | solution.py:351
  115.6 15.3 %all_to_all.36 = bf16[32,16,384]{2,1,0:T(8,128)(2,1)S(1)} all-to-all(bf16[32,16,384]{2,1,0:T(8,128)(2,1)S(1)} %bitcast.54), channel_id=1, replica_groups=mesh['grp'=2,'seq_0'=2,'seq_1'=16,'head_0'=4,'head_1'=2] {'head_0','head..., dimensions={0} | all-to-all | bytes 786432 | tf_op jit(solution)/shard_map/all_to_all | solution.py:360
  131.7 5.1 %all-to-all-start.5 = ((bf16[16,16,384]{2,1,0:T(8,128)(2,1)}), bf16[16,16,384]{2,1,0:T(8,128)(2,1)S(1)}, u32[]{:S(2)}, u32[]{:S(2)}) async-start(bf16[16,16,384]{2,1,0:T(8,128)(2,1)} %broadcast_in_dim.17), calls=%async_computation.5 | async-start | bytes 393216 | tf_op jit(solution)/shard_map/all_to_all | solution.py:29
  137.0 1.9 %collective-permute-start.6 = (bf16[128,128]{0,1:T(8,128)(2,1)S(1)}, bf16[128,128]{0,1:T(8,128)(2,1)S(1)}, u32[]{:S(2)}, u32[]{:S(2)}) collective-permute-start(bf16[128,128]{0,1:T(8,128)(2,1)S(1)} %bitcast.63), channel_id=1, source_target_pairs={{0,128},{128,0},{1,129},{129,1},{2,130},{130,2},{3,131},{131,3},{4... | collective-permute-start | bytes 98312 | tf_op jit(solution)/shard_map/ppermute | solution.py:344
  138.9 14.0 %all-to-all-done.5 = bf16[16,16,384]{2,1,0:T(8,128)(2,1)S(1)} async-done(((bf16[16,16,384]{2,1,0:T(8,128)(2,1)}), bf16[16,16,384]{2,1,0:T(8,128)(2,1)S(1)}, u32[]{:S(2)}, u32[]{:S(2)}) %all-to-all-start.5) | async-done | bytes 196640 | tf_op jit(solution)/shard_map/all_to_all | solution.py:29
  153.6 3.3 %all-to-all-start.6 = ((f32[4,16,384]{2,1,0:T(8,128)}), f32[4,16,384]{2,1,0:T(8,128)S(1)}, u32[]{:S(2)}, u32[]{:S(2)}) async-start(f32[4,16,384]{2,1,0:T(8,128)} %broadcast_in_dim.18), calls=%async_computation.6 | async-start | bytes 196608 | tf_op jit(solution)/shard_map/all_to_all | solution.py:29
  157.7 5.0 %all-to-all-done.6 = f32[4,16,384]{2,1,0:T(8,128)S(1)} async-done(((f32[4,16,384]{2,1,0:T(8,128)}), f32[4,16,384]{2,1,0:T(8,128)S(1)}, u32[]{:S(2)}, u32[]{:S(2)}) %all-to-all-start.6) | async-done | bytes 98336 | tf_op jit(solution)/shard_map/all_to_all | solution.py:29
  (64 shorter events, 9.1 us)
Async XLA Ops:
  0.6 32.7 %copy-start = (bf16[64,3072]{1,0:T(8,128)(2,1)S(1)}, bf16[64,3072]{1,0:T(8,128)(2,1)}, u32[]{:S(2)}) copy-start(bf16[64,3072]{1,0:T(8,128)(2,1)} %param.12) | copy-start | bytes 1179652
  0.6 32.7 %copy-start.2 = (f32[3072]{0:T(1024)S(1)}, f32[3072]{0:T(1024)}, u32[]{:S(2)}) copy-start(f32[3072]{0:T(1024)} %param.13) | copy-start | bytes 36868
  0.7 32.8 %copy-start.3 = (f32[16]{0:T(128)S(1)}, f32[16]{0:T(128)}, u32[]{:S(2)}) copy-start(f32[16]{0:T(128)} %param.10) | copy-start | bytes 196
  3.7 24.6 %collective-permute-start = (f32[16,128]{1,0:T(8,128)S(1)}, f32[16,128]{1,0:T(8,128)S(1)}, u32[]{:S(2)}, u32[]{:S(2)}) collective-permute-start(f32[16,128]{1,0:T(8,128)S(1)} %get-tuple-element.32), channel_id=1, source_target_pairs={{0,8},{8,16},{16,24},{24,32},{32,40},{40,48},{48,56},{56,64},{64,7... | collective-permute-start | bytes 24584 | tf_op jit(solution)/shard_map/ppermute | solution.py:24
  7.5 20.7 %collective-permute-start.1 = (f32[16,128]{1,0:T(8,128)S(1)}, f32[16,128]{1,0:T(8,128)S(1)}, u32[]{:S(2)}, u32[]{:S(2)}) collective-permute-start(f32[16,128]{1,0:T(8,128)S(1)} %get-tuple-element.33), channel_id=1, source_target_pairs={{0,16},{8,24},{16,32},{24,40},{32,48},{40,56},{48,64},{56,72},{64,... | collective-permute-start | bytes 24584 | tf_op jit(solution)/shard_map/ppermute | solution.py:24
  15.9 30.3 %all-to-all-start = ((bf16[32,24,96]{2,1,0:T(8,128)(2,1)}), bf16[32,24,96]{2,1,0:T(8,128)(2,1)S(1)}, u32[]{:S(2)}, u32[]{:S(2)}) async-start(bf16[32,24,96]{2,1,0:T(8,128)(2,1)} %bitcast.8), calls=%async_computation | async-start | bytes 393216 | tf_op jit(solution)/shard_map/all_to_all | solution.py:309
  29.0 5.2 %collective-permute-start.3 = (f32[16,128]{1,0:T(8,128)S(1)}, f32[16,128]{1,0:T(8,128)S(1)}, u32[]{:S(2)}, u32[]{:S(2)}) collective-permute-start(f32[16,128]{1,0:T(8,128)S(1)} %fusion.25), channel_id=1, source_target_pairs={{1,0},{2,1},{3,2},{4,3},{5,4},{6,5},{7,6},{9,8},{10,9},{11,10},{12... | collective-permute-start | bytes 24584 | tf_op jit(solution)/shard_map/ppermute | solution.py:24
  30.3 3.8 %collective-permute-start.2 = (f32[16,128]{1,0:T(8,128)S(1)}, f32[16,128]{1,0:T(8,128)S(1)}, u32[]{:S(2)}, u32[]{:S(2)}) collective-permute-start(f32[16,128]{1,0:T(8,128)S(1)} %fusion.25), channel_id=1, source_target_pairs={{0,1},{1,2},{2,3},{3,4},{4,5},{5,6},{6,7},{8,9},{9,10},{10,11},{11... | collective-permute-start | bytes 24584 | tf_op jit(solution)/shard_map/ppermute | solution.py:24
  46.3 6.4 %copy-start.4 = (s32[128]{0:T(128)S(1)}, s32[128]{0:T(128)}, u32[]{:S(2)}) copy-start(s32[128]{0:T(128)} %param.11) | copy-start | bytes 1540
  46.3 8.8 %copy-start.1 = (bf16[1,128,256]{2,1,0:T(8,128)(2,1)S(1)}, bf16[1,128,256]{2,1,0:T(8,128)(2,1)}, u32[]{:S(2)}) copy-start(bf16[1,128,256]{2,1,0:T(8,128)(2,1)} %param.15) | copy-start | bytes 196612
  47.7 17.3 %all-to-all-start.1 = ((bf16[16,32,128]{2,1,0:T(8,128)(2,1)}), bf16[16,32,128]{2,1,0:T(8,128)(2,1)S(1)}, u32[]{:S(2)}, u32[]{:S(2)}) async-start(bf16[16,32,128]{2,1,0:T(8,128)(2,1)} %broadcast_in_dim.15), calls=%async_computation.1 | async-start | bytes 262144 | tf_op jit(solution)/shard_map/all_to_all | solution.py:29
  52.7 5.9 %collective-permute-start.4 = (s32[128]{0:T(128)S(1)}, s32[128]{0:T(128)S(1)}, u32[]{:S(2)}, u32[]{:S(2)}) collective-permute-start(s32[128]{0:T(128)S(1)} %copy-done.4), channel_id=1, source_target_pairs={{0,128},{128,0},{1,129},{129,1},{2,130},{130,2},{3,131},{131,3},{4... | collective-permute-start | bytes 1544 | tf_op jit(solution)/shard_map/ppermute | solution.py:329
  55.1 15.9 %collective-permute-start.5 = (bf16[128,128]{1,0:T(8,128)(2,1)S(1)}, bf16[128,128]{1,0:T(8,128)(2,1)S(1)}, u32[]{:S(2)}, u32[]{:S(2)}) collective-permute-start(bf16[128,128]{1,0:T(8,128)(2,1)S(1)} %get-tuple-element.31), channel_id=1, source_target_pairs={{0,128},{128,0},{1,129},{129,1},{2,130},{130,2},{3,131},{131,3},{4... | collective-permute-start | bytes 98312 | tf_op jit(solution)/shard_map/ppermute | solution.py:302
  66.0 15.4 %all-to-all-start.2 = ((bf16[16,16,8,128]{3,2,1,0:T(8,128)(2,1)}), bf16[16,16,8,128]{3,2,1,0:T(8,128)(2,1)S(1)}, u32[]{:S(2)}, u32[]{:S(2)}) async-start(bf16[16,16,8,128]{3,2,1,0:T(8,128)(2,1)} %broadcast_in_dim.16), calls=%async_computation.2 | async-start | bytes 1048576 | tf_op jit(solution)/shard_map/all_to_all | solution.py:29
  131.7 21.3 %all-to-all-start.5 = ((bf16[16,16,384]{2,1,0:T(8,128)(2,1)}), bf16[16,16,384]{2,1,0:T(8,128)(2,1)S(1)}, u32[]{:S(2)}, u32[]{:S(2)}) async-start(bf16[16,16,384]{2,1,0:T(8,128)(2,1)} %broadcast_in_dim.17), calls=%async_computation.5 | async-start | bytes 393216 | tf_op jit(solution)/shard_map/all_to_all | solution.py:29
  137.0 20.0 %collective-permute-start.6 = (bf16[128,128]{0,1:T(8,128)(2,1)S(1)}, bf16[128,128]{0,1:T(8,128)(2,1)S(1)}, u32[]{:S(2)}, u32[]{:S(2)}) collective-permute-start(bf16[128,128]{0,1:T(8,128)(2,1)S(1)} %bitcast.63), channel_id=1, source_target_pairs={{0,128},{128,0},{1,129},{129,1},{2,130},{130,2},{3,131},{131,3},{4... | collective-permute-start | bytes 98312 | tf_op jit(solution)/shard_map/ppermute | solution.py:344
  153.6 9.1 %all-to-all-start.6 = ((f32[4,16,384]{2,1,0:T(8,128)}), f32[4,16,384]{2,1,0:T(8,128)S(1)}, u32[]{:S(2)}, u32[]{:S(2)}) async-start(f32[4,16,384]{2,1,0:T(8,128)} %broadcast_in_dim.18), calls=%async_computation.6 | async-start | bytes 196608 | tf_op jit(solution)/shard_map/all_to_all | solution.py:29

commit v5 on v4

--- a/solution.py
+++ b/solution.py
@@ -88,15 +88,19 @@
         out_ref[a] = sums[a]
 
 
-def encode_tile(tile, conv_weight, conv_bias):
+def taps(tile, conv_weight):
     rows, columns, channels = tile.shape
     lat = conv_weight.shape[-1]
     weight = jnp.moveaxis(conv_weight, 4, 3).reshape(27 * lat, channels)
-    parts = pl.pallas_call(
+    return pl.pallas_call(
         conv_kernel,
         out_shape=jax.ShapeDtypeStruct((3, columns // 2, 8 * lat), F32),
         name="taps",
     )(tile.reshape(rows * columns, channels), weight)
+
+
+def latent_patches(parts, conv_bias):
+    lat = conv_bias.shape[0]
     total = (parts[2] + shifted(parts[1], SEQ, 1)) + shifted(parts[0], SEQ, 2)
     above, below = shifted(total, HEAD, 1), shifted(total, HEAD, -1)
     own = total[:, 2 * lat : 6 * lat]
@@ -307,6 +311,9 @@
     w = qkv_weight.reshape(depth, 3, 2, 2, HEAD_DIM)
     w = jnp.transpose(w, (2, 1, 4, 3, 0)).reshape(2 * near_count, rows_each * 2, depth)
     w_slice = lax.all_to_all(w, SEQ, 0, 0, tiled=True)
+    parts = taps(features[0, 0], conv_weight)
+    parts, w_slice = lax.optimization_barrier((parts, w_slice))
+    patch = latent_patches(parts, conv_bias)
     w_slice = jnp.transpose(w_slice, (1, 0, 2)).reshape(rows_each * 2, D)
     embed32 = embed_weight.astype(F32)
     gained = jnp.concatenate(two(embed32 * norm_gain), axis=0)
@@ -316,7 +323,6 @@
         embed_weight, embed_weight, (((1,), (1,)), ((), ())), preferred_element_type=F32
     ) * (1.0 / D)
 
-    patch = encode_tile(features[0, 0], conv_weight, conv_bias)
     token_order, grad_out, patch = lax.optimization_barrier((token_order, grad_out, patch))
     own_rows = patch.shape[0]
     arrived = from_everyone(jnp.concatenate([patch, *two(m_slice)], axis=0), "seq_1")

time: 164 us -> 173 us (1.055)
  waiting for transfers between devices: 47.9 us -> 54.2 us
  starting transfers between devices: 52.3 us -> 56.5 us
    all_to_all x4, starting transfers between devices: 17.7 us -> 23.5 us  [from_everyone(): return lax.all_to_all(copies, axis, split_axis=0, concat_axis=0, tiled=True)]
    ppermute x4, starting transfers between devices: 14.5 us -> 8.96 us  [shifted(): lax.ppermute(value, axis, [(source, source + steps) for source in range(l...]
    all_to_all x1, starting transfers between devices: 12.4 us -> 16.3 us  [per_device(): w_slice = lax.all_to_all(w, SEQ, 0, 0, tiled=True)]
    all_to_all x1, waiting for transfers between devices: 11.8 us -> 15.1 us  [per_device(): w_slice = lax.all_to_all(w, SEQ, 0, 0, tiled=True)]
    all_to_all x4, waiting for transfers between devices: 35.5 us -> 37.4 us  [from_everyone(): return lax.all_to_all(copies, axis, split_axis=0, concat_axis=0, tiled=True)]
  transfers between devices with their start and end apart: 12 -> 12, of which waited for: 6 -> 8; matrix products, arithmetic and copies ran while one was open for 4% -> 3% of each run, Pallas kernels for 0% -> 1%
where the time goes in v5:
time: 173 us; the launch traced here: 172 us
  starting transfers between devices  56.5 us (33%)
  waiting for transfers between devices  54.2 us (31%)
  blocking collectives  33.4 us (19%)
  Pallas kernels  16.2 us (9%)
  local copies, waits for them, and re-layouts  8.19 us (5%)
    all_to_all x4, waiting for transfers between devices, from_everyone(): return lax.all_to_all(copies, axis, split_axis=0, concat_axis=0, tiled=True)  37.4 us
    all_to_all x4, starting transfers between devices, from_everyone(): return lax.all_to_all(copies, axis, split_axis=0, concat_axis=0, tiled=True)  23.5 us
    all_to_all x1, blocking collectives, per_device(): lax.all_to_all(at.reshape(near_count, rows_each, 2 * FEAT), 'seq_1', 0, 0...  18.1 us
    all_to_all x1, starting transfers between devices, per_device(): w_slice = lax.all_to_all(w, SEQ, 0, 0, tiled=True)  16.3 us
    all_to_all x1, blocking collectives, per_device(): t = lax.all_to_all(t, PLANE, 0, 0, tiled=True)  15.3 us
    all_to_all x1, waiting for transfers between devices, per_device(): w_slice = lax.all_to_all(w, SEQ, 0, 0, tiled=True)  15.1 us
    pallas_call x1, Pallas kernels, attention(): pl.pallas_call(attention_kernel, grid=(heads,), in_specs=[whole(*x.shape)...  13.9 us
    ppermute x4, starting transfers between devices, shifted(): lax.ppermute(value, axis, [(source, source + steps) for source in range(l...  8.96 us
  transfers between devices with their start and end apart: 12, of which 8 were waited for; matrix products, arithmetic and copies ran while one was open for 3% of the time, Pallas kernels for 1%

profile of v5, /device:TPU:32, one launch (start us, length us, event | category | flops | bytes accessed | tf_op | source)
XLA Modules:
  0.0 171.9 jit_solution(10111710507871717215)
XLA Ops:
  0.7 1.1 copy.23
  1.8 0.9 copy.24
  2.7 16.3 %all-to-all-start = ((bf16[32,24,96]{2,1,0:T(8,128)(2,1)}), bf16[32,24,96]{2,1,0:T(8,128)(2,1)S(1)}, u32[]{:S(2)}, u32[]{:S(2)}) async-start(bf16[32,24,96]{2,1,0:T(8,128)(2,1)} %bitcast.5), calls=%async_computation | async-start | bytes 393216 | tf_op jit(solution)/shard_map/all_to_all | solution.py:313
  19.7 2.3 %taps.1 = f32[3,16,128]{2,1,0:T(8,128)} custom-call(bf16[64,512]{1,0:T(8,128)(2,1)} %bitcast.58, bf16[432,512]{1,0:T(8,128)(2,1)} %bitcast.54), custom_call_target="tpu_custom_call" | custom-call | tf_op jit(solution)/shard_map/taps/pallas_call | solution.py:95
  22.1 15.1 %all-to-all-done = bf16[32,24,96]{2,1,0:T(8,128)(2,1)S(1)} async-done(((bf16[32,24,96]{2,1,0:T(8,128)(2,1)}), bf16[32,24,96]{2,1,0:T(8,128)(2,1)S(1)}, u32[]{:S(2)}, u32[]{:S(2)}) %all-to-all-start) | async-done | bytes 147488 | tf_op jit(solution)/shard_map/all_to_all | solution.py:313
  37.6 2.1 %collective-permute-start = (f32[16,128]{1,0:T(8,128)S(1)}, f32[16,128]{1,0:T(8,128)S(1)}, u32[]{:S(2)}, u32[]{:S(2)}) collective-permute-start(f32[16,128]{1,0:T(8,128)S(1)} %get-tuple-element.36), channel_id=1, source_target_pairs={{0,8},{8,16},{16,24},{24,32},{32,40},{40,48},{48,56},{56,64},{64,7... | collective-permute-start | bytes 24584 | tf_op jit(solution)/shard_map/ppermute | solution.py:24
  39.7 2.6 %collective-permute-start.1 = (f32[16,128]{1,0:T(8,128)S(1)}, f32[16,128]{1,0:T(8,128)S(1)}, u32[]{:S(2)}, u32[]{:S(2)}) collective-permute-start(f32[16,128]{1,0:T(8,128)S(1)} %get-tuple-element.37), channel_id=1, source_target_pairs={{0,16},{8,24},{16,32},{24,40},{32,48},{40,56},{48,64},{56,72},{64,... | collective-permute-start | bytes 24584 | tf_op jit(solution)/shard_map/ppermute | solution.py:24
  43.6 1.3 collective-permute-start.3
  44.9 3.0 %collective-permute-start.2 = (f32[16,128]{1,0:T(8,128)S(1)}, f32[16,128]{1,0:T(8,128)S(1)}, u32[]{:S(2)}, u32[]{:S(2)}) collective-permute-start(f32[16,128]{1,0:T(8,128)S(1)} %fusion.25), channel_id=1, source_target_pairs={{0,1},{1,2},{2,3},{3,4},{4,5},{5,6},{6,7},{8,9},{9,10},{10,11},{11... | collective-permute-start | bytes 24584 | tf_op jit(solution)/shard_map/ppermute | solution.py:24
  49.7 8.8 %all-to-all-start.1 = ((bf16[16,32,128]{2,1,0:T(8,128)(2,1)}), bf16[16,32,128]{2,1,0:T(8,128)(2,1)S(1)}, u32[]{:S(2)}, u32[]{:S(2)}) async-start(bf16[16,32,128]{2,1,0:T(8,128)(2,1)} %broadcast_in_dim.15), calls=%async_computation.1 | async-start | bytes 262144 | tf_op jit(solution)/shard_map/all_to_all | solution.py:29
  58.7 3.3 %collective-permute-start.4 = (s32[128]{0:T(128)S(1)}, s32[128]{0:T(128)S(1)}, u32[]{:S(2)}, u32[]{:S(2)}) collective-permute-start(s32[128]{0:T(128)S(1)} %copy-done.4), channel_id=1, source_target_pairs={{0,128},{128,0},{1,129},{129,1},{2,130},{130,2},{3,131},{131,3},{4... | collective-permute-start | bytes 1544 | tf_op jit(solution)/shard_map/ppermute | solution.py:335
  62.0 2.5 %collective-permute-start.5 = (bf16[128,128]{1,0:T(8,128)(2,1)S(1)}, bf16[128,128]{1,0:T(8,128)(2,1)S(1)}, u32[]{:S(2)}, u32[]{:S(2)}) collective-permute-start(bf16[128,128]{1,0:T(8,128)(2,1)S(1)} %get-tuple-element.35), channel_id=1, source_target_pairs={{0,128},{128,0},{1,129},{129,1},{2,130},{130,2},{3,131},{131,3},{4... | collective-permute-start | bytes 98312 | tf_op jit(solution)/shard_map/ppermute | solution.py:306
  64.7 8.2 %all-to-all-done.1 = bf16[16,32,128]{2,1,0:T(8,128)(2,1)S(1)} async-done(((bf16[16,32,128]{2,1,0:T(8,128)(2,1)}), bf16[16,32,128]{2,1,0:T(8,128)(2,1)S(1)}, u32[]{:S(2)}, u32[]{:S(2)}) %all-to-all-start.1) | async-done | bytes 131104 | tf_op jit(solution)/shard_map/all_to_all | solution.py:29
  73.0 0.9 broadcast_in_dim.16
  73.9 6.3 %all-to-all-start.2 = ((bf16[16,16,8,128]{3,2,1,0:T(8,128)(2,1)}), bf16[16,16,8,128]{3,2,1,0:T(8,128)(2,1)S(1)}, u32[]{:S(2)}, u32[]{:S(2)}) async-start(bf16[16,16,8,128]{3,2,1,0:T(8,128)(2,1)} %broadcast_in_dim.16), calls=%async_computation.2 | async-start | bytes 1048576 | tf_op jit(solution)/shard_map/all_to_all | solution.py:29
  80.9 10.2 %all-to-all-done.2 = bf16[16,16,8,128]{3,2,1,0:T(8,128)(2,1)S(1)} async-done(((bf16[16,16,8,128]{3,2,1,0:T(8,128)(2,1)}), bf16[16,16,8,128]{3,2,1,0:T(8,128)(2,1)S(1)}, u32[]{:S(2)}, u32[]{:S(2)}) %all-to-all-start.2) | async-done | bytes 524320 | tf_op jit(solution)/shard_map/all_to_all | solution.py:29
  91.0 13.9 %attention.1 = (bf16[2,256,64]{2,1,0:T(8,128)(2,1)S(1)}, f32[192,128]{1,0:T(8,128)S(1)}, f32[64,64]{1,0:T(8,128)S(1)}) custom-call(bf16[2048,128]{1,0:T(8,128)(2,1)S(1)} %bitcast.46, bf16[192,128]{1,0:T(8,128)(2,1)S(1)} %reshape.597.high_ref, bf16[192,128]{1,0:T(8,128)(2,1)S(1)} %reshape.598.low_ref, f32[64,64]{1,0:T(8,128)S(1)} %convolution_multiply_fusion.gram_ref, ...), custom_call_target="tpu_custom_call" | custom-call | tf_op jit(solution)/shard_map/attention/pallas_call | solution.py:263
  104.9 18.1 %all_to_all.35 = f32[16,12,128]{2,1,0:T(8,128)S(1)} all-to-all(f32[16,12,128]{2,1,0:T(8,128)S(1)} %reshape.599), channel_id=1, replica_groups=mesh['grp'=2,'seq_0'=2,'seq_1'=16,'head_0'=4,'head_1'=2] {'seq_1'}, dimensions={0} | all-to-all | bytes 196608 | tf_op jit(solution)/shard_map/all_to_all | solution.py:357
  124.2 15.3 %all_to_all.36 = bf16[32,16,384]{2,1,0:T(8,128)(2,1)S(1)} all-to-all(bf16[32,16,384]{2,1,0:T(8,128)(2,1)S(1)} %bitcast.50), channel_id=1, replica_groups=mesh['grp'=2,'seq_0'=2,'seq_1'=16,'head_0'=4,'head_1'=2] {'head_0','head..., dimensions={0} | all-to-all | bytes 786432 | tf_op jit(solution)/shard_map/all_to_all | solution.py:366
  140.2 5.1 %all-to-all-start.5 = ((bf16[16,16,384]{2,1,0:T(8,128)(2,1)}), bf16[16,16,384]{2,1,0:T(8,128)(2,1)S(1)}, u32[]{:S(2)}, u32[]{:S(2)}) async-start(bf16[16,16,384]{2,1,0:T(8,128)(2,1)} %broadcast_in_dim.17), calls=%async_computation.5 | async-start | bytes 393216 | tf_op jit(solution)/shard_map/all_to_all | solution.py:29
  145.6 1.9 %collective-permute-start.6 = (bf16[128,128]{0,1:T(8,128)(2,1)S(1)}, bf16[128,128]{0,1:T(8,128)(2,1)S(1)}, u32[]{:S(2)}, u32[]{:S(2)}) collective-permute-start(bf16[128,128]{0,1:T(8,128)(2,1)S(1)} %bitcast.59), channel_id=1, source_target_pairs={{0,128},{128,0},{1,129},{129,1},{2,130},{130,2},{3,131},{131,3},{4... | collective-permute-start | bytes 98312 | tf_op jit(solution)/shard_map/ppermute | solution.py:350
  147.5 14.0 %all-to-all-done.5 = bf16[16,16,384]{2,1,0:T(8,128)(2,1)S(1)} async-done(((bf16[16,16,384]{2,1,0:T(8,128)(2,1)}), bf16[16,16,384]{2,1,0:T(8,128)(2,1)S(1)}, u32[]{:S(2)}, u32[]{:S(2)}) %all-to-all-start.5) | async-done | bytes 196640 | tf_op jit(solution)/shard_map/all_to_all | solution.py:29
  162.2 3.3 %all-to-all-start.6 = ((f32[4,16,384]{2,1,0:T(8,128)}), f32[4,16,384]{2,1,0:T(8,128)S(1)}, u32[]{:S(2)}, u32[]{:S(2)}) async-start(f32[4,16,384]{2,1,0:T(8,128)} %broadcast_in_dim.18), calls=%async_computation.6 | async-start | bytes 196608 | tf_op jit(solution)/shard_map/all_to_all | solution.py:29
  166.3 5.0 %all-to-all-done.6 = f32[4,16,384]{2,1,0:T(8,128)S(1)} async-done(((f32[4,16,384]{2,1,0:T(8,128)}), f32[4,16,384]{2,1,0:T(8,128)S(1)}, u32[]{:S(2)}, u32[]{:S(2)}) %all-to-all-start.6) | async-done | bytes 98336 | tf_op jit(solution)/shard_map/all_to_all | solution.py:29
  (64 shorter events, 9.5 us)
Async XLA Ops:
  0.6 21.4 %copy-start = (bf16[64,3072]{1,0:T(8,128)(2,1)S(1)}, bf16[64,3072]{1,0:T(8,128)(2,1)}, u32[]{:S(2)}) copy-start(bf16[64,3072]{1,0:T(8,128)(2,1)} %param.12) | copy-start | bytes 1179652
  0.6 21.4 %copy-start.3 = (f32[3072]{0:T(1024)S(1)}, f32[3072]{0:T(1024)}, u32[]{:S(2)}) copy-start(f32[3072]{0:T(1024)} %param.13) | copy-start | bytes 36868
  2.7 34.6 %all-to-all-start = ((bf16[32,24,96]{2,1,0:T(8,128)(2,1)}), bf16[32,24,96]{2,1,0:T(8,128)(2,1)S(1)}, u32[]{:S(2)}, u32[]{:S(2)}) async-start(bf16[32,24,96]{2,1,0:T(8,128)(2,1)} %bitcast.5), calls=%async_computation | async-start | bytes 393216 | tf_op jit(solution)/shard_map/all_to_all | solution.py:313
  22.0 15.6 %copy-start.1 = (f32[3,16,128]{2,1,0:T(8,128)S(1)}, f32[3,16,128]{2,1,0:T(8,128)}, u32[]{:S(2)}) copy-start(f32[3,16,128]{2,1,0:T(8,128)} %taps.1) | copy-start | bytes 73732
  37.3 21.4 %copy-start.4 = (s32[128]{0:T(128)S(1)}, s32[128]{0:T(128)}, u32[]{:S(2)}) copy-start(s32[128]{0:T(128)} %param.11) | copy-start | bytes 1540
  37.3 24.7 %copy-start.2 = (bf16[1,128,256]{2,1,0:T(8,128)(2,1)S(1)}, bf16[1,128,256]{2,1,0:T(8,128)(2,1)}, u32[]{:S(2)}) copy-start(bf16[1,128,256]{2,1,0:T(8,128)(2,1)} %param.15) | copy-start | bytes 196612
  37.6 5.5 %collective-permute-start = (f32[16,128]{1,0:T(8,128)S(1)}, f32[16,128]{1,0:T(8,128)S(1)}, u32[]{:S(2)}, u32[]{:S(2)}) collective-permute-start(f32[16,128]{1,0:T(8,128)S(1)} %get-tuple-element.36), channel_id=1, source_target_pairs={{0,8},{8,16},{16,24},{24,32},{32,40},{40,48},{48,56},{56,64},{64,7... | collective-permute-start | bytes 24584 | tf_op jit(solution)/shard_map/ppermute | solution.py:24
  39.7 3.9 %collective-permute-start.1 = (f32[16,128]{1,0:T(8,128)S(1)}, f32[16,128]{1,0:T(8,128)S(1)}, u32[]{:S(2)}, u32[]{:S(2)}) collective-permute-start(f32[16,128]{1,0:T(8,128)S(1)} %get-tuple-element.37), channel_id=1, source_target_pairs={{0,16},{8,24},{16,32},{24,40},{32,48},{40,56},{48,64},{56,72},{64,... | collective-permute-start | bytes 24584 | tf_op jit(solution)/shard_map/ppermute | solution.py:24
  43.6 5.2 %collective-permute-start.3 = (f32[16,128]{1,0:T(8,128)S(1)}, f32[16,128]{1,0:T(8,128)S(1)}, u32[]{:S(2)}, u32[]{:S(2)}) collective-permute-start(f32[16,128]{1,0:T(8,128)S(1)} %fusion.25), channel_id=1, source_target_pairs={{1,0},{2,1},{3,2},{4,3},{5,4},{6,5},{7,6},{9,8},{10,9},{11,10},{12... | collective-permute-start | bytes 24584 | tf_op jit(solution)/shard_map/ppermute | solution.py:24
  44.9 3.8 %collective-permute-start.2 = (f32[16,128]{1,0:T(8,128)S(1)}, f32[16,128]{1,0:T(8,128)S(1)}, u32[]{:S(2)}, u32[]{:S(2)}) collective-permute-start(f32[16,128]{1,0:T(8,128)S(1)} %fusion.25), channel_id=1, source_target_pairs={{0,1},{1,2},{2,3},{3,4},{4,5},{5,6},{6,7},{8,9},{9,10},{10,11},{11... | collective-permute-start | bytes 24584 | tf_op jit(solution)/shard_map/ppermute | solution.py:24
  49.7 23.3 %all-to-all-start.1 = ((bf16[16,32,128]{2,1,0:T(8,128)(2,1)}), bf16[16,32,128]{2,1,0:T(8,128)(2,1)S(1)}, u32[]{:S(2)}, u32[]{:S(2)}) async-start(bf16[16,32,128]{2,1,0:T(8,128)(2,1)} %broadcast_in_dim.15), calls=%async_computation.1 | async-start | bytes 262144 | tf_op jit(solution)/shard_map/all_to_all | solution.py:29
  58.7 5.9 %collective-permute-start.4 = (s32[128]{0:T(128)S(1)}, s32[128]{0:T(128)S(1)}, u32[]{:S(2)}, u32[]{:S(2)}) collective-permute-start(s32[128]{0:T(128)S(1)} %copy-done.4), channel_id=1, source_target_pairs={{0,128},{128,0},{1,129},{129,1},{2,130},{130,2},{3,131},{131,3},{4... | collective-permute-start | bytes 1544 | tf_op jit(solution)/shard_map/ppermute | solution.py:335
  62.0 18.6 %collective-permute-start.5 = (bf16[128,128]{1,0:T(8,128)(2,1)S(1)}, bf16[128,128]{1,0:T(8,128)(2,1)S(1)}, u32[]{:S(2)}, u32[]{:S(2)}) collective-permute-start(bf16[128,128]{1,0:T(8,128)(2,1)S(1)} %get-tuple-element.35), channel_id=1, source_target_pairs={{0,128},{128,0},{1,129},{129,1},{2,130},{130,2},{3,131},{131,3},{4... | collective-permute-start | bytes 98312 | tf_op jit(solution)/shard_map/ppermute | solution.py:306
  73.9 17.2 %all-to-all-start.2 = ((bf16[16,16,8,128]{3,2,1,0:T(8,128)(2,1)}), bf16[16,16,8,128]{3,2,1,0:T(8,128)(2,1)S(1)}, u32[]{:S(2)}, u32[]{:S(2)}) async-start(bf16[16,16,8,128]{3,2,1,0:T(8,128)(2,1)} %broadcast_in_dim.16), calls=%async_computation.2 | async-start | bytes 1048576 | tf_op jit(solution)/shard_map/all_to_all | solution.py:29
  140.2 21.3 %all-to-all-start.5 = ((bf16[16,16,384]{2,1,0:T(8,128)(2,1)}), bf16[16,16,384]{2,1,0:T(8,128)(2,1)S(1)}, u32[]{:S(2)}, u32[]{:S(2)}) async-start(bf16[16,16,384]{2,1,0:T(8,128)(2,1)} %broadcast_in_dim.17), calls=%async_computation.5 | async-start | bytes 393216 | tf_op jit(solution)/shard_map/all_to_all | solution.py:29
  145.6 20.0 %collective-permute-start.6 = (bf16[128,128]{0,1:T(8,128)(2,1)S(1)}, bf16[128,128]{0,1:T(8,128)(2,1)S(1)}, u32[]{:S(2)}, u32[]{:S(2)}) collective-permute-start(bf16[128,128]{0,1:T(8,128)(2,1)S(1)} %bitcast.59), channel_id=1, source_target_pairs={{0,128},{128,0},{1,129},{129,1},{2,130},{130,2},{3,131},{131,3},{4... | collective-permute-start | bytes 98312 | tf_op jit(solution)/shard_map/ppermute | solution.py:350
  162.2 9.1 %all-to-all-start.6 = ((f32[4,16,384]{2,1,0:T(8,128)}), f32[4,16,384]{2,1,0:T(8,128)S(1)}, u32[]{:S(2)}, u32[]{:S(2)}) async-start(f32[4,16,384]{2,1,0:T(8,128)} %broadcast_in_dim.18), calls=%async_computation.6 | async-start | bytes 196608 | tf_op jit(solution)/shard_map/all_to_all | solution.py:29

commit v6 on v4

--- a/solution.py
+++ b/solution.py
@@ -11,7 +11,6 @@
 FEAT = 64
 SEQ = ("seq_0", "seq_1")
 HEAD = ("head_0", "head_1")
-PLANE = ("head_0", "head_1", "grp", "seq_0")
 F32 = jnp.float32
 BF16 = jnp.bfloat16
 CHUNK = 512
@@ -113,13 +112,13 @@
 ):
     head = pl.program_id(0)
     heads = pl.num_programs(0)
-    pairs = x_ref.shape[0]
+    pairs = both.shape[0]
     factor = HEAD_DIM**-0.5
     zero = jnp.zeros((FEAT, FEAT), BF16)
 
     @pl.when(head == 0)
     def _():
-        x = x_ref[...]
+        x = x_ref[:, : pairs // x_ref.shape[0], :].reshape(pairs, 2 * FEAT)
         pieces = [
             jnp.concatenate(
                 [jnp.concatenate([g, zero], axis=1), jnp.concatenate([zero, g], axis=1)], axis=0
@@ -251,9 +250,8 @@
         b_ref[...] = ((full[:FEAT, :FEAT] + full[FEAT:, FEAT:]) + own_part) * (1.0 / D)
 
 
-def attention(x, high, low, gram, row, half, cot):
+def attention(x, pairs, high, low, gram, row, half, cot):
     heads, count, _ = cot.shape
-    pairs = x.shape[0]
     whole = lambda *shape: pl.BlockSpec(shape, lambda i: (0,) * len(shape))
     per_head = pl.BlockSpec((1, count, HEAD_DIM), lambda i: (i, 0, 0))
     return pl.pallas_call(
@@ -307,11 +305,21 @@
     w = qkv_weight.reshape(depth, 3, 2, 2, HEAD_DIM)
     w = jnp.transpose(w, (2, 1, 4, 3, 0)).reshape(2 * near_count, rows_each * 2, depth)
     w_slice = lax.all_to_all(w, SEQ, 0, 0, tiled=True)
+    w_blocks = w_slice
     w_slice = jnp.transpose(w_slice, (1, 0, 2)).reshape(rows_each * 2, D)
     embed32 = embed_weight.astype(F32)
     gained = jnp.concatenate(two(embed32 * norm_gain), axis=0)
     m_slice = mm(w_slice, gained, NT)
     m_slice = (m_slice[:, :FEAT] + m_slice[:, FEAT:]).reshape(rows_each, 2 * FEAT)
+    columns = lax.axis_index(HEAD) * lax.axis_size(("grp", "seq_0"))
+    columns = (columns + lax.axis_index(("grp", "seq_0"))) * depth
+    gain_own = lax.dynamic_slice_in_dim(norm_gain, columns, depth, 0)
+    embed_own = lax.dynamic_slice_in_dim(embed32, columns, depth, 1)
+    b_each = FEAT // 2 // near_count
+    b_at = lax.axis_index("seq_1") * b_each
+    embed_own = jnp.concatenate(
+        [lax.dynamic_slice_in_dim(embed_own, b_at + k, b_each, 0) for k in (0, FEAT // 2)], axis=0
+    )
     gram = lax.dot_general(
         embed_weight, embed_weight, (((1,), (1,)), ((), ())), preferred_element_type=F32
     ) * (1.0 / D)
@@ -320,24 +328,35 @@
     token_order, grad_out, patch = lax.optimization_barrier((token_order, grad_out, patch))
     own_rows = patch.shape[0]
     arrived = from_everyone(jnp.concatenate([patch, *two(m_slice)], axis=0), "seq_1")
-    every = from_everyone(arrived[:, :own_rows], ("seq_0", *HEAD)).reshape(-1, 2 * FEAT)
+    far_count, head_count = lax.axis_size("seq_0"), lax.axis_size(HEAD)
+    plane = far_count * head_count
+    mine = w_blocks.reshape(head_count, -1, far_count, rows_each * 2, depth)
+    mine = jnp.swapaxes(lax.dynamic_index_in_dim(mine, lax.axis_index("grp"), 1, False), 0, 1)
+    mine = mine.reshape(plane, rows_each * 2, depth)
+    mine = jnp.pad(mine, ((0, 0), (0, 0), (0, 2 * FEAT - depth)))
+    latents = arrived[:, :own_rows].reshape(1, -1, 2 * FEAT)
+    pairs_each = latents.shape[1]
+    latents = jnp.broadcast_to(latents, (plane, pairs_each, 2 * FEAT))
+    every = lax.all_to_all(
+        jnp.concatenate([latents, mine], axis=1), ("seq_0", *HEAD), 0, 0, tiled=True
+    )
+    w_own = every[:, pairs_each:, :depth].reshape(-1, depth)
     m_high = arrived[:, own_rows : own_rows + rows_each].reshape(rows, 2 * FEAT)
     m_low = arrived[:, own_rows + rows_each :].reshape(rows, 2 * FEAT)
 
     per_patch_row = own_rows
-    head_count = lax.axis_size(HEAD)
     order = in_order(token_order, lax.ppermute(token_order, "seq_0", [(0, 1), (1, 0)]))
     order = order.reshape(-1, 1)
     j = order % (2 * per_patch_row)
     i = (order // (2 * per_patch_row)) % head_count
     f = order // (2 * per_patch_row * head_count)
-    plane = (f // near_count) * head_count + i
-    row = (plane * near_count + f % near_count) * per_patch_row + j % per_patch_row
+    at_plane = (f // near_count) * head_count + i
+    row = (at_plane * near_count + f % near_count) * per_patch_row + j % per_patch_row
     half = j // per_patch_row
 
     cot = in_order(*swapped(grad_out[0], 1)).reshape(-1, 2, HEAD_DIM)
     out, at, b = attention(
-        every, m_high, m_low, gram, row, half, jnp.transpose(cot, (1, 0, 2))
+        every, plane * pairs_each, m_high, m_low, gram, row, half, jnp.transpose(cot, (1, 0, 2))
     )
     out = jnp.transpose(out, (1, 0, 2)).reshape(2, -1, pair)
     mine = jnp.where(far == 0, out[0], out[1])
@@ -348,19 +367,28 @@
         jnp.concatenate([other, mine], axis=1),
     )[None]
 
-    at = lax.all_to_all(at.reshape(near_count, rows_each, 2 * FEAT), "seq_1", 0, 0, tiled=True)
-    a_slice = jnp.sum(at, axis=0).reshape(rows_each * 2, FEAT)
-    a_both = jnp.concatenate(two(a_slice), axis=1)
-    t = mm(a_both, w_slice, TN)
-    t = t[:FEAT] + t[FEAT:]
-    t = t * norm_gain - mm(b, embed32, precision=HIGHEST)
-    parts = lax.axis_size(("grp", "seq_0"))
-    t = jnp.transpose(t.reshape(parts, FEAT // parts, head_count, -1), (2, 0, 1, 3))
-    t = t.astype(BF16).reshape(parts * head_count, FEAT // parts, -1)
-    t = lax.all_to_all(t, PLANE, 0, 0, tiled=True)
-    t = jnp.sum(t.astype(F32), axis=0).astype(BF16)
-    t = jnp.sum(from_everyone(t, "seq_1").astype(F32), axis=0)
-    embed_grad = from_everyone(t, ("grp", "seq_0")).reshape(FEAT, -1)
+    first, second = jnp.split(b, 2, axis=0)
+    b = jnp.concatenate([first, second], axis=1)
+    at = jnp.concatenate(
+        [
+            at.reshape(near_count, rows_each, 2 * FEAT),
+            b.reshape(near_count, b_each, 2 * FEAT),
+        ],
+        axis=1,
+    )
+    at = jnp.sum(lax.all_to_all(at, "seq_1", 0, 0, tiled=True), axis=0)
+    at = from_everyone(at, ("grp", "seq_0", *HEAD))
+    at = jnp.sum(at.reshape(-1, plane, *at.shape[1:]), axis=0)
+    a_both = jnp.concatenate(two(at[:, :rows_each].reshape(-1, FEAT)), axis=1)
+    t = mm(a_both, w_own, TN)
+    t = (t[:FEAT] + t[FEAT:]) * gain_own
+    b_rows = jnp.sum(at[:, rows_each:], axis=0).reshape(b_each, 2, FEAT)
+    t = t - mm(jnp.swapaxes(b_rows, 0, 1).reshape(-1, FEAT), embed_own, TN, HIGHEST)
+    parts = FEAT * depth // (D // head_count)
+    t = jnp.swapaxes(t.reshape(FEAT // parts, parts, depth), 0, 1).reshape(parts, -1)
+    t = jnp.sum(from_everyone(t.astype(BF16), "seq_1").astype(F32), axis=0)
+    t = from_everyone(t, ("grp", "seq_0")).reshape(-1, parts, FEAT // parts, depth)
+    embed_grad = jnp.transpose(t, (2, 1, 0, 3)).reshape(FEAT, -1)
     return (attended, embed_grad)
 
 

time: 164 us -> 164 us (level)
  blocking collectives: 34.5 us -> 19.1 us
  waiting for transfers between devices: 47.9 us -> 57.3 us
  starting transfers between devices: 52.3 us -> 58 us
    all_to_all x2 -> x1, blocking collectives: 34.5 us -> 19.1 us  [per_device(): at = jnp.sum(lax.all_to_all(at, 'seq_1', 0, 0, tiled=True), axis=0)]
    all_to_all x0 -> x1, waiting for transfers between devices: none -> 11.1 us  [per_device(): lax.all_to_all(jnp.concatenate([latents, mine], axis=1), ('seq_0', *HEAD)...]
    all_to_all x0 -> x1, starting transfers between devices: none -> 4.6 us  [per_device(): lax.all_to_all(jnp.concatenate([latents, mine], axis=1), ('seq_0', *HEAD)...]
    all_to_all x4, waiting for transfers between devices: 35.5 us -> 33.8 us  [from_everyone(): return lax.all_to_all(copies, axis, split_axis=0, concat_axis=0, tiled=True)]
  transfers between devices with their start and end apart: 12 -> 13, of which waited for: 6 -> 7; matrix products, arithmetic and copies ran while one was open for 4% -> 4% of each run, Pallas kernels for 0% -> 0%
where the time goes in v6:
time: 164 us; the launch traced here: 163 us
  starting transfers between devices  58 us (35%)
  waiting for transfers between devices  57.3 us (35%)
  blocking collectives  19.1 us (12%)
  Pallas kernels  16.2 us (10%)
  local copies, waits for them, and re-layouts  7.89 us (5%)
  other arithmetic  2.76 us (2%)
    all_to_all x4, waiting for transfers between devices, from_everyone(): return lax.all_to_all(copies, axis, split_axis=0, concat_axis=0, tiled=True)  33.8 us
    all_to_all x1, blocking collectives, per_device(): at = jnp.sum(lax.all_to_all(at, 'seq_1', 0, 0, tiled=True), axis=0)  19.1 us
    all_to_all x4, starting transfers between devices, from_everyone(): return lax.all_to_all(copies, axis, split_axis=0, concat_axis=0, tiled=True)  18.2 us
    ppermute x4, starting transfers between devices, shifted(): lax.ppermute(value, axis, [(source, source + steps) for source in range(l...  14.5 us
    pallas_call x1, Pallas kernels, attention(): pl.pallas_call(attention_kernel, grid=(heads,), in_specs=[whole(*x.shape)...  13.8 us
    all_to_all x1, starting transfers between devices, per_device(): w_slice = lax.all_to_all(w, SEQ, 0, 0, tiled=True)  12.4 us
    all_to_all x1, waiting for transfers between devices, per_device(): w_slice = lax.all_to_all(w, SEQ, 0, 0, tiled=True)  11.8 us
    all_to_all x1, waiting for transfers between devices, per_device(): lax.all_to_all(jnp.concatenate([latents, mine], axis=1), ('seq_0', *HEAD)...  11.1 us
  transfers between devices with their start and end apart: 13, of which 7 were waited for; matrix products, arithmetic and copies ran while one was open for 4% of the time, Pallas kernels for 0%

profile of v6, /device:TPU:32, one launch (start us, length us, event | category | flops | bytes accessed | tf_op | source)
XLA Modules:
  0.0 163.4 jit_solution(1803532774512494090)
XLA Ops:
  0.6 2.3 %taps.1 = f32[3,16,128]{2,1,0:T(8,128)} custom-call(bf16[64,512]{1,0:T(8,128)(2,1)} %bitcast.74, bf16[432,512]{1,0:T(8,128)(2,1)} %bitcast.67), custom_call_target="tpu_custom_call" | custom-call | tf_op jit(solution)/shard_map/taps/pallas_call | solution.py:94
  3.7 5.2 %collective-permute-start.1 = (f32[16,128]{1,0:T(8,128)S(1)}, f32[16,128]{1,0:T(8,128)S(1)}, u32[]{:S(2)}, u32[]{:S(2)}) collective-permute-start(f32[16,128]{1,0:T(8,128)S(1)} %get-tuple-element.45), channel_id=1, source_target_pairs={{0,16},{8,24},{16,32},{24,40},{32,48},{40,56},{48,64},{56,72},{64,... | collective-permute-start | bytes 24584 | tf_op jit(solution)/shard_map/ppermute | solution.py:23
  8.9 5.0 %collective-permute-start = (f32[16,128]{1,0:T(8,128)S(1)}, f32[16,128]{1,0:T(8,128)S(1)}, u32[]{:S(2)}, u32[]{:S(2)}) collective-permute-start(f32[16,128]{1,0:T(8,128)S(1)} %get-tuple-element.44), channel_id=1, source_target_pairs={{0,8},{8,16},{16,24},{24,32},{32,40},{40,48},{48,56},{56,64},{64,7... | collective-permute-start | bytes 24584 | tf_op jit(solution)/shard_map/ppermute | solution.py:23
  14.1 0.9 copy.105
  15.0 12.4 %all-to-all-start = ((bf16[32,24,96]{2,1,0:T(8,128)(2,1)}), bf16[32,24,96]{2,1,0:T(8,128)(2,1)S(1)}, u32[]{:S(2)}, u32[]{:S(2)}) async-start(bf16[32,24,96]{2,1,0:T(8,128)(2,1)} %bitcast.8), calls=%async_computation | async-start | bytes 393216 | tf_op jit(solution)/shard_map/all_to_all | solution.py:307
  28.2 1.3 collective-permute-start.3
  29.4 3.0 %collective-permute-start.2 = (f32[16,128]{1,0:T(8,128)S(1)}, f32[16,128]{1,0:T(8,128)S(1)}, u32[]{:S(2)}, u32[]{:S(2)}) collective-permute-start(f32[16,128]{1,0:T(8,128)S(1)} %fusion.30), channel_id=1, source_target_pairs={{0,1},{1,2},{2,3},{3,4},{4,5},{5,6},{6,7},{8,9},{9,10},{10,11},{11... | collective-permute-start | bytes 24584 | tf_op jit(solution)/shard_map/ppermute | solution.py:23
  33.5 11.8 %all-to-all-done = bf16[32,24,96]{2,1,0:T(8,128)(2,1)S(1)} async-done(((bf16[32,24,96]{2,1,0:T(8,128)(2,1)}), bf16[32,24,96]{2,1,0:T(8,128)(2,1)S(1)}, u32[]{:S(2)}, u32[]{:S(2)}) %all-to-all-start) | async-done | bytes 147488 | tf_op jit(solution)/shard_map/all_to_all | solution.py:307
  46.8 4.7 %all-to-all-start.1 = ((bf16[16,32,128]{2,1,0:T(8,128)(2,1)}), bf16[16,32,128]{2,1,0:T(8,128)(2,1)S(1)}, u32[]{:S(2)}, u32[]{:S(2)}) async-start(bf16[16,32,128]{2,1,0:T(8,128)(2,1)} %broadcast_in_dim.22), calls=%async_computation.1 | async-start | bytes 262144 | tf_op jit(solution)/shard_map/all_to_all | solution.py:28
  51.8 2.4 %collective-permute-start.4 = (s32[128]{0:T(128)S(1)}, s32[128]{0:T(128)S(1)}, u32[]{:S(2)}, u32[]{:S(2)}) collective-permute-start(s32[128]{0:T(128)S(1)} %copy-done.5), channel_id=1, source_target_pairs={{0,128},{128,0},{1,129},{129,1},{2,130},{130,2},{3,131},{131,3},{4... | collective-permute-start | bytes 1544 | tf_op jit(solution)/shard_map/ppermute | solution.py:348
  54.2 3.5 %collective-permute-start.5 = (bf16[128,128]{1,0:T(8,128)(2,1)S(1)}, bf16[128,128]{1,0:T(8,128)(2,1)S(1)}, u32[]{:S(2)}, u32[]{:S(2)}) collective-permute-start(bf16[128,128]{1,0:T(8,128)(2,1)S(1)} %get-tuple-element.41), channel_id=1, source_target_pairs={{0,128},{128,0},{1,129},{129,1},{2,130},{130,2},{3,131},{131,3},{4... | collective-permute-start | bytes 98312 | tf_op jit(solution)/shard_map/ppermute | solution.py:300
  57.7 6.4 %all-to-all-done.1 = bf16[16,32,128]{2,1,0:T(8,128)(2,1)S(1)} async-done(((bf16[16,32,128]{2,1,0:T(8,128)(2,1)}), bf16[16,32,128]{2,1,0:T(8,128)(2,1)S(1)}, u32[]{:S(2)}, u32[]{:S(2)}) %all-to-all-start.1) | async-done | bytes 131104 | tf_op jit(solution)/shard_map/all_to_all | solution.py:28
  64.2 0.9 fusion.5
  65.1 4.6 %all-to-all-start.2 = ((bf16[16,152,128]{2,1,0:T(8,128)(2,1)}), bf16[16,152,128]{2,1,0:T(8,128)(2,1)S(1)}, u32[]{:S(2)}, u32[]{:S(2)}) async-start(bf16[16,152,128]{2,1,0:T(8,128)(2,1)} %fusion.5), calls=%async_computation.2 | async-start | bytes 1245184 | tf_op jit(solution)/shard_map/all_to_all | solution.py:340
  70.6 11.1 %all-to-all-done.2.x_ref = bf16[16,152,128]{2,1,0:T(8,128)(2,1)S(1)} async-done(((bf16[16,152,128]{2,1,0:T(8,128)(2,1)}), bf16[16,152,128]{2,1,0:T(8,128)(2,1)S(1)}, u32[]{:S(2)}, u32[]{:S(2)}) %all-to-all-start.2) | async-done | bytes 622624 | tf_op jit(solution)/shard_map/all_to_all | solution.py:340
  81.7 13.8 %attention.1 = (bf16[2,256,64]{2,1,0:T(8,128)(2,1)S(1)}, f32[192,128]{1,0:T(8,128)S(1)}, f32[64,64]{1,0:T(8,128)S(1)}) custom-call(bf16[16,152,128]{2,1,0:T(8,128)(2,1)S(1)} %all-to-all-done.2.x_ref, bf16[192,128]{1,0:T(8,128)(2,1)S(1)} %reshape.621.high_ref, bf16[192,128]{1,0:T(8,128)(2,1)S(1)} %reshape.622.low_ref, ...), custom_call_target="tpu_custom_call" | custom-call | tf_op jit(solution)/shard_map/attention/pallas_call | solution.py:257
  95.7 19.1 %all_to_all.35 = f32[16,14,128]{2,1,0:T(8,128)S(1)} all-to-all(f32[16,14,128]{2,1,0:T(8,128)S(1)} %pad_maximum_fusion), channel_id=1, replica_groups=mesh['grp'=2,'seq_0'=2,'seq_1'=16,'head_0'=4,'head_1'=2] {'seq_1'}, dimensions={0} | all-to-all | bytes 229376 | tf_op jit(solution)/shard_map/all_to_all | solution.py:379
  115.5 5.1 %all-to-all-start.4 = ((f32[32,14,128]{2,1,0:T(8,128)}), f32[32,14,128]{2,1,0:T(8,128)S(1)}, u32[]{:S(2)}, u32[]{:S(2)}) async-start(f32[32,14,128]{2,1,0:T(8,128)} %broadcast_in_dim.25), calls=%async_computation.4 | async-start | bytes 524288 | tf_op jit(solution)/shard_map/all_to_all | solution.py:28
  120.8 8.7 %all-to-all-done.4 = f32[32,14,128]{2,1,0:T(8,128)S(1)} async-done(((f32[32,14,128]{2,1,0:T(8,128)}), f32[32,14,128]{2,1,0:T(8,128)S(1)}, u32[]{:S(2)}, u32[]{:S(2)}) %all-to-all-start.4) | async-done | bytes 229408 | tf_op jit(solution)/shard_map/all_to_all | solution.py:28
  131.2 5.1 %all-to-all-start.5 = ((bf16[16,16,384]{2,1,0:T(8,128)(2,1)}), bf16[16,16,384]{2,1,0:T(8,128)(2,1)S(1)}, u32[]{:S(2)}, u32[]{:S(2)}) async-start(bf16[16,16,384]{2,1,0:T(8,128)(2,1)} %broadcast_in_dim.26), calls=%async_computation.5 | async-start | bytes 393216 | tf_op jit(solution)/shard_map/all_to_all | solution.py:28
  136.4 2.5 %collective-permute-start.6 = (bf16[128,128]{0,1:T(8,128)(2,1)S(1)}, bf16[128,128]{0,1:T(8,128)(2,1)S(1)}, u32[]{:S(2)}, u32[]{:S(2)}) collective-permute-start(bf16[128,128]{0,1:T(8,128)(2,1)S(1)} %bitcast.75), channel_id=1, source_target_pairs={{0,128},{128,0},{1,129},{129,1},{2,130},{130,2},{3,131},{131,3},{4... | collective-permute-start | bytes 98312 | tf_op jit(solution)/shard_map/ppermute | solution.py:363
  139.0 13.7 %all-to-all-done.5 = bf16[16,16,384]{2,1,0:T(8,128)(2,1)S(1)} async-done(((bf16[16,16,384]{2,1,0:T(8,128)(2,1)}), bf16[16,16,384]{2,1,0:T(8,128)(2,1)S(1)}, u32[]{:S(2)}, u32[]{:S(2)}) %all-to-all-start.5) | async-done | bytes 196640 | tf_op jit(solution)/shard_map/all_to_all | solution.py:28
  153.3 3.3 %all-to-all-start.6 = ((f32[4,16,384]{2,1,0:T(8,128)}), f32[4,16,384]{2,1,0:T(8,128)S(1)}, u32[]{:S(2)}, u32[]{:S(2)}) async-start(f32[4,16,384]{2,1,0:T(8,128)} %broadcast_in_dim.27), calls=%async_computation.6 | async-start | bytes 196608 | tf_op jit(solution)/shard_map/all_to_all | solution.py:28
  157.4 5.0 %all-to-all-done.6 = f32[4,16,384]{2,1,0:T(8,128)S(1)} async-done(((f32[4,16,384]{2,1,0:T(8,128)}), f32[4,16,384]{2,1,0:T(8,128)S(1)}, u32[]{:S(2)}, u32[]{:S(2)}) %all-to-all-start.6) | async-done | bytes 98336 | tf_op jit(solution)/shard_map/all_to_all | solution.py:28
  (82 shorter events, 10.5 us)
Async XLA Ops:
  0.6 13.3 %copy-start.1 = (bf16[96,3,256]{2,0,1:T(8,128)(2,1)S(1)}, bf16[96,3,256]{2,0,1:T(8,128)(2,1)}, u32[]{:S(2)}) copy-start(bf16[96,3,256]{2,0,1:T(8,128)(2,1)} %param.14) | copy-start | bytes 442372
  3.0 29.5 %copy-start = (bf16[64,3072]{1,0:T(8,128)(2,1)S(1)}, bf16[64,3072]{1,0:T(8,128)(2,1)}, u32[]{:S(2)}) copy-start(bf16[64,3072]{1,0:T(8,128)(2,1)} %param.12) | copy-start | bytes 1179652
  3.0 29.5 %copy-start.3 = (f32[3072]{0:T(1024)S(1)}, f32[3072]{0:T(1024)}, u32[]{:S(2)}) copy-start(f32[3072]{0:T(1024)} %param.13) | copy-start | bytes 36868
  3.7 23.7 %collective-permute-start.1 = (f32[16,128]{1,0:T(8,128)S(1)}, f32[16,128]{1,0:T(8,128)S(1)}, u32[]{:S(2)}, u32[]{:S(2)}) collective-permute-start(f32[16,128]{1,0:T(8,128)S(1)} %get-tuple-element.45), channel_id=1, source_target_pairs={{0,16},{8,24},{16,32},{24,40},{32,48},{40,56},{48,64},{56,72},{64,... | collective-permute-start | bytes 24584 | tf_op jit(solution)/shard_map/ppermute | solution.py:23
  8.9 18.5 %collective-permute-start = (f32[16,128]{1,0:T(8,128)S(1)}, f32[16,128]{1,0:T(8,128)S(1)}, u32[]{:S(2)}, u32[]{:S(2)}) collective-permute-start(f32[16,128]{1,0:T(8,128)S(1)} %get-tuple-element.44), channel_id=1, source_target_pairs={{0,8},{8,16},{16,24},{24,32},{32,40},{40,48},{48,56},{56,64},{64,7... | collective-permute-start | bytes 24584 | tf_op jit(solution)/shard_map/ppermute | solution.py:23
  15.0 30.3 %all-to-all-start = ((bf16[32,24,96]{2,1,0:T(8,128)(2,1)}), bf16[32,24,96]{2,1,0:T(8,128)(2,1)S(1)}, u32[]{:S(2)}, u32[]{:S(2)}) async-start(bf16[32,24,96]{2,1,0:T(8,128)(2,1)} %bitcast.8), calls=%async_computation | async-start | bytes 393216 | tf_op jit(solution)/shard_map/all_to_all | solution.py:307
  27.4 5.2 %copy-start.4 = (f32[16]{0:T(128)S(1)}, f32[16]{0:T(128)}, u32[]{:S(2)}) copy-start(f32[16]{0:T(128)} %param.10) | copy-start | bytes 196
  28.2 5.2 %collective-permute-start.3 = (f32[16,128]{1,0:T(8,128)S(1)}, f32[16,128]{1,0:T(8,128)S(1)}, u32[]{:S(2)}, u32[]{:S(2)}) collective-permute-start(f32[16,128]{1,0:T(8,128)S(1)} %fusion.30), channel_id=1, source_target_pairs={{1,0},{2,1},{3,2},{4,3},{5,4},{6,5},{7,6},{9,8},{10,9},{11,10},{12... | collective-permute-start | bytes 24584 | tf_op jit(solution)/shard_map/ppermute | solution.py:23
  29.4 3.8 %collective-permute-start.2 = (f32[16,128]{1,0:T(8,128)S(1)}, f32[16,128]{1,0:T(8,128)S(1)}, u32[]{:S(2)}, u32[]{:S(2)}) collective-permute-start(f32[16,128]{1,0:T(8,128)S(1)} %fusion.30), channel_id=1, source_target_pairs={{0,1},{1,2},{2,3},{3,4},{4,5},{5,6},{6,7},{8,9},{9,10},{10,11},{11... | collective-permute-start | bytes 24584 | tf_op jit(solution)/shard_map/ppermute | solution.py:23
  46.1 5.7 %copy-start.5 = (s32[128]{0:T(128)S(1)}, s32[128]{0:T(128)}, u32[]{:S(2)}) copy-start(s32[128]{0:T(128)} %param.11) | copy-start | bytes 1540
  46.1 8.0 %copy-start.2 = (bf16[1,128,256]{2,1,0:T(8,128)(2,1)S(1)}, bf16[1,128,256]{2,1,0:T(8,128)(2,1)}, u32[]{:S(2)}) copy-start(bf16[1,128,256]{2,1,0:T(8,128)(2,1)} %param.15) | copy-start | bytes 196612
  46.8 17.3 %all-to-all-start.1 = ((bf16[16,32,128]{2,1,0:T(8,128)(2,1)}), bf16[16,32,128]{2,1,0:T(8,128)(2,1)S(1)}, u32[]{:S(2)}, u32[]{:S(2)}) async-start(bf16[16,32,128]{2,1,0:T(8,128)(2,1)} %broadcast_in_dim.22), calls=%async_computation.1 | async-start | bytes 262144 | tf_op jit(solution)/shard_map/all_to_all | solution.py:28
  51.8 18.0 %collective-permute-start.4 = (s32[128]{0:T(128)S(1)}, s32[128]{0:T(128)S(1)}, u32[]{:S(2)}, u32[]{:S(2)}) collective-permute-start(s32[128]{0:T(128)S(1)} %copy-done.5), channel_id=1, source_target_pairs={{0,128},{128,0},{1,129},{129,1},{2,130},{130,2},{3,131},{131,3},{4... | collective-permute-start | bytes 1544 | tf_op jit(solution)/shard_map/ppermute | solution.py:348
  54.2 16.2 %collective-permute-start.5 = (bf16[128,128]{1,0:T(8,128)(2,1)S(1)}, bf16[128,128]{1,0:T(8,128)(2,1)S(1)}, u32[]{:S(2)}, u32[]{:S(2)}) collective-permute-start(bf16[128,128]{1,0:T(8,128)(2,1)S(1)} %get-tuple-element.41), channel_id=1, source_target_pairs={{0,128},{128,0},{1,129},{129,1},{2,130},{130,2},{3,131},{131,3},{4... | collective-permute-start | bytes 98312 | tf_op jit(solution)/shard_map/ppermute | solution.py:300
  65.1 16.6 %all-to-all-start.2 = ((bf16[16,152,128]{2,1,0:T(8,128)(2,1)}), bf16[16,152,128]{2,1,0:T(8,128)(2,1)S(1)}, u32[]{:S(2)}, u32[]{:S(2)}) async-start(bf16[16,152,128]{2,1,0:T(8,128)(2,1)} %fusion.5), calls=%async_computation.2 | async-start | bytes 1245184 | tf_op jit(solution)/shard_map/all_to_all | solution.py:340
  115.5 14.0 %all-to-all-start.4 = ((f32[32,14,128]{2,1,0:T(8,128)}), f32[32,14,128]{2,1,0:T(8,128)S(1)}, u32[]{:S(2)}, u32[]{:S(2)}) async-start(f32[32,14,128]{2,1,0:T(8,128)} %broadcast_in_dim.25), calls=%async_computation.4 | async-start | bytes 524288 | tf_op jit(solution)/shard_map/all_to_all | solution.py:28
  131.2 21.5 %all-to-all-start.5 = ((bf16[16,16,384]{2,1,0:T(8,128)(2,1)}), bf16[16,16,384]{2,1,0:T(8,128)(2,1)S(1)}, u32[]{:S(2)}, u32[]{:S(2)}) async-start(bf16[16,16,384]{2,1,0:T(8,128)(2,1)} %broadcast_in_dim.26), calls=%async_computation.5 | async-start | bytes 393216 | tf_op jit(solution)/shard_map/all_to_all | solution.py:28
  136.4 20.3 %collective-permute-start.6 = (bf16[128,128]{0,1:T(8,128)(2,1)S(1)}, bf16[128,128]{0,1:T(8,128)(2,1)S(1)}, u32[]{:S(2)}, u32[]{:S(2)}) collective-permute-start(bf16[128,128]{0,1:T(8,128)(2,1)S(1)} %bitcast.75), channel_id=1, source_target_pairs={{0,128},{128,0},{1,129},{129,1},{2,130},{130,2},{3,131},{131,3},{4... | collective-permute-start | bytes 98312 | tf_op jit(solution)/shard_map/ppermute | solution.py:363
  153.3 9.1 %all-to-all-start.6 = ((f32[4,16,384]{2,1,0:T(8,128)}), f32[4,16,384]{2,1,0:T(8,128)S(1)}, u32[]{:S(2)}, u32[]{:S(2)}) async-start(f32[4,16,384]{2,1,0:T(8,128)} %broadcast_in_dim.27), calls=%async_computation.6 | async-start | bytes 196608 | tf_op jit(solution)/shard_map/all_to_all | solution.py:28

commit v7 on v6

--- a/solution.py
+++ b/solution.py
@@ -302,15 +302,24 @@
     def in_order(mine, other):
         return jnp.where(far == 0, jnp.stack([mine, other]), jnp.stack([other, mine]))
 
+    clip = lax.axis_index("grp")
+    half_rows = rows_each // 2
+
+    def both_halves(mine, given, axis):
+        other = lax.ppermute(given, "grp", [(0, 1), (1, 0)])
+        return jnp.where(
+            clip == 0, jnp.stack([mine, other], axis), jnp.stack([other, mine], axis)
+        )
+
     w = qkv_weight.reshape(depth, 3, 2, 2, HEAD_DIM)
-    w = jnp.transpose(w, (2, 1, 4, 3, 0)).reshape(2 * near_count, rows_each * 2, depth)
-    w_slice = lax.all_to_all(w, SEQ, 0, 0, tiled=True)
-    w_blocks = w_slice
-    w_slice = jnp.transpose(w_slice, (1, 0, 2)).reshape(rows_each * 2, D)
+    w = jnp.transpose(w, (2, 1, 4, 3, 0)).reshape(2 * near_count, 2, rows_each, depth)
+    w = jnp.where(clip == 0, w[:, 0], w[:, 1])
+    w_blocks = lax.all_to_all(w, SEQ, 0, 0, tiled=True)
+    w_slice = jnp.transpose(w_blocks, (1, 0, 2)).reshape(rows_each, D)
     embed32 = embed_weight.astype(F32)
     gained = jnp.concatenate(two(embed32 * norm_gain), axis=0)
     m_slice = mm(w_slice, gained, NT)
-    m_slice = (m_slice[:, :FEAT] + m_slice[:, FEAT:]).reshape(rows_each, 2 * FEAT)
+    m_slice = (m_slice[:, :FEAT] + m_slice[:, FEAT:]).reshape(half_rows, 2 * FEAT)
     columns = lax.axis_index(HEAD) * lax.axis_size(("grp", "seq_0"))
     columns = (columns + lax.axis_index(("grp", "seq_0"))) * depth
     gain_own = lax.dynamic_slice_in_dim(norm_gain, columns, depth, 0)
@@ -330,8 +339,13 @@
     arrived = from_everyone(jnp.concatenate([patch, *two(m_slice)], axis=0), "seq_1")
     far_count, head_count = lax.axis_size("seq_0"), lax.axis_size(HEAD)
     plane = far_count * head_count
-    mine = w_blocks.reshape(head_count, -1, far_count, rows_each * 2, depth)
-    mine = jnp.swapaxes(lax.dynamic_index_in_dim(mine, lax.axis_index("grp"), 1, False), 0, 1)
+    mine = w_blocks.reshape(head_count, -1, far_count, rows_each, depth)
+    mine = both_halves(
+        lax.dynamic_index_in_dim(mine, clip, 1, False),
+        lax.dynamic_index_in_dim(mine, 1 - clip, 1, False),
+        2,
+    )
+    mine = jnp.swapaxes(mine, 0, 1)
     mine = mine.reshape(plane, rows_each * 2, depth)
     mine = jnp.pad(mine, ((0, 0), (0, 0), (0, 2 * FEAT - depth)))
     latents = arrived[:, :own_rows].reshape(1, -1, 2 * FEAT)
@@ -341,8 +355,10 @@
         jnp.concatenate([latents, mine], axis=1), ("seq_0", *HEAD), 0, 0, tiled=True
     )
     w_own = every[:, pairs_each:, :depth].reshape(-1, depth)
-    m_high = arrived[:, own_rows : own_rows + rows_each].reshape(rows, 2 * FEAT)
-    m_low = arrived[:, own_rows + rows_each :].reshape(rows, 2 * FEAT)
+    m_half = arrived[:, own_rows:]
+    m_both = both_halves(m_half, m_half, 1).reshape(near_count, 2, 2, half_rows, 2 * FEAT)
+    m_high = m_both[:, :, 0].reshape(rows, 2 * FEAT)
+    m_low = m_both[:, :, 1].reshape(rows, 2 * FEAT)
 
     per_patch_row = own_rows
     order = in_order(token_order, lax.ppermute(token_order, "seq_0", [(0, 1), (1, 0)]))

time: 164 us -> 175 us (1.067)
  starting transfers between devices: 58 us -> 77.1 us
  waiting for transfers between devices: 57.3 us -> 46.7 us
    all_to_all x1, waiting for transfers between devices: 11.8 us -> 0.01 us  [per_device(): w_blocks = lax.all_to_all(w, SEQ, 0, 0, tiled=True)]
    all_to_all x1, waiting for transfers between devices: 11.1 us -> 0.01 us  [per_device(): lax.all_to_all(jnp.concatenate([latents, mine], axis=1), ('seq_0', *HEAD)...]
    ppermute x0 -> x2, waiting for transfers between devices: none -> 9.91 us  [both_halves(): other = lax.ppermute(given, 'grp', [(0, 1), (1, 0)])]
    ppermute x0 -> x2, starting transfers between devices: none -> 9.28 us  [both_halves(): other = lax.ppermute(given, 'grp', [(0, 1), (1, 0)])]
    all_to_all x4, starting transfers between devices: 18.2 us -> 23.4 us  [from_everyone(): return lax.all_to_all(copies, axis, split_axis=0, concat_axis=0, tiled=True)]
    all_to_all x1, starting transfers between devices: 12.4 us -> 16.3 us  [per_device(): w_blocks = lax.all_to_all(w, SEQ, 0, 0, tiled=True)]
    ppermute x4, waiting for transfers between devices: 0.55 us -> 4.3 us  [shifted(): lax.ppermute(value, axis, [(source, source + steps) for source in range(l...]
    ppermute x4, starting transfers between devices: 14.5 us -> 11.4 us  [shifted(): lax.ppermute(value, axis, [(source, source + steps) for source in range(l...]
  transfers between devices with their start and end apart: 13 -> 15, of which waited for: 7 -> 8; matrix products, arithmetic and copies ran while one was open for 4% -> 4% of each run, Pallas kernels for 0% -> 1%
where the time goes in v7:
time: 175 us; the launch traced here: 174 us
  starting transfers between devices  77.1 us (44%)
  waiting for transfers between devices  46.7 us (27%)
  blocking collectives  20.2 us (12%)
  Pallas kernels  16.2 us (9%)
  local copies, waits for them, and re-layouts  8.27 us (5%)
  other arithmetic  3.46 us (2%)
    all_to_all x4, waiting for transfers between devices, from_everyone(): return lax.all_to_all(copies, axis, split_axis=0, concat_axis=0, tiled=True)  32.5 us
    all_to_all x4, starting transfers between devices, from_everyone(): return lax.all_to_all(copies, axis, split_axis=0, concat_axis=0, tiled=True)  23.4 us
    all_to_all x1, blocking collectives, per_device(): at = jnp.sum(lax.all_to_all(at, 'seq_1', 0, 0, tiled=True), axis=0)  20.2 us
    all_to_all x1, starting transfers between devices, per_device(): w_blocks = lax.all_to_all(w, SEQ, 0, 0, tiled=True)  16.3 us
    pallas_call x1, Pallas kernels, attention(): pl.pallas_call(attention_kernel, grid=(heads,), in_specs=[whole(*x.shape)...  13.9 us
    ppermute x4, starting transfers between devices, shifted(): lax.ppermute(value, axis, [(source, source + steps) for source in range(l...  11.4 us
    ppermute x2, waiting for transfers between devices, both_halves(): other = lax.ppermute(given, 'grp', [(0, 1), (1, 0)])  9.91 us
    ppermute x2, starting transfers between devices, both_halves(): other = lax.ppermute(given, 'grp', [(0, 1), (1, 0)])  9.28 us
  transfers between devices with their start and end apart: 15, of which 8 were waited for; matrix products, arithmetic and copies ran while one was open for 4% of the time, Pallas kernels for 1%

profile of v7, /device:TPU:32, one launch (start us, length us, event | category | flops | bytes accessed | tf_op | source)
XLA Modules:
  0.0 174.2 jit_solution(7437570374351555655)
XLA Ops:
  2.7 16.3 %all-to-all-start = ((bf16[32,12,96]{2,1,0:T(8,128)(2,1)}), bf16[32,12,96]{2,1,0:T(8,128)(2,1)S(1)}, u32[]{:S(2)}, u32[]{:S(2)}) async-start(bf16[32,12,96]{2,1,0:T(8,128)(2,1)} %fusion.15), calls=%async_computation | async-start | bytes 262144 | tf_op jit(solution)/shard_map/all_to_all | solution.py:317
  19.0 2.3 %taps.1 = f32[3,16,128]{2,1,0:T(8,128)} custom-call(bf16[64,512]{1,0:T(8,128)(2,1)} %bitcast.87, bf16[432,512]{1,0:T(8,128)(2,1)} %bitcast.76), custom_call_target="tpu_custom_call" | custom-call | tf_op jit(solution)/shard_map/taps/pallas_call | solution.py:94
  22.0 3.4 %collective-permute-start = (f32[16,128]{1,0:T(8,128)S(1)}, f32[16,128]{1,0:T(8,128)S(1)}, u32[]{:S(2)}, u32[]{:S(2)}) collective-permute-start(f32[16,128]{1,0:T(8,128)S(1)} %get-tuple-element.46), channel_id=1, source_target_pairs={{0,8},{8,16},{16,24},{24,32},{32,40},{40,48},{48,56},{56,64},{64,7... | collective-permute-start | bytes 24584 | tf_op jit(solution)/shard_map/ppermute | solution.py:23
  25.4 5.5 %collective-permute-start.1 = (f32[16,128]{1,0:T(8,128)S(1)}, f32[16,128]{1,0:T(8,128)S(1)}, u32[]{:S(2)}, u32[]{:S(2)}) collective-permute-start(f32[16,128]{1,0:T(8,128)S(1)} %get-tuple-element.47), channel_id=1, source_target_pairs={{0,16},{8,24},{16,32},{24,40},{32,48},{40,56},{48,64},{56,72},{64,... | collective-permute-start | bytes 24584 | tf_op jit(solution)/shard_map/ppermute | solution.py:23
  34.2 1.3 collective-permute-start.3
  35.9 3.1 %collective-permute-done.3 = f32[16,128]{1,0:T(8,128)S(1)} collective-permute-done((f32[16,128]{1,0:T(8,128)S(1)}, f32[16,128]{1,0:T(8,128)S(1)}, u32[]{:S(2)}, u32[]{:S(2)}) %collective-permute-start.3) | collective-permute-done | bytes 8224 | tf_op jit(solution)/shard_map/ppermute | solution.py:23
  39.2 5.2 %collective-permute-start.7 = (bf16[128,128]{1,0:T(8,128)(2,1)S(1)}, bf16[128,128]{1,0:T(8,128)(2,1)S(1)}, u32[]{:S(2)}, u32[]{:S(2)}) collective-permute-start(bf16[128,128]{1,0:T(8,128)(2,1)S(1)} %get-tuple-element.43), channel_id=1, source_target_pairs={{0,128},{128,0},{1,129},{129,1},{2,130},{130,2},{3,131},{131,3},{4... | collective-permute-start | bytes 98312 | tf_op jit(solution)/shard_map/ppermute | solution.py:300
  44.5 1.9 %collective-permute-start.6 = (s32[128]{0:T(128)S(1)}, s32[128]{0:T(128)S(1)}, u32[]{:S(2)}, u32[]{:S(2)}) collective-permute-start(s32[128]{0:T(128)S(1)} %copy-done.4), channel_id=1, source_target_pairs={{0,128},{128,0},{1,129},{129,1},{2,130},{130,2},{3,131},{131,3},{4... | collective-permute-start | bytes 1544 | tf_op jit(solution)/shard_map/ppermute | solution.py:364
  47.8 10.7 %all-to-all-start.1 = ((bf16[16,20,128]{2,1,0:T(8,128)(2,1)}), bf16[16,20,128]{2,1,0:T(8,128)(2,1)S(1)}, u32[]{:S(2)}, u32[]{:S(2)}) async-start(bf16[16,20,128]{2,1,0:T(8,128)(2,1)} %broadcast_in_dim.22), calls=%async_computation.1 | async-start | bytes 196608 | tf_op jit(solution)/shard_map/all_to_all | solution.py:28
  58.6 4.6 %collective-permute-start.4 = (bf16[8,2,12,96]{3,0,2,1:T(8,128)(2,1)S(1)}, bf16[8,2,12,96]{3,0,2,1:T(8,128)(2,1)S(1)}, u32[]{:S(2)}, u32[]{:S(2)}) collective-permute-start(bf16[8,2,12,96]{3,0,2,1:T(8,128)(2,1)S(1)} %bitcast.88), channel_id=1, source_target_pairs={{0,256},{256,0},{1,257},{257,1},{2,258},{258,2},{3,259},{259,3},{4... | collective-permute-start | bytes 110600 | tf_op jit(solution)/shard_map/ppermute | solution.py:309
  63.4 2.9 %collective-permute-done.4 = bf16[8,2,12,96]{3,0,2,1:T(8,128)(2,1)S(1)} collective-permute-done((bf16[8,2,12,96]{3,0,2,1:T(8,128)(2,1)S(1)}, bf16[8,2,12,96]{3,0,2,1:T(8,128)(2,1)S(1)}, u32[]{:S(2)}, u32[]{:S(2)}) %collective-permute-start.4) | collective-permute-done | bytes 36896 | tf_op jit(solution)/shard_map/ppermute | solution.py:309
  66.4 5.1 %all-to-all-done.1 = bf16[16,20,128]{2,1,0:T(8,128)(2,1)S(1)} async-done(((bf16[16,20,128]{2,1,0:T(8,128)(2,1)}), bf16[16,20,128]{2,1,0:T(8,128)(2,1)S(1)}, u32[]{:S(2)}, u32[]{:S(2)}) %all-to-all-start.1) | async-done | bytes 81952 | tf_op jit(solution)/shard_map/all_to_all | solution.py:28
  72.4 7.1 %all-to-all-start.2 = ((bf16[16,152,128]{2,1,0:T(8,128)(2,1)}), bf16[16,152,128]{2,1,0:T(8,128)(2,1)S(1)}, u32[]{:S(2)}, u32[]{:S(2)}) async-start(bf16[16,152,128]{2,1,0:T(8,128)(2,1)} %fusion.6), calls=%async_computation.2 | async-start | bytes 1245184 | tf_op jit(solution)/shard_map/all_to_all | solution.py:354
  80.0 4.6 %collective-permute-start.5 = (bf16[16,12,128]{2,1,0:T(8,128)(2,1)S(1)}, bf16[16,12,128]{2,1,0:T(8,128)(2,1)S(1)}, u32[]{:S(2)}, u32[]{:S(2)}) collective-permute-start(bf16[16,12,128]{2,1,0:T(8,128)(2,1)S(1)} %slice.99), channel_id=1, source_target_pairs={{0,256},{256,0},{1,257},{257,1},{2,258},{258,2},{3,259},{259,3},{4... | collective-permute-start | bytes 147464 | tf_op jit(solution)/shard_map/ppermute | solution.py:309
  84.9 7.0 %collective-permute-done.5 = bf16[16,12,128]{2,1,0:T(8,128)(2,1)S(1)} collective-permute-done((bf16[16,12,128]{2,1,0:T(8,128)(2,1)S(1)}, bf16[16,12,128]{2,1,0:T(8,128)(2,1)S(1)}, u32[]{:S(2)}, u32[]{:S(2)}) %collective-permute-start.5) | collective-permute-done | bytes 49184 | tf_op jit(solution)/shard_map/ppermute | solution.py:309
  92.1 13.9 %attention.1 = (bf16[2,256,64]{2,1,0:T(8,128)(2,1)S(1)}, f32[192,128]{1,0:T(8,128)S(1)}, f32[64,64]{1,0:T(8,128)S(1)}) custom-call(bf16[16,152,128]{2,1,0:T(8,128)(2,1)S(1)} %all-to-all-done.2.x_ref, bf16[192,128]{1,0:T(8,128)(2,1)S(1)} %reshape_squeeze.10.high_ref, bf16[192,128]{1,0:T(8,128)(2,1)S(1)} %reshape_squeeze.11.low_ref, ...), custom_call_target="tpu_custom_call" | custom-call | tf_op jit(solution)/shard_map/attention/pallas_call | solution.py:257
  106.1 20.2 %all_to_all.35 = f32[16,14,128]{2,1,0:T(8,128)S(1)} all-to-all(f32[16,14,128]{2,1,0:T(8,128)S(1)} %pad_maximum_fusion), channel_id=1, replica_groups=mesh['grp'=2,'seq_0'=2,'seq_1'=16,'head_0'=4,'head_1'=2] {'seq_1'}, dimensions={0} | all-to-all | bytes 229376 | tf_op jit(solution)/shard_map/all_to_all | solution.py:395
  127.1 5.0 %all-to-all-start.4 = ((f32[32,14,128]{2,1,0:T(8,128)}), f32[32,14,128]{2,1,0:T(8,128)S(1)}, u32[]{:S(2)}, u32[]{:S(2)}) async-start(f32[32,14,128]{2,1,0:T(8,128)} %broadcast_in_dim.25), calls=%async_computation.4 | async-start | bytes 524288 | tf_op jit(solution)/shard_map/all_to_all | solution.py:28
  132.3 8.7 %all-to-all-done.4 = f32[32,14,128]{2,1,0:T(8,128)S(1)} async-done(((f32[32,14,128]{2,1,0:T(8,128)}), f32[32,14,128]{2,1,0:T(8,128)S(1)}, u32[]{:S(2)}, u32[]{:S(2)}) %all-to-all-start.4) | async-done | bytes 229408 | tf_op jit(solution)/shard_map/all_to_all | solution.py:28
  142.6 4.4 %all-to-all-start.5 = ((bf16[16,16,384]{2,1,0:T(8,128)(2,1)}), bf16[16,16,384]{2,1,0:T(8,128)(2,1)S(1)}, u32[]{:S(2)}, u32[]{:S(2)}) async-start(bf16[16,16,384]{2,1,0:T(8,128)(2,1)} %broadcast_in_dim.26), calls=%async_computation.5 | async-start | bytes 393216 | tf_op jit(solution)/shard_map/all_to_all | solution.py:28
  147.2 2.5 %collective-permute-start.8 = (bf16[128,128]{0,1:T(8,128)(2,1)S(1)}, bf16[128,128]{0,1:T(8,128)(2,1)S(1)}, u32[]{:S(2)}, u32[]{:S(2)}) collective-permute-start(bf16[128,128]{0,1:T(8,128)(2,1)S(1)} %bitcast.90), channel_id=1, source_target_pairs={{0,128},{128,0},{1,129},{129,1},{2,130},{130,2},{3,131},{131,3},{4... | collective-permute-start | bytes 98312 | tf_op jit(solution)/shard_map/ppermute | solution.py:379
  149.8 13.7 %all-to-all-done.5 = bf16[16,16,384]{2,1,0:T(8,128)(2,1)S(1)} async-done(((bf16[16,16,384]{2,1,0:T(8,128)(2,1)}), bf16[16,16,384]{2,1,0:T(8,128)(2,1)S(1)}, u32[]{:S(2)}, u32[]{:S(2)}) %all-to-all-start.5) | async-done | bytes 196640 | tf_op jit(solution)/shard_map/all_to_all | solution.py:28
  164.2 3.3 %all-to-all-start.6 = ((f32[4,16,384]{2,1,0:T(8,128)}), f32[4,16,384]{2,1,0:T(8,128)S(1)}, u32[]{:S(2)}, u32[]{:S(2)}) async-start(f32[4,16,384]{2,1,0:T(8,128)} %broadcast_in_dim.27), calls=%async_computation.6 | async-start | bytes 196608 | tf_op jit(solution)/shard_map/all_to_all | solution.py:28
  168.2 5.0 %all-to-all-done.6 = f32[4,16,384]{2,1,0:T(8,128)S(1)} async-done(((f32[4,16,384]{2,1,0:T(8,128)}), f32[4,16,384]{2,1,0:T(8,128)S(1)}, u32[]{:S(2)}, u32[]{:S(2)}) %all-to-all-start.6) | async-done | bytes 98336 | tf_op jit(solution)/shard_map/all_to_all | solution.py:28
  (97 shorter events, 15.2 us)
Async XLA Ops:
  2.0 28.9 %copy-start = (bf16[64,3072]{1,0:T(8,128)(2,1)S(1)}, bf16[64,3072]{1,0:T(8,128)(2,1)}, u32[]{:S(2)}) copy-start(bf16[64,3072]{1,0:T(8,128)(2,1)} %param.12) | copy-start | bytes 1179652
  2.0 28.9 %copy-start.2 = (f32[3072]{0:T(1024)S(1)}, f32[3072]{0:T(1024)}, u32[]{:S(2)}) copy-start(f32[3072]{0:T(1024)} %param.13) | copy-start | bytes 36868
  2.7 43.7 %all-to-all-start = ((bf16[32,12,96]{2,1,0:T(8,128)(2,1)}), bf16[32,12,96]{2,1,0:T(8,128)(2,1)S(1)}, u32[]{:S(2)}, u32[]{:S(2)}) async-start(bf16[32,12,96]{2,1,0:T(8,128)(2,1)} %fusion.15), calls=%async_computation | async-start | bytes 262144 | tf_op jit(solution)/shard_map/all_to_all | solution.py:317
  22.0 9.0 %collective-permute-start = (f32[16,128]{1,0:T(8,128)S(1)}, f32[16,128]{1,0:T(8,128)S(1)}, u32[]{:S(2)}, u32[]{:S(2)}) collective-permute-start(f32[16,128]{1,0:T(8,128)S(1)} %get-tuple-element.46), channel_id=1, source_target_pairs={{0,8},{8,16},{16,24},{24,32},{32,40},{40,48},{48,56},{56,64},{64,7... | collective-permute-start | bytes 24584 | tf_op jit(solution)/shard_map/ppermute | solution.py:23
  25.4 6.8 %collective-permute-start.1 = (f32[16,128]{1,0:T(8,128)S(1)}, f32[16,128]{1,0:T(8,128)S(1)}, u32[]{:S(2)}, u32[]{:S(2)}) collective-permute-start(f32[16,128]{1,0:T(8,128)S(1)} %get-tuple-element.47), channel_id=1, source_target_pairs={{0,16},{8,24},{16,32},{24,40},{32,48},{40,56},{48,64},{56,72},{64,... | collective-permute-start | bytes 24584 | tf_op jit(solution)/shard_map/ppermute | solution.py:23
  31.0 4.7 %copy-start.3 = (f32[16]{0:T(128)S(1)}, f32[16]{0:T(128)}, u32[]{:S(2)}) copy-start(f32[16]{0:T(128)} %param.10) | copy-start | bytes 196
  31.0 8.2 %copy-start.1 = (bf16[1,128,256]{2,1,0:T(8,128)(2,1)S(1)}, bf16[1,128,256]{2,1,0:T(8,128)(2,1)}, u32[]{:S(2)}) copy-start(bf16[1,128,256]{2,1,0:T(8,128)(2,1)} %param.15) | copy-start | bytes 196612
  31.0 13.4 %copy-start.4 = (s32[128]{0:T(128)S(1)}, s32[128]{0:T(128)}, u32[]{:S(2)}) copy-start(s32[128]{0:T(128)} %param.11) | copy-start | bytes 1540
  32.9 2.9 %collective-permute-start.2 = (f32[16,128]{1,0:T(8,128)S(1)}, f32[16,128]{1,0:T(8,128)S(1)}, u32[]{:S(2)}, u32[]{:S(2)}) collective-permute-start(f32[16,128]{1,0:T(8,128)S(1)} %fusion.33), channel_id=1, source_target_pairs={{0,1},{1,2},{2,3},{3,4},{4,5},{5,6},{6,7},{8,9},{9,10},{10,11},{11... | collective-permute-start | bytes 24584 | tf_op jit(solution)/shard_map/ppermute | solution.py:23
  34.2 4.9 %collective-permute-start.3 = (f32[16,128]{1,0:T(8,128)S(1)}, f32[16,128]{1,0:T(8,128)S(1)}, u32[]{:S(2)}, u32[]{:S(2)}) collective-permute-start(f32[16,128]{1,0:T(8,128)S(1)} %fusion.33), channel_id=1, source_target_pairs={{1,0},{2,1},{3,2},{4,3},{5,4},{6,5},{7,6},{9,8},{10,9},{11,10},{12... | collective-permute-start | bytes 24584 | tf_op jit(solution)/shard_map/ppermute | solution.py:23
  39.2 45.4 %collective-permute-start.7 = (bf16[128,128]{1,0:T(8,128)(2,1)S(1)}, bf16[128,128]{1,0:T(8,128)(2,1)S(1)}, u32[]{:S(2)}, u32[]{:S(2)}) collective-permute-start(bf16[128,128]{1,0:T(8,128)(2,1)S(1)} %get-tuple-element.43), channel_id=1, source_target_pairs={{0,128},{128,0},{1,129},{129,1},{2,130},{130,2},{3,131},{131,3},{4... | collective-permute-start | bytes 98312 | tf_op jit(solution)/shard_map/ppermute | solution.py:300
  44.5 18.8 %collective-permute-start.6 = (s32[128]{0:T(128)S(1)}, s32[128]{0:T(128)S(1)}, u32[]{:S(2)}, u32[]{:S(2)}) collective-permute-start(s32[128]{0:T(128)S(1)} %copy-done.4), channel_id=1, source_target_pairs={{0,128},{128,0},{1,129},{129,1},{2,130},{130,2},{3,131},{131,3},{4... | collective-permute-start | bytes 1544 | tf_op jit(solution)/shard_map/ppermute | solution.py:364
  47.8 23.7 %all-to-all-start.1 = ((bf16[16,20,128]{2,1,0:T(8,128)(2,1)}), bf16[16,20,128]{2,1,0:T(8,128)(2,1)S(1)}, u32[]{:S(2)}, u32[]{:S(2)}) async-start(bf16[16,20,128]{2,1,0:T(8,128)(2,1)} %broadcast_in_dim.22), calls=%async_computation.1 | async-start | bytes 196608 | tf_op jit(solution)/shard_map/all_to_all | solution.py:28
  58.6 7.7 %collective-permute-start.4 = (bf16[8,2,12,96]{3,0,2,1:T(8,128)(2,1)S(1)}, bf16[8,2,12,96]{3,0,2,1:T(8,128)(2,1)S(1)}, u32[]{:S(2)}, u32[]{:S(2)}) collective-permute-start(bf16[8,2,12,96]{3,0,2,1:T(8,128)(2,1)S(1)} %bitcast.88), channel_id=1, source_target_pairs={{0,256},{256,0},{1,257},{257,1},{2,258},{258,2},{3,259},{259,3},{4... | collective-permute-start | bytes 110600 | tf_op jit(solution)/shard_map/ppermute | solution.py:309
  72.4 19.6 %all-to-all-start.2 = ((bf16[16,152,128]{2,1,0:T(8,128)(2,1)}), bf16[16,152,128]{2,1,0:T(8,128)(2,1)S(1)}, u32[]{:S(2)}, u32[]{:S(2)}) async-start(bf16[16,152,128]{2,1,0:T(8,128)(2,1)} %fusion.6), calls=%async_computation.2 | async-start | bytes 1245184 | tf_op jit(solution)/shard_map/all_to_all | solution.py:354
  80.0 11.9 %collective-permute-start.5 = (bf16[16,12,128]{2,1,0:T(8,128)(2,1)S(1)}, bf16[16,12,128]{2,1,0:T(8,128)(2,1)S(1)}, u32[]{:S(2)}, u32[]{:S(2)}) collective-permute-start(bf16[16,12,128]{2,1,0:T(8,128)(2,1)S(1)} %slice.99), channel_id=1, source_target_pairs={{0,256},{256,0},{1,257},{257,1},{2,258},{258,2},{3,259},{259,3},{4... | collective-permute-start | bytes 147464 | tf_op jit(solution)/shard_map/ppermute | solution.py:309
  127.1 13.9 %all-to-all-start.4 = ((f32[32,14,128]{2,1,0:T(8,128)}), f32[32,14,128]{2,1,0:T(8,128)S(1)}, u32[]{:S(2)}, u32[]{:S(2)}) async-start(f32[32,14,128]{2,1,0:T(8,128)} %broadcast_in_dim.25), calls=%async_computation.4 | async-start | bytes 524288 | tf_op jit(solution)/shard_map/all_to_all | solution.py:28
  142.6 20.8 %all-to-all-start.5 = ((bf16[16,16,384]{2,1,0:T(8,128)(2,1)}), bf16[16,16,384]{2,1,0:T(8,128)(2,1)S(1)}, u32[]{:S(2)}, u32[]{:S(2)}) async-start(bf16[16,16,384]{2,1,0:T(8,128)(2,1)} %broadcast_in_dim.26), calls=%async_computation.5 | async-start | bytes 393216 | tf_op jit(solution)/shard_map/all_to_all | solution.py:28
  147.2 20.3 %collective-permute-start.8 = (bf16[128,128]{0,1:T(8,128)(2,1)S(1)}, bf16[128,128]{0,1:T(8,128)(2,1)S(1)}, u32[]{:S(2)}, u32[]{:S(2)}) collective-permute-start(bf16[128,128]{0,1:T(8,128)(2,1)S(1)} %bitcast.90), channel_id=1, source_target_pairs={{0,128},{128,0},{1,129},{129,1},{2,130},{130,2},{3,131},{131,3},{4... | collective-permute-start | bytes 98312 | tf_op jit(solution)/shard_map/ppermute | solution.py:379
  164.2 9.1 %all-to-all-start.6 = ((f32[4,16,384]{2,1,0:T(8,128)}), f32[4,16,384]{2,1,0:T(8,128)S(1)}, u32[]{:S(2)}, u32[]{:S(2)}) async-start(f32[4,16,384]{2,1,0:T(8,128)} %broadcast_in_dim.27), calls=%async_computation.6 | async-start | bytes 196608 | tf_op jit(solution)/shard_map/all_to_all | solution.py:28

commit v8 on v7

--- a/solution.py
+++ b/solution.py
@@ -87,7 +87,7 @@
         out_ref[a] = sums[a]
 
 
-def encode_tile(tile, conv_weight, conv_bias):
+def taps(tile, conv_weight):
     rows, columns, channels = tile.shape
     lat = conv_weight.shape[-1]
     weight = jnp.moveaxis(conv_weight, 4, 3).reshape(27 * lat, channels)
@@ -96,6 +96,11 @@
         out_shape=jax.ShapeDtypeStruct((3, columns // 2, 8 * lat), F32),
         name="taps",
     )(tile.reshape(rows * columns, channels), weight)
+    return parts
+
+
+def latent_patches(parts, conv_bias):
+    lat = conv_bias.shape[0]
     total = (parts[2] + shifted(parts[1], SEQ, 1)) + shifted(parts[0], SEQ, 2)
     above, below = shifted(total, HEAD, 1), shifted(total, HEAD, -1)
     own = total[:, 2 * lat : 6 * lat]
@@ -314,6 +319,8 @@
     w = qkv_weight.reshape(depth, 3, 2, 2, HEAD_DIM)
     w = jnp.transpose(w, (2, 1, 4, 3, 0)).reshape(2 * near_count, 2, rows_each, depth)
     w = jnp.where(clip == 0, w[:, 0], w[:, 1])
+    parts = taps(features[0, 0], conv_weight)
+    parts, w = lax.optimization_barrier((parts, w))
     w_blocks = lax.all_to_all(w, SEQ, 0, 0, tiled=True)
     w_slice = jnp.transpose(w_blocks, (1, 0, 2)).reshape(rows_each, D)
     embed32 = embed_weight.astype(F32)
@@ -329,24 +336,20 @@
     embed_own = jnp.concatenate(
         [lax.dynamic_slice_in_dim(embed_own, b_at + k, b_each, 0) for k in (0, FEAT // 2)], axis=0
     )
+
+    patch = latent_patches(parts, conv_bias)
+    token_order, m_slice, patch, embed_late = lax.optimization_barrier(
+        (token_order, m_slice, patch, embed_weight)
+    )
     gram = lax.dot_general(
-        embed_weight, embed_weight, (((1,), (1,)), ((), ())), preferred_element_type=F32
+        embed_late, embed_late, (((1,), (1,)), ((), ())), preferred_element_type=F32
     ) * (1.0 / D)
-
-    patch = encode_tile(features[0, 0], conv_weight, conv_bias)
-    token_order, grad_out, patch = lax.optimization_barrier((token_order, grad_out, patch))
     own_rows = patch.shape[0]
     arrived = from_everyone(jnp.concatenate([patch, *two(m_slice)], axis=0), "seq_1")
     far_count, head_count = lax.axis_size("seq_0"), lax.axis_size(HEAD)
     plane = far_count * head_count
     mine = w_blocks.reshape(head_count, -1, far_count, rows_each, depth)
-    mine = both_halves(
-        lax.dynamic_index_in_dim(mine, clip, 1, False),
-        lax.dynamic_index_in_dim(mine, 1 - clip, 1, False),
-        2,
-    )
-    mine = jnp.swapaxes(mine, 0, 1)
-    mine = mine.reshape(plane, rows_each * 2, depth)
+    mine = jnp.transpose(mine, (2, 0, 1, 3, 4)).reshape(plane, rows_each * 2, depth)
     mine = jnp.pad(mine, ((0, 0), (0, 0), (0, 2 * FEAT - depth)))
     latents = arrived[:, :own_rows].reshape(1, -1, 2 * FEAT)
     pairs_each = latents.shape[1]
@@ -354,8 +357,8 @@
     every = lax.all_to_all(
         jnp.concatenate([latents, mine], axis=1), ("seq_0", *HEAD), 0, 0, tiled=True
     )
-    w_own = every[:, pairs_each:, :depth].reshape(-1, depth)
     m_half = arrived[:, own_rows:]
+    grad_out, m_half = lax.optimization_barrier((grad_out, m_half))
     m_both = both_halves(m_half, m_half, 1).reshape(near_count, 2, 2, half_rows, 2 * FEAT)
     m_high = m_both[:, :, 0].reshape(rows, 2 * FEAT)
     m_low = m_both[:, :, 1].reshape(rows, 2 * FEAT)
@@ -383,6 +386,14 @@
         jnp.concatenate([other, mine], axis=1),
     )[None]
 
+    w_own, at = lax.optimization_barrier((every, at))
+    w_own = w_own[:, pairs_each:].reshape(plane, 2, rows_each, 2 * FEAT)
+    w_own = both_halves(
+        lax.dynamic_index_in_dim(w_own, clip, 1, False),
+        lax.dynamic_index_in_dim(w_own, 1 - clip, 1, False),
+        1,
+    )
+    w_own = w_own.reshape(-1, 2 * FEAT)[:, :depth]
     first, second = jnp.split(b, 2, axis=0)
     b = jnp.concatenate([first, second], axis=1)
     at = jnp.concatenate(

time: 175 us -> 165 us (0.943)
  blocking collectives: 20.2 us -> 0 us
  waiting for transfers between devices: 46.7 us -> 61.3 us
  starting transfers between devices: 77.1 us -> 72.1 us
    all_to_all x1 -> x0, blocking collectives: 20.2 us -> none  [per_device(): at = jnp.sum(lax.all_to_all(at, 'seq_1', 0, 0, tiled=True), axis=0)]
    all_to_all x0 -> x1, waiting for transfers between devices: none -> 10.6 us  [per_device(): at = jnp.sum(lax.all_to_all(at, 'seq_1', 0, 0, tiled=True), axis=0)]
    all_to_all x1, waiting for transfers between devices: 0.01 us -> 9.2 us  [per_device(): w_blocks = lax.all_to_all(w, SEQ, 0, 0, tiled=True)]
    ppermute x2, waiting for transfers between devices: 9.91 us -> 1.94 us  [both_halves(): other = lax.ppermute(given, 'grp', [(0, 1), (1, 0)])]
    all_to_all x4, starting transfers between devices: 23.4 us -> 17.2 us  [from_everyone(): return lax.all_to_all(copies, axis, split_axis=0, concat_axis=0, tiled=True)]
    all_to_all x0 -> x1, starting transfers between devices: none -> 5.65 us  [per_device(): at = jnp.sum(lax.all_to_all(at, 'seq_1', 0, 0, tiled=True), axis=0)]
    all_to_all x1, starting transfers between devices: 16.3 us -> 12.4 us  [per_device(): w_blocks = lax.all_to_all(w, SEQ, 0, 0, tiled=True)]
    ppermute x4, waiting for transfers between devices: 4.3 us -> 0.55 us  [shifted(): lax.ppermute(value, axis, [(source, source + steps) for source in range(l...]
  transfers between devices with their start and end apart: 15 -> 16, of which waited for: 8 -> 10; matrix products, arithmetic and copies ran while one was open for 4% -> 3% of each run, Pallas kernels for 1% -> 0%
where the time goes in v8:
time: 165 us; the launch traced here: 164 us
  starting transfers between devices  72.1 us (44%)
  waiting for transfers between devices  61.3 us (37%)
  Pallas kernels  16.2 us (10%)
  local copies, waits for them, and re-layouts  8.29 us (5%)
  other arithmetic  4.07 us (2%)
    all_to_all x4, waiting for transfers between devices, from_everyone(): return lax.all_to_all(copies, axis, split_axis=0, concat_axis=0, tiled=True)  34.4 us
    all_to_all x4, starting transfers between devices, from_everyone(): return lax.all_to_all(copies, axis, split_axis=0, concat_axis=0, tiled=True)  17.2 us
    ppermute x4, starting transfers between devices, shifted(): lax.ppermute(value, axis, [(source, source + steps) for source in range(l...  14.5 us
    pallas_call x1, Pallas kernels, attention(): pl.pallas_call(attention_kernel, grid=(heads,), in_specs=[whole(*x.shape)...  13.9 us
    all_to_all x1, starting transfers between devices, per_device(): w_blocks = lax.all_to_all(w, SEQ, 0, 0, tiled=True)  12.4 us
    all_to_all x1, waiting for transfers between devices, per_device(): at = jnp.sum(lax.all_to_all(at, 'seq_1', 0, 0, tiled=True), axis=0)  10.6 us
    all_to_all x1, waiting for transfers between devices, per_device(): w_blocks = lax.all_to_all(w, SEQ, 0, 0, tiled=True)  9.2 us
    ppermute x2, starting transfers between devices, both_halves(): other = lax.ppermute(given, 'grp', [(0, 1), (1, 0)])  8.46 us
  transfers between devices with their start and end apart: 16, of which 10 were waited for; matrix products, arithmetic and copies ran while one was open for 3% of the time, Pallas kernels for 0%

profile of v8, /device:TPU:32, one launch (start us, length us, event | category | flops | bytes accessed | tf_op | source)
XLA Modules:
  0.0 164.2 jit_solution(9878460992700667909)
XLA Ops:
  2.0 2.4 %taps.1 = f32[3,16,128]{2,1,0:T(8,128)} custom-call(bf16[64,512]{1,0:T(8,128)(2,1)} %bitcast.79, bf16[432,512]{1,0:T(8,128)(2,1)} %bitcast.69), custom_call_target="tpu_custom_call" | custom-call | tf_op jit(solution)/shard_map/taps/pallas_call | solution.py:94
  5.8 5.2 %collective-permute-start.1 = (f32[16,128]{1,0:T(8,128)S(1)}, f32[16,128]{1,0:T(8,128)S(1)}, u32[]{:S(2)}, u32[]{:S(2)}) collective-permute-start(f32[16,128]{1,0:T(8,128)S(1)} %get-tuple-element.61), channel_id=1, source_target_pairs={{0,16},{8,24},{16,32},{24,40},{32,48},{40,56},{48,64},{56,72},{64,... | collective-permute-start | bytes 24584 | tf_op jit(solution)/shard_map/ppermute | solution.py:23
  10.9 5.0 %collective-permute-start = (f32[16,128]{1,0:T(8,128)S(1)}, f32[16,128]{1,0:T(8,128)S(1)}, u32[]{:S(2)}, u32[]{:S(2)}) collective-permute-start(f32[16,128]{1,0:T(8,128)S(1)} %get-tuple-element.60), channel_id=1, source_target_pairs={{0,8},{8,16},{16,24},{24,32},{32,40},{40,48},{48,56},{56,64},{64,7... | collective-permute-start | bytes 24584 | tf_op jit(solution)/shard_map/ppermute | solution.py:23
  16.0 12.4 %all-to-all-start = ((bf16[32,12,96]{2,1,0:T(8,128)(2,1)}), bf16[32,12,96]{2,1,0:T(8,128)(2,1)S(1)}, u32[]{:S(2)}, u32[]{:S(2)}) async-start(bf16[32,12,96]{2,1,0:T(8,128)(2,1)} %fusion.15), calls=%async_computation | async-start | bytes 262144 | tf_op jit(solution)/shard_map/all_to_all | solution.py:324
  30.4 3.0 %collective-permute-start.2 = (f32[16,128]{1,0:T(8,128)S(1)}, f32[16,128]{1,0:T(8,128)S(1)}, u32[]{:S(2)}, u32[]{:S(2)}) collective-permute-start(f32[16,128]{1,0:T(8,128)S(1)} %fusion.32), channel_id=1, source_target_pairs={{0,1},{1,2},{2,3},{3,4},{4,5},{5,6},{6,7},{8,9},{9,10},{10,11},{11... | collective-permute-start | bytes 24584 | tf_op jit(solution)/shard_map/ppermute | solution.py:23
  34.5 9.2 %all-to-all-done = bf16[32,12,96]{2,1,0:T(8,128)(2,1)S(1)} async-done(((bf16[32,12,96]{2,1,0:T(8,128)(2,1)}), bf16[32,12,96]{2,1,0:T(8,128)(2,1)S(1)}, u32[]{:S(2)}, u32[]{:S(2)}) %all-to-all-start) | async-done | bytes 73760 | tf_op jit(solution)/shard_map/all_to_all | solution.py:324
  45.0 4.5 %all-to-all-start.1 = ((bf16[16,20,128]{2,1,0:T(8,128)(2,1)}), bf16[16,20,128]{2,1,0:T(8,128)(2,1)S(1)}, u32[]{:S(2)}, u32[]{:S(2)}) async-start(bf16[16,20,128]{2,1,0:T(8,128)(2,1)} %broadcast_in_dim.22), calls=%async_computation.1 | async-start | bytes 196608 | tf_op jit(solution)/shard_map/all_to_all | solution.py:28
  49.5 2.4 %collective-permute-start.5 = (s32[128]{0:T(128)S(1)}, s32[128]{0:T(128)S(1)}, u32[]{:S(2)}, u32[]{:S(2)}) collective-permute-start(s32[128]{0:T(128)S(1)} %copy-done.4), channel_id=1, source_target_pairs={{0,128},{128,0},{1,129},{129,1},{2,130},{130,2},{3,131},{131,3},{4... | collective-permute-start | bytes 1544 | tf_op jit(solution)/shard_map/ppermute | solution.py:367
  52.3 2.6 %collective-permute-done.5 = s32[128]{0:T(128)S(1)} collective-permute-done((s32[128]{0:T(128)S(1)}, s32[128]{0:T(128)S(1)}, u32[]{:S(2)}, u32[]{:S(2)}) %collective-permute-start.5) | collective-permute-done | bytes 544 | tf_op jit(solution)/shard_map/ppermute | solution.py:367
  55.1 7.0 %all-to-all-done.1 = bf16[16,20,128]{2,1,0:T(8,128)(2,1)S(1)} async-done(((bf16[16,20,128]{2,1,0:T(8,128)(2,1)}), bf16[16,20,128]{2,1,0:T(8,128)(2,1)S(1)}, u32[]{:S(2)}, u32[]{:S(2)}) %all-to-all-start.1) | async-done | bytes 81952 | tf_op jit(solution)/shard_map/all_to_all | solution.py:28
  63.1 5.2 %all-to-all-start.2 = ((bf16[16,152,128]{2,1,0:T(8,128)(2,1)}), bf16[16,152,128]{2,1,0:T(8,128)(2,1)S(1)}, u32[]{:S(2)}, u32[]{:S(2)}) async-start(bf16[16,152,128]{2,1,0:T(8,128)(2,1)} %fusion.6), calls=%async_computation.2 | async-start | bytes 1245184 | tf_op jit(solution)/shard_map/all_to_all | solution.py:357
  68.3 3.8 %collective-permute-start.6 = (bf16[128,128]{1,0:T(8,128)(2,1)S(1)}, bf16[128,128]{1,0:T(8,128)(2,1)S(1)}, u32[]{:S(2)}, u32[]{:S(2)}) collective-permute-start(bf16[128,128]{1,0:T(8,128)(2,1)S(1)} %get-tuple-element.57), channel_id=1, source_target_pairs={{0,128},{128,0},{1,129},{129,1},{2,130},{130,2},{3,131},{131,3},{4... | collective-permute-start | bytes 98312 | tf_op jit(solution)/shard_map/ppermute | solution.py:305
  72.6 4.6 %collective-permute-start.4 = (bf16[16,12,128]{2,1,0:T(8,128)(2,1)S(1)}, bf16[16,12,128]{2,1,0:T(8,128)(2,1)S(1)}, u32[]{:S(2)}, u32[]{:S(2)}) collective-permute-start(bf16[16,12,128]{2,1,0:T(8,128)(2,1)S(1)} %slice.100), channel_id=1, source_target_pairs={{0,256},{256,0},{1,257},{257,1},{2,258},{258,2},{3,259},{259,3},{4... | collective-permute-start | bytes 147464 | tf_op jit(solution)/shard_map/ppermute | solution.py:314
  81.5 13.9 %attention.1 = (bf16[2,256,64]{2,1,0:T(8,128)(2,1)S(1)}, f32[192,128]{1,0:T(8,128)S(1)}, f32[64,64]{1,0:T(8,128)S(1)}) custom-call(bf16[16,152,128]{2,1,0:T(8,128)(2,1)S(1)} %all-to-all-done.2.x_ref, bf16[192,128]{1,0:T(8,128)(2,1)S(1)} %reshape_squeeze.10.high_ref, bf16[192,128]{1,0:T(8,128)(2,1)S(1)} %reshape_squeeze.11.low_ref, ...), custom_call_target="tpu_custom_call" | custom-call | tf_op jit(solution)/shard_map/attention/pallas_call | solution.py:262
  96.2 5.7 %all-to-all-start.3 = ((f32[16,14,128]{2,1,0:T(8,128)}), f32[16,14,128]{2,1,0:T(8,128)S(1)}, u32[]{:S(2)}, u32[]{:S(2)}) async-start(f32[16,14,128]{2,1,0:T(8,128)} %pad_maximum_fusion), calls=%async_computation.3 | async-start | bytes 262144 | tf_op jit(solution)/shard_map/all_to_all | solution.py:406
  101.9 3.8 %collective-permute-start.8 = (bf16[16,12,128]{2,0,1:T(8,128)(2,1)S(1)}, bf16[16,12,128]{2,0,1:T(8,128)(2,1)S(1)}, u32[]{:S(2)}, u32[]{:S(2)}) collective-permute-start(bf16[16,12,128]{2,0,1:T(8,128)(2,1)S(1)} %get-tuple-element.53), channel_id=1, source_target_pairs={{0,256},{256,0},{1,257},{257,1},{2,258},{258,2},{3,259},{259,3},{4... | collective-permute-start | bytes 147464 | tf_op jit(solution)/shard_map/ppermute | solution.py:314
  105.7 10.6 %all-to-all-done.3 = f32[16,14,128]{2,1,0:T(8,128)S(1)} async-done(((f32[16,14,128]{2,1,0:T(8,128)}), f32[16,14,128]{2,1,0:T(8,128)S(1)}, u32[]{:S(2)}, u32[]{:S(2)}) %all-to-all-start.3) | async-done | bytes 114720 | tf_op jit(solution)/shard_map/all_to_all | solution.py:406
  117.1 5.0 %all-to-all-start.4 = ((f32[32,14,128]{2,1,0:T(8,128)}), f32[32,14,128]{2,1,0:T(8,128)S(1)}, u32[]{:S(2)}, u32[]{:S(2)}) async-start(f32[32,14,128]{2,1,0:T(8,128)} %broadcast_in_dim.25), calls=%async_computation.4 | async-start | bytes 524288 | tf_op jit(solution)/shard_map/all_to_all | solution.py:28
  122.4 8.7 %all-to-all-done.4 = f32[32,14,128]{2,1,0:T(8,128)S(1)} async-done(((f32[32,14,128]{2,1,0:T(8,128)}), f32[32,14,128]{2,1,0:T(8,128)S(1)}, u32[]{:S(2)}, u32[]{:S(2)}) %all-to-all-start.4) | async-done | bytes 229408 | tf_op jit(solution)/shard_map/all_to_all | solution.py:28
  132.6 4.4 %all-to-all-start.5 = ((bf16[16,16,384]{2,1,0:T(8,128)(2,1)}), bf16[16,16,384]{2,1,0:T(8,128)(2,1)S(1)}, u32[]{:S(2)}, u32[]{:S(2)}) async-start(bf16[16,16,384]{2,1,0:T(8,128)(2,1)} %broadcast_in_dim.26), calls=%async_computation.5 | async-start | bytes 393216 | tf_op jit(solution)/shard_map/all_to_all | solution.py:28
  137.2 2.5 %collective-permute-start.7 = (bf16[128,128]{0,1:T(8,128)(2,1)S(1)}, bf16[128,128]{0,1:T(8,128)(2,1)S(1)}, u32[]{:S(2)}, u32[]{:S(2)}) collective-permute-start(bf16[128,128]{0,1:T(8,128)(2,1)S(1)} %bitcast.81), channel_id=1, source_target_pairs={{0,128},{128,0},{1,129},{129,1},{2,130},{130,2},{3,131},{131,3},{4... | collective-permute-start | bytes 98312 | tf_op jit(solution)/shard_map/ppermute | solution.py:382
  139.8 13.7 %all-to-all-done.5 = bf16[16,16,384]{2,1,0:T(8,128)(2,1)S(1)} async-done(((bf16[16,16,384]{2,1,0:T(8,128)(2,1)}), bf16[16,16,384]{2,1,0:T(8,128)(2,1)S(1)}, u32[]{:S(2)}, u32[]{:S(2)}) %all-to-all-start.5) | async-done | bytes 196640 | tf_op jit(solution)/shard_map/all_to_all | solution.py:28
  154.2 3.3 %all-to-all-start.6 = ((f32[4,16,384]{2,1,0:T(8,128)}), f32[4,16,384]{2,1,0:T(8,128)S(1)}, u32[]{:S(2)}, u32[]{:S(2)}) async-start(f32[4,16,384]{2,1,0:T(8,128)} %broadcast_in_dim.27), calls=%async_computation.6 | async-start | bytes 196608 | tf_op jit(solution)/shard_map/all_to_all | solution.py:28
  158.3 5.0 %all-to-all-done.6 = f32[4,16,384]{2,1,0:T(8,128)S(1)} async-done(((f32[4,16,384]{2,1,0:T(8,128)}), f32[4,16,384]{2,1,0:T(8,128)S(1)}, u32[]{:S(2)}, u32[]{:S(2)}) %all-to-all-start.6) | async-done | bytes 98336 | tf_op jit(solution)/shard_map/all_to_all | solution.py:28
  (99 shorter events, 19.2 us)
Async XLA Ops:
  2.0 31.4 %copy-start = (bf16[64,3072]{1,0:T(8,128)(2,1)S(1)}, bf16[64,3072]{1,0:T(8,128)(2,1)}, u32[]{:S(2)}) copy-start(bf16[64,3072]{1,0:T(8,128)(2,1)} %param.12) | copy-start | bytes 1179652
  2.0 31.4 %copy-start.2 = (f32[3072]{0:T(1024)S(1)}, f32[3072]{0:T(1024)}, u32[]{:S(2)}) copy-start(f32[3072]{0:T(1024)} %param.13) | copy-start | bytes 36868
  5.8 22.6 %collective-permute-start.1 = (f32[16,128]{1,0:T(8,128)S(1)}, f32[16,128]{1,0:T(8,128)S(1)}, u32[]{:S(2)}, u32[]{:S(2)}) collective-permute-start(f32[16,128]{1,0:T(8,128)S(1)} %get-tuple-element.61), channel_id=1, source_target_pairs={{0,16},{8,24},{16,32},{24,40},{32,48},{40,56},{48,64},{56,72},{64,... | collective-permute-start | bytes 24584 | tf_op jit(solution)/shard_map/ppermute | solution.py:23
  10.9 17.5 %collective-permute-start = (f32[16,128]{1,0:T(8,128)S(1)}, f32[16,128]{1,0:T(8,128)S(1)}, u32[]{:S(2)}, u32[]{:S(2)}) collective-permute-start(f32[16,128]{1,0:T(8,128)S(1)} %get-tuple-element.60), channel_id=1, source_target_pairs={{0,8},{8,16},{16,24},{24,32},{32,40},{40,48},{48,56},{56,64},{64,7... | collective-permute-start | bytes 24584 | tf_op jit(solution)/shard_map/ppermute | solution.py:23
  16.0 27.7 %all-to-all-start = ((bf16[32,12,96]{2,1,0:T(8,128)(2,1)}), bf16[32,12,96]{2,1,0:T(8,128)(2,1)S(1)}, u32[]{:S(2)}, u32[]{:S(2)}) async-start(bf16[32,12,96]{2,1,0:T(8,128)(2,1)} %fusion.15), calls=%async_computation | async-start | bytes 262144 | tf_op jit(solution)/shard_map/all_to_all | solution.py:324
  28.4 5.2 %copy-start.3 = (f32[16]{0:T(128)S(1)}, f32[16]{0:T(128)}, u32[]{:S(2)}) copy-start(f32[16]{0:T(128)} %param.10) | copy-start | bytes 196
  29.1 5.2 %collective-permute-start.3 = (f32[16,128]{1,0:T(8,128)S(1)}, f32[16,128]{1,0:T(8,128)S(1)}, u32[]{:S(2)}, u32[]{:S(2)}) collective-permute-start(f32[16,128]{1,0:T(8,128)S(1)} %fusion.32), channel_id=1, source_target_pairs={{1,0},{2,1},{3,2},{4,3},{5,4},{6,5},{7,6},{9,8},{10,9},{11,10},{12... | collective-permute-start | bytes 24584 | tf_op jit(solution)/shard_map/ppermute | solution.py:23
  30.4 3.8 %collective-permute-start.2 = (f32[16,128]{1,0:T(8,128)S(1)}, f32[16,128]{1,0:T(8,128)S(1)}, u32[]{:S(2)}, u32[]{:S(2)}) collective-permute-start(f32[16,128]{1,0:T(8,128)S(1)} %fusion.32), channel_id=1, source_target_pairs={{0,1},{1,2},{2,3},{3,4},{4,5},{5,6},{6,7},{8,9},{9,10},{10,11},{11... | collective-permute-start | bytes 24584 | tf_op jit(solution)/shard_map/ppermute | solution.py:23
  43.9 5.6 %copy-start.4 = (s32[128]{0:T(128)S(1)}, s32[128]{0:T(128)}, u32[]{:S(2)}) copy-start(s32[128]{0:T(128)} %param.11) | copy-start | bytes 1540
  45.0 17.1 %all-to-all-start.1 = ((bf16[16,20,128]{2,1,0:T(8,128)(2,1)}), bf16[16,20,128]{2,1,0:T(8,128)(2,1)S(1)}, u32[]{:S(2)}, u32[]{:S(2)}) async-start(bf16[16,20,128]{2,1,0:T(8,128)(2,1)} %broadcast_in_dim.22), calls=%async_computation.1 | async-start | bytes 196608 | tf_op jit(solution)/shard_map/all_to_all | solution.py:28
  49.5 5.4 %collective-permute-start.5 = (s32[128]{0:T(128)S(1)}, s32[128]{0:T(128)S(1)}, u32[]{:S(2)}, u32[]{:S(2)}) collective-permute-start(s32[128]{0:T(128)S(1)} %copy-done.4), channel_id=1, source_target_pairs={{0,128},{128,0},{1,129},{129,1},{2,130},{130,2},{3,131},{131,3},{4... | collective-permute-start | bytes 1544 | tf_op jit(solution)/shard_map/ppermute | solution.py:367
  63.1 5.2 %copy-start.1 = (bf16[1,128,256]{2,1,0:T(8,128)(2,1)S(1)}, bf16[1,128,256]{2,1,0:T(8,128)(2,1)}, u32[]{:S(2)}) copy-start(bf16[1,128,256]{2,1,0:T(8,128)(2,1)} %param.15) | copy-start | bytes 196612
  63.1 18.4 %all-to-all-start.2 = ((bf16[16,152,128]{2,1,0:T(8,128)(2,1)}), bf16[16,152,128]{2,1,0:T(8,128)(2,1)S(1)}, u32[]{:S(2)}, u32[]{:S(2)}) async-start(bf16[16,152,128]{2,1,0:T(8,128)(2,1)} %fusion.6), calls=%async_computation.2 | async-start | bytes 1245184 | tf_op jit(solution)/shard_map/all_to_all | solution.py:357
  68.3 10.9 %collective-permute-start.6 = (bf16[128,128]{1,0:T(8,128)(2,1)S(1)}, bf16[128,128]{1,0:T(8,128)(2,1)S(1)}, u32[]{:S(2)}, u32[]{:S(2)}) collective-permute-start(bf16[128,128]{1,0:T(8,128)(2,1)S(1)} %get-tuple-element.57), channel_id=1, source_target_pairs={{0,128},{128,0},{1,129},{129,1},{2,130},{130,2},{3,131},{131,3},{4... | collective-permute-start | bytes 98312 | tf_op jit(solution)/shard_map/ppermute | solution.py:305
  72.6 8.7 %collective-permute-start.4 = (bf16[16,12,128]{2,1,0:T(8,128)(2,1)S(1)}, bf16[16,12,128]{2,1,0:T(8,128)(2,1)S(1)}, u32[]{:S(2)}, u32[]{:S(2)}) collective-permute-start(bf16[16,12,128]{2,1,0:T(8,128)(2,1)S(1)} %slice.100), channel_id=1, source_target_pairs={{0,256},{256,0},{1,257},{257,1},{2,258},{258,2},{3,259},{259,3},{4... | collective-permute-start | bytes 147464 | tf_op jit(solution)/shard_map/ppermute | solution.py:314
  96.2 20.1 %all-to-all-start.3 = ((f32[16,14,128]{2,1,0:T(8,128)}), f32[16,14,128]{2,1,0:T(8,128)S(1)}, u32[]{:S(2)}, u32[]{:S(2)}) async-start(f32[16,14,128]{2,1,0:T(8,128)} %pad_maximum_fusion), calls=%async_computation.3 | async-start | bytes 262144 | tf_op jit(solution)/shard_map/all_to_all | solution.py:406
  101.9 20.4 %collective-permute-start.8 = (bf16[16,12,128]{2,0,1:T(8,128)(2,1)S(1)}, bf16[16,12,128]{2,0,1:T(8,128)(2,1)S(1)}, u32[]{:S(2)}, u32[]{:S(2)}) collective-permute-start(bf16[16,12,128]{2,0,1:T(8,128)(2,1)S(1)} %get-tuple-element.53), channel_id=1, source_target_pairs={{0,256},{256,0},{1,257},{257,1},{2,258},{258,2},{3,259},{259,3},{4... | collective-permute-start | bytes 147464 | tf_op jit(solution)/shard_map/ppermute | solution.py:314
  117.1 14.0 %all-to-all-start.4 = ((f32[32,14,128]{2,1,0:T(8,128)}), f32[32,14,128]{2,1,0:T(8,128)S(1)}, u32[]{:S(2)}, u32[]{:S(2)}) async-start(f32[32,14,128]{2,1,0:T(8,128)} %broadcast_in_dim.25), calls=%async_computation.4 | async-start | bytes 524288 | tf_op jit(solution)/shard_map/all_to_all | solution.py:28
  132.6 20.8 %all-to-all-start.5 = ((bf16[16,16,384]{2,1,0:T(8,128)(2,1)}), bf16[16,16,384]{2,1,0:T(8,128)(2,1)S(1)}, u32[]{:S(2)}, u32[]{:S(2)}) async-start(bf16[16,16,384]{2,1,0:T(8,128)(2,1)} %broadcast_in_dim.26), calls=%async_computation.5 | async-start | bytes 393216 | tf_op jit(solution)/shard_map/all_to_all | solution.py:28
  137.2 20.3 %collective-permute-start.7 = (bf16[128,128]{0,1:T(8,128)(2,1)S(1)}, bf16[128,128]{0,1:T(8,128)(2,1)S(1)}, u32[]{:S(2)}, u32[]{:S(2)}) collective-permute-start(bf16[128,128]{0,1:T(8,128)(2,1)S(1)} %bitcast.81), channel_id=1, source_target_pairs={{0,128},{128,0},{1,129},{129,1},{2,130},{130,2},{3,131},{131,3},{4... | collective-permute-start | bytes 98312 | tf_op jit(solution)/shard_map/ppermute | solution.py:382
  154.2 9.1 %all-to-all-start.6 = ((f32[4,16,384]{2,1,0:T(8,128)}), f32[4,16,384]{2,1,0:T(8,128)S(1)}, u32[]{:S(2)}, u32[]{:S(2)}) async-start(f32[4,16,384]{2,1,0:T(8,128)} %broadcast_in_dim.27), calls=%async_computation.6 | async-start | bytes 196608 | tf_op jit(solution)/shard_map/all_to_all | solution.py:28

commit v9 on v6

--- a/solution.py
+++ b/solution.py
@@ -87,15 +87,19 @@
         out_ref[a] = sums[a]
 
 
-def encode_tile(tile, conv_weight, conv_bias):
+def taps(tile, conv_weight):
     rows, columns, channels = tile.shape
     lat = conv_weight.shape[-1]
     weight = jnp.moveaxis(conv_weight, 4, 3).reshape(27 * lat, channels)
-    parts = pl.pallas_call(
+    return pl.pallas_call(
         conv_kernel,
         out_shape=jax.ShapeDtypeStruct((3, columns // 2, 8 * lat), F32),
         name="taps",
     )(tile.reshape(rows * columns, channels), weight)
+
+
+def latent_patches(parts, conv_bias):
+    lat = conv_bias.shape[0]
     total = (parts[2] + shifted(parts[1], SEQ, 1)) + shifted(parts[0], SEQ, 2)
     above, below = shifted(total, HEAD, 1), shifted(total, HEAD, -1)
     own = total[:, 2 * lat : 6 * lat]
@@ -108,160 +112,144 @@
 def attention_kernel(
     x_ref, high_ref, low_ref, gram_ref, row_ref, half_ref, cot_ref,
     out_ref, at_ref, b_ref,
-    both, keys, scores, probs, csum, query, qsum,
+    both, keys_all, scores_all, probs_all, csum, query, qsum,
 ):
-    head = pl.program_id(0)
-    heads = pl.num_programs(0)
+    heads = cot_ref.shape[0]
     pairs = both.shape[0]
     factor = HEAD_DIM**-0.5
     zero = jnp.zeros((FEAT, FEAT), BF16)
 
-    @pl.when(head == 0)
-    def _():
-        x = x_ref[:, : pairs // x_ref.shape[0], :].reshape(pairs, 2 * FEAT)
-        pieces = [
-            jnp.concatenate(
-                [jnp.concatenate([g, zero], axis=1), jnp.concatenate([zero, g], axis=1)], axis=0
+    x = x_ref[:, : pairs // x_ref.shape[0], :].reshape(pairs, 2 * FEAT)
+    pieces = [
+        jnp.concatenate(
+            [jnp.concatenate([g, zero], axis=1), jnp.concatenate([zero, g], axis=1)], axis=0
+        )
+        for g in three(gram_ref[...])
+    ]
+    y = (mm(x, pieces[2]) + mm(x, pieces[1])) + mm(x, pieces[0])
+    lane_i = lax.broadcasted_iota(jnp.int32, (2 * FEAT, 2 * FEAT), 0) // FEAT
+    lane_j = lax.broadcasted_iota(jnp.int32, (2 * FEAT, 2 * FEAT), 1) // FEAT
+    ones = (lane_i == lane_j).astype(F32).astype(BF16)
+    z = three(y * x.astype(F32))
+    square = (mm(z[2], ones) + mm(z[1], ones)) + mm(z[0], ones)
+    normed = x.astype(F32) * lax.rsqrt(jnp.maximum(square, 0.0) + 1e-06)
+    high, low = two(normed)
+    both[:, : 2 * FEAT] = high
+    both[:, 2 * FEAT :] = low
+    csum[...] = jnp.zeros_like(csum)
+    qsum[...] = jnp.zeros_like(qsum)
+    hot = lax.broadcasted_iota(jnp.int32, (row_ref.shape[0], pairs), 1) == row_ref[...]
+    got = mm(hot.astype(F32).astype(BF16), both[...])
+    second = half_ref[...] == 1
+    for k in range(2):
+        piece = got[:, 2 * FEAT * k : 2 * FEAT * (k + 1)]
+        query[:, FEAT * k : FEAT * (k + 1)] = jnp.where(
+            second, piece[:, FEAT:], piece[:, :FEAT]
+        ).astype(BF16)
+
+    for head in range(heads):
+        keys, scores, probs = keys_all.at[head], scores_all.at[head], probs_all.at[head]
+
+        def weight(t, ref):
+            block = ref[t * FEAT : (t + 1) * FEAT, :]
+            block = block.astype(F32)
+            return block[:, head * FEAT : (head + 1) * FEAT]
+
+        w_high = [weight(t, high_ref) for t in range(3)]
+        w_low = [weight(t, low_ref) for t in range(3)]
+        w_k, w_v = w_high[1] + w_low[1], w_high[2] + w_low[2]
+
+        def stacked(parts):
+            rows = []
+            for m in parts:
+                rows.append(jnp.concatenate([m, zero], axis=1))
+                rows.append(jnp.concatenate([zero, m], axis=1))
+            return jnp.concatenate(rows, axis=0)
+
+        main = stacked([w.astype(BF16) for w in w_high[1:]])
+        rest = stacked([w.astype(BF16) for w in w_low[1:]])
+        keys[...] = (
+            mm(jnp.concatenate([main, main], axis=1), both[...], NT)
+            + mm(rest, both[:, : 2 * FEAT], NT)
+        ).astype(BF16)
+
+        q_high, q_low = query[:, :FEAT], query[:, FEAT:]
+        wq_high, wq_low = w_high[0].astype(BF16), w_low[0].astype(BF16)
+        q = (mm(q_high, wq_high, NT) + (mm(q_high, wq_low, NT) + mm(q_low, wq_high, NT))).astype(BF16)
+        q_scaled = (q.astype(F32) * factor).astype(BF16)
+        cot = cot_ref[head]
+        count = q.shape[0]
+
+        top = jnp.full((count, 128), -jnp.inf, F32)
+        for part in range(2):
+            for c in range(0, pairs, CHUNK):
+                s = mm(q_scaled, keys[part * FEAT : (part + 1) * FEAT, c : c + CHUNK])
+                scores[:, part * pairs + c : part * pairs + c + CHUNK] = s
+                for k in range(0, CHUNK, 128):
+                    top = jnp.maximum(top, s[:, k : k + 128])
+        top = jnp.max(top, axis=1, keepdims=True)
+
+        total = jnp.zeros((count, 128), F32)
+        mixed = [jnp.zeros((count, 4 * FEAT), F32) for _ in range(2)]
+        for part in range(2):
+            for c in range(0, pairs, CHUNK):
+                at = part * pairs + c
+                p = jnp.exp(scores[:, at : at + CHUNK] - top)
+                probs[:, at : at + CHUNK] = p
+                for k in range(0, CHUNK, 128):
+                    total = total + p[:, k : k + 128]
+                mixed[part] = mixed[part] + mm(p.astype(BF16), both[c : c + CHUNK, :])
+
+        def folded(m):
+            return (m[0][:, :FEAT] + m[0][:, 2 * FEAT : 3 * FEAT]) + (
+                m[1][:, FEAT : 2 * FEAT] + m[1][:, 3 * FEAT :]
             )
-            for g in three(gram_ref[...])
-        ]
-        y = (mm(x, pieces[2]) + mm(x, pieces[1])) + mm(x, pieces[0])
-        lane_i = lax.broadcasted_iota(jnp.int32, (2 * FEAT, 2 * FEAT), 0) // FEAT
-        lane_j = lax.broadcasted_iota(jnp.int32, (2 * FEAT, 2 * FEAT), 1) // FEAT
-        ones = (lane_i == lane_j).astype(F32).astype(BF16)
-        z = three(y * x.astype(F32))
-        square = (mm(z[2], ones) + mm(z[1], ones)) + mm(z[0], ones)
-        normed = x.astype(F32) * lax.rsqrt(jnp.maximum(square, 0.0) + 1e-06)
-        high, low = two(normed)
-        both[:, : 2 * FEAT] = high
-        both[:, 2 * FEAT :] = low
-        csum[...] = jnp.zeros_like(csum)
-        qsum[...] = jnp.zeros_like(qsum)
-        hot = lax.broadcasted_iota(jnp.int32, (row_ref.shape[0], pairs), 1) == row_ref[...]
-        got = mm(hot.astype(F32).astype(BF16), both[...])
-        second = half_ref[...] == 1
-        for k in range(2):
-            piece = got[:, 2 * FEAT * k : 2 * FEAT * (k + 1)]
-            query[:, FEAT * k : FEAT * (k + 1)] = jnp.where(
-                second, piece[:, FEAT:], piece[:, :FEAT]
-            ).astype(BF16)
-
-    odd = head % 2
-
-    def weight(t, ref):
-        block = ref[t * FEAT : (t + 1) * FEAT, :]
-        block = block.astype(F32)
-        return jnp.where(odd == 1, block[:, FEAT:], block[:, :FEAT])
-
-    w_high = [weight(t, high_ref) for t in range(3)]
-    w_low = [weight(t, low_ref) for t in range(3)]
-    w_k, w_v = w_high[1] + w_low[1], w_high[2] + w_low[2]
-
-    def stacked(parts):
-        rows = []
-        for m in parts:
-            rows.append(jnp.concatenate([m, zero], axis=1))
-            rows.append(jnp.concatenate([zero, m], axis=1))
-        return jnp.concatenate(rows, axis=0)
-
-    main = stacked([w.astype(BF16) for w in w_high[1:]])
-    rest = stacked([w.astype(BF16) for w in w_low[1:]])
-    keys[...] = (
-        mm(jnp.concatenate([main, main], axis=1), both[...], NT)
-        + mm(rest, both[:, : 2 * FEAT], NT)
-    ).astype(BF16)
-
-    q_high, q_low = query[:, :FEAT], query[:, FEAT:]
-    wq_high, wq_low = w_high[0].astype(BF16), w_low[0].astype(BF16)
-    q = (mm(q_high, wq_high, NT) + (mm(q_high, wq_low, NT) + mm(q_low, wq_high, NT))).astype(BF16)
-    q_scaled = (q.astype(F32) * factor).astype(BF16)
-    cot = cot_ref[0]
-    count = q.shape[0]
-
-    top = jnp.full((count, 128), -jnp.inf, F32)
-    for part in range(2):
-        for c in range(0, pairs, CHUNK):
-            s = mm(q_scaled, keys[part * FEAT : (part + 1) * FEAT, c : c + CHUNK])
-            scores[:, part * pairs + c : part * pairs + c + CHUNK] = s
-            for k in range(0, CHUNK, 128):
-                top = jnp.maximum(top, s[:, k : k + 128])
-    top = jnp.max(top, axis=1, keepdims=True)
-
-    total = jnp.zeros((count, 128), F32)
-    mixed = [jnp.zeros((count, 4 * FEAT), F32) for _ in range(2)]
-    for part in range(2):
-        for c in range(0, pairs, CHUNK):
-            at = part * pairs + c
-            p = jnp.exp(scores[:, at : at + CHUNK] - top)
-            probs[:, at : at + CHUNK] = p
-            for k in range(0, CHUNK, 128):
-                total = total + p[:, k : k + 128]
-            mixed[part] = mixed[part] + mm(p.astype(BF16), both[c : c + CHUNK, :])
-
-    def folded(m):
-        return (m[0][:, :FEAT] + m[0][:, 2 * FEAT : 3 * FEAT]) + (
-            m[1][:, FEAT : 2 * FEAT] + m[1][:, 3 * FEAT :]
-        )
-
-    inverse = 1.0 / jnp.sum(total, axis=1, keepdims=True)
-    value = folded(mixed) * inverse
-    out = mm(value, w_v, NT, HIGHEST).astype(BF16)
-    out_ref[0] = out
-    delta = jnp.sum(cot.astype(F32) * out.astype(F32), axis=1, keepdims=True)
-
-    mixed = [jnp.zeros((count, 4 * FEAT), F32) for _ in range(2)]
-    for part in range(2):
-        for c in range(0, pairs, CHUNK):
-            at = part * pairs + c
-            dp = mm(cot, keys[(2 + part) * FEAT : (3 + part) * FEAT, c : c + CHUNK])
-            p = probs[:, at : at + CHUNK] * inverse
-            ds = p * (dp - delta)
-            mixed[part] = mixed[part] + mm(ds.astype(BF16), both[c : c + CHUNK, :])
-            both_sides = ds * scores[:, at : at + CHUNK] + p * dp
-            csum[:, at : at + CHUNK] += jnp.sum(both_sides.reshape(count // 8, 8, CHUNK), axis=0)
-    grad = folded(mixed)
-    dq = mm(grad, w_k, NT, HIGHEST) * factor
-    q32 = q.astype(F32)
-    qsum[...] += jnp.broadcast_to(jnp.sum(dq * q32, axis=1, keepdims=True), qsum.shape)
-    own = q_high.astype(F32) + q_low.astype(F32)
-    a_q = mm(dq, own, TN, HIGHEST)
-    a_k = mm(q_scaled.astype(F32), grad, TN, HIGHEST)
-    a_v = mm(cot.astype(F32), value, TN, HIGHEST)
-    for t, a in enumerate((a_q, a_k, a_v)):
-        for side in range(2):
-
-            @pl.when(odd == side)
-            def _():
-                at_ref[t * FEAT : (t + 1) * FEAT, side * FEAT : (side + 1) * FEAT] = a
-
-    @pl.when(head == heads - 1)
-    def _():
-        eye_i = lax.broadcasted_iota(jnp.int32, (2 * FEAT, 2 * FEAT), 0)
-        eye_j = lax.broadcasted_iota(jnp.int32, (2 * FEAT, 2 * FEAT), 1)
-        eye = (eye_i == eye_j).astype(F32).astype(BF16)
-        high = both[:, : 2 * FEAT]
-        turned = mm(eye, high, NT)
-        c_all = jnp.sum(csum[...], axis=0, keepdims=True)
-        weighted = jnp.concatenate(
-            [turned[:FEAT] * c_all[:, :pairs], turned[FEAT:] * c_all[:, pairs:]], axis=0
-        )
-        full = mm(weighted.astype(BF16), high)
-        own_part = mm(own * qsum[:, :FEAT], own, TN, HIGHEST)
-        b_ref[...] = ((full[:FEAT, :FEAT] + full[FEAT:, FEAT:]) + own_part) * (1.0 / D)
+
+        inverse = 1.0 / jnp.sum(total, axis=1, keepdims=True)
+        value = folded(mixed) * inverse
+        out = mm(value, w_v, NT, HIGHEST).astype(BF16)
+        out_ref[head] = out
+        delta = jnp.sum(cot.astype(F32) * out.astype(F32), axis=1, keepdims=True)
+
+        mixed = [jnp.zeros((count, 4 * FEAT), F32) for _ in range(2)]
+        for part in range(2):
+            for c in range(0, pairs, CHUNK):
+                at = part * pairs + c
+                dp = mm(cot, keys[(2 + part) * FEAT : (3 + part) * FEAT, c : c + CHUNK])
+                p = probs[:, at : at + CHUNK] * inverse
+                ds = p * (dp - delta)
+                mixed[part] = mixed[part] + mm(ds.astype(BF16), both[c : c + CHUNK, :])
+                both_sides = ds * scores[:, at : at + CHUNK] + p * dp
+                csum[:, at : at + CHUNK] += jnp.sum(both_sides.reshape(count // 8, 8, CHUNK), axis=0)
+        grad = folded(mixed)
+        dq = mm(grad, w_k, NT, HIGHEST) * factor
+        q32 = q.astype(F32)
+        qsum[...] += jnp.broadcast_to(jnp.sum(dq * q32, axis=1, keepdims=True), qsum.shape)
+        own = q_high.astype(F32) + q_low.astype(F32)
+        a_q = mm(dq, own, TN, HIGHEST)
+        a_k = mm(q_scaled.astype(F32), grad, TN, HIGHEST)
+        a_v = mm(cot.astype(F32), value, TN, HIGHEST)
+        for t, a in enumerate((a_q, a_k, a_v)):
+            at_ref[t * FEAT : (t + 1) * FEAT, head * FEAT : (head + 1) * FEAT] = a
+
+    eye_i = lax.broadcasted_iota(jnp.int32, (2 * FEAT, 2 * FEAT), 0)
+    eye_j = lax.broadcasted_iota(jnp.int32, (2 * FEAT, 2 * FEAT), 1)
+    eye = (eye_i == eye_j).astype(F32).astype(BF16)
+    high = both[:, : 2 * FEAT]
+    turned = mm(eye, high, NT)
+    c_all = jnp.sum(csum[...], axis=0, keepdims=True)
+    weighted = jnp.concatenate(
+        [turned[:FEAT] * c_all[:, :pairs], turned[FEAT:] * c_all[:, pairs:]], axis=0
+    )
+    full = mm(weighted.astype(BF16), high)
+    own_part = mm(own * qsum[:, :FEAT], own, TN, HIGHEST)
+    b_ref[...] = ((full[:FEAT, :FEAT] + full[FEAT:, FEAT:]) + own_part) * (1.0 / D)
 
 
 def attention(x, pairs, high, low, gram, row, half, cot):
     heads, count, _ = cot.shape
-    whole = lambda *shape: pl.BlockSpec(shape, lambda i: (0,) * len(shape))
-    per_head = pl.BlockSpec((1, count, HEAD_DIM), lambda i: (i, 0, 0))
     return pl.pallas_call(
         attention_kernel,
-        grid=(heads,),
-        in_specs=[
-            whole(*x.shape), whole(*high.shape), whole(*low.shape), whole(*gram.shape),
-            whole(*row.shape), whole(*half.shape), per_head,
-        ],
-        out_specs=[per_head, whole(*high.shape), whole(*gram.shape)],
         out_shape=[
             jax.ShapeDtypeStruct(cot.shape, BF16),
             jax.ShapeDtypeStruct(high.shape, F32),
@@ -269,15 +257,15 @@
         ],
         scratch_shapes=[
             pltpu.VMEM((pairs, 4 * FEAT), BF16),
-            pltpu.VMEM((4 * FEAT, pairs), BF16),
-            pltpu.VMEM((count, 2 * pairs), F32),
-            pltpu.VMEM((count, 2 * pairs), F32),
+            pltpu.VMEM((heads, 4 * FEAT, pairs), BF16),
+            pltpu.VMEM((heads, count, 2 * pairs), F32),
+            pltpu.VMEM((heads, count, 2 * pairs), F32),
             pltpu.VMEM((8, 2 * pairs), F32),
             pltpu.VMEM((count, 2 * FEAT), BF16),
             pltpu.VMEM((count, 128), F32),
         ],
         compiler_params=pltpu.CompilerParams(
-            dimension_semantics=("arbitrary",), vmem_limit_bytes=48 * 1024 * 1024
+            vmem_limit_bytes=48 * 1024 * 1024
         ),
         name="attention",
     )(x, high, low, gram, row, half, cot)
@@ -304,6 +292,8 @@
 
     w = qkv_weight.reshape(depth, 3, 2, 2, HEAD_DIM)
     w = jnp.transpose(w, (2, 1, 4, 3, 0)).reshape(2 * near_count, rows_each * 2, depth)
+    parts = taps(features[0, 0], conv_weight)
+    parts, w = lax.optimization_barrier((parts, w))
     w_slice = lax.all_to_all(w, SEQ, 0, 0, tiled=True)
     w_blocks = w_slice
     w_slice = jnp.transpose(w_slice, (1, 0, 2)).reshape(rows_each * 2, D)
@@ -324,10 +314,13 @@
         embed_weight, embed_weight, (((1,), (1,)), ((), ())), preferred_element_type=F32
     ) * (1.0 / D)
 
-    patch = encode_tile(features[0, 0], conv_weight, conv_bias)
-    token_order, grad_out, patch = lax.optimization_barrier((token_order, grad_out, patch))
+    patch = latent_patches(parts, conv_bias)
+    token_order, m_slice, patch, gram = lax.optimization_barrier(
+        (token_order, m_slice, patch, gram)
+    )
     own_rows = patch.shape[0]
     arrived = from_everyone(jnp.concatenate([patch, *two(m_slice)], axis=0), "seq_1")
+    grad_out, arrived = lax.optimization_barrier((grad_out, arrived))
     far_count, head_count = lax.axis_size("seq_0"), lax.axis_size(HEAD)
     plane = far_count * head_count
     mine = w_blocks.reshape(head_count, -1, far_count, rows_each * 2, depth)

time: 164 us -> 165 us (level)
  starting transfers between devices: 58 us -> 69.4 us
  waiting for transfers between devices: 57.3 us -> 48.8 us
  blocking collectives: 19.1 us -> 17.3 us
    all_to_all x1, waiting for transfers between devices: 11.8 us -> 1.3 us  [per_device(): w_slice = lax.all_to_all(w, SEQ, 0, 0, tiled=True)]
    all_to_all x1, waiting for transfers between devices: 11.1 us -> 1.66 us  [per_device(): lax.all_to_all(jnp.concatenate([latents, mine], axis=1), ('seq_0', *HEAD)...]
    ppermute x1, waiting for transfers between devices: 0.01 us -> 5.91 us  [swapped(): return (mine, lax.ppermute(given, 'seq_0', [(0, 1), (1, 0)]))]
    all_to_all x4, starting transfers between devices: 18.2 us -> 23.8 us  [from_everyone(): return lax.all_to_all(copies, axis, split_axis=0, concat_axis=0, tiled=True)]
    all_to_all x1, starting transfers between devices: 12.4 us -> 16.3 us  [per_device(): w_slice = lax.all_to_all(w, SEQ, 0, 0, tiled=True)]
    all_to_all x4, waiting for transfers between devices: 33.8 us -> 36.3 us  [from_everyone(): return lax.all_to_all(copies, axis, split_axis=0, concat_axis=0, tiled=True)]
    ppermute x1, waiting for transfers between devices: 0.01 us -> 1.95 us  [per_device(): lax.ppermute(token_order, 'seq_0', [(0, 1), (1, 0)])]
    all_to_all x1, blocking collectives: 19.1 us -> 17.3 us  [per_device(): at = jnp.sum(lax.all_to_all(at, 'seq_1', 0, 0, tiled=True), axis=0)]
  transfers between devices with their start and end apart: 13 -> 13, of which waited for: 7 -> 10; matrix products, arithmetic and copies ran while one was open for 4% -> 3% of each run, Pallas kernels for 0% -> 0%
where the time goes in v9:
time: 165 us; the launch traced here: 164 us
  starting transfers between devices  69.4 us (42%)
  waiting for transfers between devices  48.8 us (30%)
  blocking collectives  17.3 us (10%)
  Pallas kernels  15.1 us (9%)
  local copies, waits for them, and re-layouts  8.78 us (5%)
  other arithmetic  2.76 us (2%)
    all_to_all x4, waiting for transfers between devices, from_everyone(): return lax.all_to_all(copies, axis, split_axis=0, concat_axis=0, tiled=True)  36.3 us
    all_to_all x4, starting transfers between devices, from_everyone(): return lax.all_to_all(copies, axis, split_axis=0, concat_axis=0, tiled=True)  23.8 us
    all_to_all x1, blocking collectives, per_device(): at = jnp.sum(lax.all_to_all(at, 'seq_1', 0, 0, tiled=True), axis=0)  17.3 us
    all_to_all x1, starting transfers between devices, per_device(): w_slice = lax.all_to_all(w, SEQ, 0, 0, tiled=True)  16.3 us
    ppermute x4, starting transfers between devices, shifted(): lax.ppermute(value, axis, [(source, source + steps) for source in range(l...  13.2 us
    pallas_call x1, Pallas kernels, attention(): pl.pallas_call(attention_kernel, out_shape=[jax.ShapeDtypeStruct(cot.shap...  12.8 us
    all_to_all x1, starting transfers between devices, per_device(): lax.all_to_all(jnp.concatenate([latents, mine], axis=1), ('seq_0', *HEAD)...  6.22 us
    ppermute x1, waiting for transfers between devices, swapped(): return (mine, lax.ppermute(given, 'seq_0', [(0, 1), (1, 0)]))  5.91 us
  transfers between devices with their start and end apart: 13, of which 10 were waited for; matrix products, arithmetic and copies ran while one was open for 3% of the time, Pallas kernels for 0%

profile of v9, /device:TPU:32, one launch (start us, length us, event | category | flops | bytes accessed | tf_op | source)
XLA Modules:
  0.0 164.3 jit_solution(10583484084771323167)
XLA Ops:
  2.6 2.3 %taps.1 = f32[3,16,128]{2,1,0:T(8,128)} custom-call(bf16[64,512]{1,0:T(8,128)(2,1)} %bitcast.70, bf16[432,512]{1,0:T(8,128)(2,1)} %bitcast.63), custom_call_target="tpu_custom_call" | custom-call | tf_op jit(solution)/shard_map/taps/pallas_call | solution.py:94
  4.9 16.3 %all-to-all-start = ((bf16[32,24,96]{2,1,0:T(8,128)(2,1)}), bf16[32,24,96]{2,1,0:T(8,128)(2,1)S(1)}, u32[]{:S(2)}, u32[]{:S(2)}) async-start(bf16[32,24,96]{2,1,0:T(8,128)(2,1)} %bitcast.5), calls=%async_computation | async-start | bytes 393216 | tf_op jit(solution)/shard_map/all_to_all | solution.py:297
  21.9 4.3 %collective-permute-start.1 = (f32[16,128]{1,0:T(8,128)S(1)}, f32[16,128]{1,0:T(8,128)S(1)}, u32[]{:S(2)}, u32[]{:S(2)}) collective-permute-start(f32[16,128]{1,0:T(8,128)S(1)} %get-tuple-element.55), channel_id=1, source_target_pairs={{0,16},{8,24},{16,32},{24,40},{32,48},{40,56},{48,64},{56,72},{64,... | collective-permute-start | bytes 24584 | tf_op jit(solution)/shard_map/ppermute | solution.py:23
  26.2 4.6 %collective-permute-start = (f32[16,128]{1,0:T(8,128)S(1)}, f32[16,128]{1,0:T(8,128)S(1)}, u32[]{:S(2)}, u32[]{:S(2)}) collective-permute-start(f32[16,128]{1,0:T(8,128)S(1)} %get-tuple-element.54), channel_id=1, source_target_pairs={{0,8},{8,16},{16,24},{24,32},{32,40},{40,48},{48,56},{56,64},{64,7... | collective-permute-start | bytes 24584 | tf_op jit(solution)/shard_map/ppermute | solution.py:23
  32.8 1.3 collective-permute-start.3
  34.1 3.0 %collective-permute-start.2 = (f32[16,128]{1,0:T(8,128)S(1)}, f32[16,128]{1,0:T(8,128)S(1)}, u32[]{:S(2)}, u32[]{:S(2)}) collective-permute-start(f32[16,128]{1,0:T(8,128)S(1)} %fusion.30), channel_id=1, source_target_pairs={{0,1},{1,2},{2,3},{3,4},{4,5},{5,6},{6,7},{8,9},{9,10},{10,11},{11... | collective-permute-start | bytes 24584 | tf_op jit(solution)/shard_map/ppermute | solution.py:23
  38.2 1.3 all-to-all-done
  41.0 9.8 %all-to-all-start.1 = ((bf16[16,32,128]{2,1,0:T(8,128)(2,1)}), bf16[16,32,128]{2,1,0:T(8,128)(2,1)S(1)}, u32[]{:S(2)}, u32[]{:S(2)}) async-start(bf16[16,32,128]{2,1,0:T(8,128)(2,1)} %broadcast_in_dim.22), calls=%async_computation.1 | async-start | bytes 262144 | tf_op jit(solution)/shard_map/all_to_all | solution.py:28
  50.7 3.4 %collective-permute-start.4 = (s32[128]{0:T(128)S(1)}, s32[128]{0:T(128)S(1)}, u32[]{:S(2)}, u32[]{:S(2)}) collective-permute-start(s32[128]{0:T(128)S(1)} %copy-done.4), channel_id=1, source_target_pairs={{0,128},{128,0},{1,129},{129,1},{2,130},{130,2},{3,131},{131,3},{4... | collective-permute-start | bytes 1544 | tf_op jit(solution)/shard_map/ppermute | solution.py:341
  54.2 2.0 %collective-permute-done.4 = s32[128]{0:T(128)S(1)} collective-permute-done((s32[128]{0:T(128)S(1)}, s32[128]{0:T(128)S(1)}, u32[]{:S(2)}, u32[]{:S(2)}) %collective-permute-start.4) | collective-permute-done | bytes 544 | tf_op jit(solution)/shard_map/ppermute | solution.py:341
  56.3 8.9 %all-to-all-done.1 = bf16[16,32,128]{2,1,0:T(8,128)(2,1)S(1)} async-done(((bf16[16,32,128]{2,1,0:T(8,128)(2,1)}), bf16[16,32,128]{2,1,0:T(8,128)(2,1)S(1)}, u32[]{:S(2)}, u32[]{:S(2)}) %all-to-all-start.1) | async-done | bytes 131104 | tf_op jit(solution)/shard_map/all_to_all | solution.py:28
  66.2 6.2 %all-to-all-start.2 = ((bf16[16,152,128]{2,1,0:T(8,128)(2,1)}), bf16[16,152,128]{2,1,0:T(8,128)(2,1)S(1)}, u32[]{:S(2)}, u32[]{:S(2)}) async-start(bf16[16,152,128]{2,1,0:T(8,128)(2,1)} %fusion.6), calls=%async_computation.2 | async-start | bytes 1245184 | tf_op jit(solution)/shard_map/all_to_all | solution.py:333
  73.0 4.0 %collective-permute-start.5 = (bf16[128,128]{1,0:T(8,128)(2,1)S(1)}, bf16[128,128]{1,0:T(8,128)(2,1)S(1)}, u32[]{:S(2)}, u32[]{:S(2)}) collective-permute-start(bf16[128,128]{1,0:T(8,128)(2,1)S(1)} %get-tuple-element.51), channel_id=1, source_target_pairs={{0,128},{128,0},{1,129},{129,1},{2,130},{130,2},{3,131},{131,3},{4... | collective-permute-start | bytes 98312 | tf_op jit(solution)/shard_map/ppermute | solution.py:288
  77.1 5.9 %collective-permute-done.5 = bf16[128,128]{1,0:T(8,128)(2,1)S(1)} collective-permute-done((bf16[128,128]{1,0:T(8,128)(2,1)S(1)}, bf16[128,128]{1,0:T(8,128)(2,1)S(1)}, u32[]{:S(2)}, u32[]{:S(2)}) %collective-permute-start.5) | collective-permute-done | bytes 32800 | tf_op jit(solution)/shard_map/ppermute | solution.py:288
  83.1 1.7 %all-to-all-done.2.x_ref = bf16[16,152,128]{2,1,0:T(8,128)(2,1)S(1)} async-done(((bf16[16,152,128]{2,1,0:T(8,128)(2,1)}), bf16[16,152,128]{2,1,0:T(8,128)(2,1)S(1)}, u32[]{:S(2)}, u32[]{:S(2)}) %all-to-all-start.2) | async-done | bytes 622624 | tf_op jit(solution)/shard_map/all_to_all | solution.py:333
  84.8 12.8 %attention.1 = (bf16[2,256,64]{2,1,0:T(8,128)(2,1)S(1)}, f32[192,128]{1,0:T(8,128)S(1)}, f32[64,64]{1,0:T(8,128)S(1)}) custom-call(bf16[16,152,128]{2,1,0:T(8,128)(2,1)S(1)} %all-to-all-done.2.x_ref, bf16[192,128]{1,0:T(8,128)(2,1)S(1)} %reshape.621.high_ref, bf16[192,128]{1,0:T(8,128)(2,1)S(1)} %reshape.622.low_ref, ...), custom_call_target="tpu_custom_call" | custom-call | tf_op jit(solution)/shard_map/attention/pallas_call | solution.py:251
  97.8 17.3 %all_to_all.35 = f32[16,14,128]{2,1,0:T(8,128)S(1)} all-to-all(f32[16,14,128]{2,1,0:T(8,128)S(1)} %pad_maximum_fusion), channel_id=1, replica_groups=mesh['grp'=2,'seq_0'=2,'seq_1'=16,'head_0'=4,'head_1'=2] {'seq_1'}, dimensions={0} | all-to-all | bytes 229376 | tf_op jit(solution)/shard_map/all_to_all | solution.py:372
  115.8 5.8 %all-to-all-start.4 = ((f32[32,14,128]{2,1,0:T(8,128)}), f32[32,14,128]{2,1,0:T(8,128)S(1)}, u32[]{:S(2)}, u32[]{:S(2)}) async-start(f32[32,14,128]{2,1,0:T(8,128)} %broadcast_in_dim.25), calls=%async_computation.4 | async-start | bytes 524288 | tf_op jit(solution)/shard_map/all_to_all | solution.py:28
  121.8 8.7 %all-to-all-done.4 = f32[32,14,128]{2,1,0:T(8,128)S(1)} async-done(((f32[32,14,128]{2,1,0:T(8,128)}), f32[32,14,128]{2,1,0:T(8,128)S(1)}, u32[]{:S(2)}, u32[]{:S(2)}) %all-to-all-start.4) | async-done | bytes 229408 | tf_op jit(solution)/shard_map/all_to_all | solution.py:28
  132.2 5.0 %all-to-all-start.5 = ((bf16[16,16,384]{2,1,0:T(8,128)(2,1)}), bf16[16,16,384]{2,1,0:T(8,128)(2,1)S(1)}, u32[]{:S(2)}, u32[]{:S(2)}) async-start(bf16[16,16,384]{2,1,0:T(8,128)(2,1)} %broadcast_in_dim.26), calls=%async_computation.5 | async-start | bytes 393216 | tf_op jit(solution)/shard_map/all_to_all | solution.py:28
  137.3 2.5 %collective-permute-start.6 = (bf16[128,128]{0,1:T(8,128)(2,1)S(1)}, bf16[128,128]{0,1:T(8,128)(2,1)S(1)}, u32[]{:S(2)}, u32[]{:S(2)}) collective-permute-start(bf16[128,128]{0,1:T(8,128)(2,1)S(1)} %bitcast.71), channel_id=1, source_target_pairs={{0,128},{128,0},{1,129},{129,1},{2,130},{130,2},{3,131},{131,3},{4... | collective-permute-start | bytes 98312 | tf_op jit(solution)/shard_map/ppermute | solution.py:356
  139.9 13.7 %all-to-all-done.5 = bf16[16,16,384]{2,1,0:T(8,128)(2,1)S(1)} async-done(((bf16[16,16,384]{2,1,0:T(8,128)(2,1)}), bf16[16,16,384]{2,1,0:T(8,128)(2,1)S(1)}, u32[]{:S(2)}, u32[]{:S(2)}) %all-to-all-start.5) | async-done | bytes 196640 | tf_op jit(solution)/shard_map/all_to_all | solution.py:28
  154.3 3.3 %all-to-all-start.6 = ((f32[4,16,384]{2,1,0:T(8,128)}), f32[4,16,384]{2,1,0:T(8,128)S(1)}, u32[]{:S(2)}, u32[]{:S(2)}) async-start(f32[4,16,384]{2,1,0:T(8,128)} %broadcast_in_dim.27), calls=%async_computation.6 | async-start | bytes 196608 | tf_op jit(solution)/shard_map/all_to_all | solution.py:28
  158.4 5.0 %all-to-all-done.6 = f32[4,16,384]{2,1,0:T(8,128)S(1)} async-done(((f32[4,16,384]{2,1,0:T(8,128)}), f32[4,16,384]{2,1,0:T(8,128)S(1)}, u32[]{:S(2)}, u32[]{:S(2)}) %all-to-all-start.6) | async-done | bytes 98336 | tf_op jit(solution)/shard_map/all_to_all | solution.py:28
  (80 shorter events, 14.2 us)
Async XLA Ops:
  1.7 29.1 %copy-start = (bf16[64,3072]{1,0:T(8,128)(2,1)S(1)}, bf16[64,3072]{1,0:T(8,128)(2,1)}, u32[]{:S(2)}) copy-start(bf16[64,3072]{1,0:T(8,128)(2,1)} %param.12) | copy-start | bytes 1179652
  1.7 29.1 %copy-start.2 = (f32[3072]{0:T(1024)S(1)}, f32[3072]{0:T(1024)}, u32[]{:S(2)}) copy-start(f32[3072]{0:T(1024)} %param.13) | copy-start | bytes 36868
  4.9 34.6 %all-to-all-start = ((bf16[32,24,96]{2,1,0:T(8,128)(2,1)}), bf16[32,24,96]{2,1,0:T(8,128)(2,1)S(1)}, u32[]{:S(2)}, u32[]{:S(2)}) async-start(bf16[32,24,96]{2,1,0:T(8,128)(2,1)} %bitcast.5), calls=%async_computation | async-start | bytes 393216 | tf_op jit(solution)/shard_map/all_to_all | solution.py:297
  21.9 9.0 %collective-permute-start.1 = (f32[16,128]{1,0:T(8,128)S(1)}, f32[16,128]{1,0:T(8,128)S(1)}, u32[]{:S(2)}, u32[]{:S(2)}) collective-permute-start(f32[16,128]{1,0:T(8,128)S(1)} %get-tuple-element.55), channel_id=1, source_target_pairs={{0,16},{8,24},{16,32},{24,40},{32,48},{40,56},{48,64},{56,72},{64,... | collective-permute-start | bytes 24584 | tf_op jit(solution)/shard_map/ppermute | solution.py:23
  26.2 5.9 %collective-permute-start = (f32[16,128]{1,0:T(8,128)S(1)}, f32[16,128]{1,0:T(8,128)S(1)}, u32[]{:S(2)}, u32[]{:S(2)}) collective-permute-start(f32[16,128]{1,0:T(8,128)S(1)} %get-tuple-element.54), channel_id=1, source_target_pairs={{0,8},{8,16},{16,24},{24,32},{32,40},{40,48},{48,56},{56,64},{64,7... | collective-permute-start | bytes 24584 | tf_op jit(solution)/shard_map/ppermute | solution.py:23
  30.9 6.5 %copy-start.3 = (f32[16]{0:T(128)S(1)}, f32[16]{0:T(128)}, u32[]{:S(2)}) copy-start(f32[16]{0:T(128)} %param.10) | copy-start | bytes 196
  32.8 5.2 %collective-permute-start.3 = (f32[16,128]{1,0:T(8,128)S(1)}, f32[16,128]{1,0:T(8,128)S(1)}, u32[]{:S(2)}, u32[]{:S(2)}) collective-permute-start(f32[16,128]{1,0:T(8,128)S(1)} %fusion.30), channel_id=1, source_target_pairs={{1,0},{2,1},{3,2},{4,3},{5,4},{6,5},{7,6},{9,8},{10,9},{11,10},{12... | collective-permute-start | bytes 24584 | tf_op jit(solution)/shard_map/ppermute | solution.py:23
  34.1 3.8 %collective-permute-start.2 = (f32[16,128]{1,0:T(8,128)S(1)}, f32[16,128]{1,0:T(8,128)S(1)}, u32[]{:S(2)}, u32[]{:S(2)}) collective-permute-start(f32[16,128]{1,0:T(8,128)S(1)} %fusion.30), channel_id=1, source_target_pairs={{0,1},{1,2},{2,3},{3,4},{4,5},{5,6},{6,7},{8,9},{9,10},{10,11},{11... | collective-permute-start | bytes 24584 | tf_op jit(solution)/shard_map/ppermute | solution.py:23
  39.8 10.9 %copy-start.4 = (s32[128]{0:T(128)S(1)}, s32[128]{0:T(128)}, u32[]{:S(2)}) copy-start(s32[128]{0:T(128)} %param.11) | copy-start | bytes 1540
  41.0 24.2 %all-to-all-start.1 = ((bf16[16,32,128]{2,1,0:T(8,128)(2,1)}), bf16[16,32,128]{2,1,0:T(8,128)(2,1)S(1)}, u32[]{:S(2)}, u32[]{:S(2)}) async-start(bf16[16,32,128]{2,1,0:T(8,128)(2,1)} %broadcast_in_dim.22), calls=%async_computation.1 | async-start | bytes 262144 | tf_op jit(solution)/shard_map/all_to_all | solution.py:28
  50.7 5.4 %collective-permute-start.4 = (s32[128]{0:T(128)S(1)}, s32[128]{0:T(128)S(1)}, u32[]{:S(2)}, u32[]{:S(2)}) collective-permute-start(s32[128]{0:T(128)S(1)} %copy-done.4), channel_id=1, source_target_pairs={{0,128},{128,0},{1,129},{129,1},{2,130},{130,2},{3,131},{131,3},{4... | collective-permute-start | bytes 1544 | tf_op jit(solution)/shard_map/ppermute | solution.py:341
  66.2 6.7 %copy-start.1 = (bf16[1,128,256]{2,1,0:T(8,128)(2,1)S(1)}, bf16[1,128,256]{2,1,0:T(8,128)(2,1)}, u32[]{:S(2)}) copy-start(bf16[1,128,256]{2,1,0:T(8,128)(2,1)} %param.15) | copy-start | bytes 196612
  66.2 18.5 %all-to-all-start.2 = ((bf16[16,152,128]{2,1,0:T(8,128)(2,1)}), bf16[16,152,128]{2,1,0:T(8,128)(2,1)S(1)}, u32[]{:S(2)}, u32[]{:S(2)}) async-start(bf16[16,152,128]{2,1,0:T(8,128)(2,1)} %fusion.6), calls=%async_computation.2 | async-start | bytes 1245184 | tf_op jit(solution)/shard_map/all_to_all | solution.py:333
  73.0 10.0 %collective-permute-start.5 = (bf16[128,128]{1,0:T(8,128)(2,1)S(1)}, bf16[128,128]{1,0:T(8,128)(2,1)S(1)}, u32[]{:S(2)}, u32[]{:S(2)}) collective-permute-start(bf16[128,128]{1,0:T(8,128)(2,1)S(1)} %get-tuple-element.51), channel_id=1, source_target_pairs={{0,128},{128,0},{1,129},{129,1},{2,130},{130,2},{3,131},{131,3},{4... | collective-permute-start | bytes 98312 | tf_op jit(solution)/shard_map/ppermute | solution.py:288
  115.8 14.8 %all-to-all-start.4 = ((f32[32,14,128]{2,1,0:T(8,128)}), f32[32,14,128]{2,1,0:T(8,128)S(1)}, u32[]{:S(2)}, u32[]{:S(2)}) async-start(f32[32,14,128]{2,1,0:T(8,128)} %broadcast_in_dim.25), calls=%async_computation.4 | async-start | bytes 524288 | tf_op jit(solution)/shard_map/all_to_all | solution.py:28
  132.2 21.4 %all-to-all-start.5 = ((bf16[16,16,384]{2,1,0:T(8,128)(2,1)}), bf16[16,16,384]{2,1,0:T(8,128)(2,1)S(1)}, u32[]{:S(2)}, u32[]{:S(2)}) async-start(bf16[16,16,384]{2,1,0:T(8,128)(2,1)} %broadcast_in_dim.26), calls=%async_computation.5 | async-start | bytes 393216 | tf_op jit(solution)/shard_map/all_to_all | solution.py:28
  137.3 20.3 %collective-permute-start.6 = (bf16[128,128]{0,1:T(8,128)(2,1)S(1)}, bf16[128,128]{0,1:T(8,128)(2,1)S(1)}, u32[]{:S(2)}, u32[]{:S(2)}) collective-permute-start(bf16[128,128]{0,1:T(8,128)(2,1)S(1)} %bitcast.71), channel_id=1, source_target_pairs={{0,128},{128,0},{1,129},{129,1},{2,130},{130,2},{3,131},{131,3},{4... | collective-permute-start | bytes 98312 | tf_op jit(solution)/shard_map/ppermute | solution.py:356
  154.3 9.1 %all-to-all-start.6 = ((f32[4,16,384]{2,1,0:T(8,128)}), f32[4,16,384]{2,1,0:T(8,128)S(1)}, u32[]{:S(2)}, u32[]{:S(2)}) async-start(f32[4,16,384]{2,1,0:T(8,128)} %broadcast_in_dim.27), calls=%async_computation.6 | async-start | bytes 196608 | tf_op jit(solution)/shard_map/all_to_all | solution.py:28

commit v10 on v9

--- a/solution.py
+++ b/solution.py
@@ -87,19 +87,15 @@
         out_ref[a] = sums[a]
 
 
-def taps(tile, conv_weight):
+def encode_tile(tile, conv_weight, conv_bias):
     rows, columns, channels = tile.shape
     lat = conv_weight.shape[-1]
     weight = jnp.moveaxis(conv_weight, 4, 3).reshape(27 * lat, channels)
-    return pl.pallas_call(
+    parts = pl.pallas_call(
         conv_kernel,
         out_shape=jax.ShapeDtypeStruct((3, columns // 2, 8 * lat), F32),
         name="taps",
     )(tile.reshape(rows * columns, channels), weight)
-
-
-def latent_patches(parts, conv_bias):
-    lat = conv_bias.shape[0]
     total = (parts[2] + shifted(parts[1], SEQ, 1)) + shifted(parts[0], SEQ, 2)
     above, below = shifted(total, HEAD, 1), shifted(total, HEAD, -1)
     own = total[:, 2 * lat : 6 * lat]
@@ -112,7 +108,7 @@
 def attention_kernel(
     x_ref, high_ref, low_ref, gram_ref, row_ref, half_ref, cot_ref,
     out_ref, at_ref, b_ref,
-    both, keys_all, scores_all, probs_all, csum, query, qsum,
+    both, keys, scores, probs, csum, query,
 ):
     heads = cot_ref.shape[0]
     pairs = both.shape[0]
@@ -136,8 +132,6 @@
     high, low = two(normed)
     both[:, : 2 * FEAT] = high
     both[:, 2 * FEAT :] = low
-    csum[...] = jnp.zeros_like(csum)
-    qsum[...] = jnp.zeros_like(qsum)
     hot = lax.broadcasted_iota(jnp.int32, (row_ref.shape[0], pairs), 1) == row_ref[...]
     got = mm(hot.astype(F32).astype(BF16), both[...])
     second = half_ref[...] == 1
@@ -147,17 +141,16 @@
             second, piece[:, FEAT:], piece[:, :FEAT]
         ).astype(BF16)
 
-    for head in range(heads):
-        keys, scores, probs = keys_all.at[head], scores_all.at[head], probs_all.at[head]
-
-        def weight(t, ref):
-            block = ref[t * FEAT : (t + 1) * FEAT, :]
-            block = block.astype(F32)
-            return block[:, head * FEAT : (head + 1) * FEAT]
-
-        w_high = [weight(t, high_ref) for t in range(3)]
-        w_low = [weight(t, low_ref) for t in range(3)]
-        w_k, w_v = w_high[1] + w_low[1], w_high[2] + w_low[2]
+    sides = [slice(head * FEAT, (head + 1) * FEAT) for head in range(heads)]
+    q_high, q_low = query[:, :FEAT], query[:, FEAT:]
+    own = q_high.astype(F32) + q_low.astype(F32)
+    count = q_high.shape[0]
+    queries, w_keys, w_values = [], [], []
+    for head, side in enumerate(sides):
+        w_high = [high_ref[t * FEAT : (t + 1) * FEAT, side] for t in range(3)]
+        w_low = [low_ref[t * FEAT : (t + 1) * FEAT, side] for t in range(3)]
+        w_keys.append(w_high[1].astype(F32) + w_low[1].astype(F32))
+        w_values.append(w_high[2].astype(F32) + w_low[2].astype(F32))
 
         def stacked(parts):
             rows = []
@@ -166,71 +159,83 @@
                 rows.append(jnp.concatenate([zero, m], axis=1))
             return jnp.concatenate(rows, axis=0)
 
-        main = stacked([w.astype(BF16) for w in w_high[1:]])
-        rest = stacked([w.astype(BF16) for w in w_low[1:]])
-        keys[...] = (
+        main, rest = stacked(w_high[1:]), stacked(w_low[1:])
+        keys[head] = (
             mm(jnp.concatenate([main, main], axis=1), both[...], NT)
             + mm(rest, both[:, : 2 * FEAT], NT)
         ).astype(BF16)
-
-        q_high, q_low = query[:, :FEAT], query[:, FEAT:]
-        wq_high, wq_low = w_high[0].astype(BF16), w_low[0].astype(BF16)
-        q = (mm(q_high, wq_high, NT) + (mm(q_high, wq_low, NT) + mm(q_low, wq_high, NT))).astype(BF16)
-        q_scaled = (q.astype(F32) * factor).astype(BF16)
-        cot = cot_ref[head]
-        count = q.shape[0]
-
-        top = jnp.full((count, 128), -jnp.inf, F32)
-        for part in range(2):
-            for c in range(0, pairs, CHUNK):
-                s = mm(q_scaled, keys[part * FEAT : (part + 1) * FEAT, c : c + CHUNK])
-                scores[:, part * pairs + c : part * pairs + c + CHUNK] = s
-                for k in range(0, CHUNK, 128):
-                    top = jnp.maximum(top, s[:, k : k + 128])
-        top = jnp.max(top, axis=1, keepdims=True)
-
-        total = jnp.zeros((count, 128), F32)
-        mixed = [jnp.zeros((count, 4 * FEAT), F32) for _ in range(2)]
-        for part in range(2):
-            for c in range(0, pairs, CHUNK):
-                at = part * pairs + c
-                p = jnp.exp(scores[:, at : at + CHUNK] - top)
-                probs[:, at : at + CHUNK] = p
-                for k in range(0, CHUNK, 128):
-                    total = total + p[:, k : k + 128]
-                mixed[part] = mixed[part] + mm(p.astype(BF16), both[c : c + CHUNK, :])
-
-        def folded(m):
-            return (m[0][:, :FEAT] + m[0][:, 2 * FEAT : 3 * FEAT]) + (
-                m[1][:, FEAT : 2 * FEAT] + m[1][:, 3 * FEAT :]
+        q = mm(q_high, w_high[0], NT) + (mm(q_high, w_low[0], NT) + mm(q_low, w_high[0], NT))
+        queries.append(q.astype(BF16))
+    scaled = [(q.astype(F32) * factor).astype(BF16) for q in queries]
+    cots = [cot_ref[head] for head in range(heads)]
+
+    def products(rows, part, c):
+        return jnp.concatenate(
+            [
+                mm(r, keys[head, part * FEAT : (part + 1) * FEAT, c : c + CHUNK])
+                for head, r in enumerate(rows)
+            ],
+            axis=0,
+        )
+
+    top = jnp.full((heads * count, 128), -jnp.inf, F32)
+    for part in range(2):
+        for c in range(0, pairs, CHUNK):
+            s = products(scaled, part, c)
+            scores[:, part * pairs + c : part * pairs + c + CHUNK] = s
+            for k in range(0, CHUNK, 128):
+                top = jnp.maximum(top, s[:, k : k + 128])
+    top = jnp.max(top, axis=1, keepdims=True)
+
+    total = jnp.zeros((heads * count, 128), F32)
+    mixed = [jnp.zeros((heads * count, 4 * FEAT), F32) for _ in range(2)]
+    for part in range(2):
+        for c in range(0, pairs, CHUNK):
+            at = part * pairs + c
+            p = jnp.exp(scores[:, at : at + CHUNK] - top)
+            probs[:, at : at + CHUNK] = p
+            for k in range(0, CHUNK, 128):
+                total = total + p[:, k : k + 128]
+            mixed[part] = mixed[part] + mm(p.astype(BF16), both[c : c + CHUNK, :])
+
+    def folded(m):
+        return (m[0][:, :FEAT] + m[0][:, 2 * FEAT : 3 * FEAT]) + (
+            m[1][:, FEAT : 2 * FEAT] + m[1][:, 3 * FEAT :]
+        )
+
+    inverse = 1.0 / jnp.sum(total, axis=1, keepdims=True)
+    value = folded(mixed) * inverse
+    deltas = []
+    for head in range(heads):
+        out = mm(value[head * count : (head + 1) * count], w_values[head], NT, HIGHEST)
+        out = out.astype(BF16)
+        out_ref[head] = out
+        deltas.append(
+            jnp.sum(cots[head].astype(F32) * out.astype(F32), axis=1, keepdims=True)
+        )
+    delta = jnp.concatenate(deltas, axis=0)
+
+    mixed = [jnp.zeros((heads * count, 4 * FEAT), F32) for _ in range(2)]
+    for part in range(2):
+        for c in range(0, pairs, CHUNK):
+            at = part * pairs + c
+            dp = products(cots, 2 + part, c)
+            p = probs[:, at : at + CHUNK] * inverse
+            ds = p * (dp - delta)
+            mixed[part] = mixed[part] + mm(ds.astype(BF16), both[c : c + CHUNK, :])
+            both_sides = ds * scores[:, at : at + CHUNK] + p * dp
+            csum[:, at : at + CHUNK] = jnp.sum(
+                both_sides.reshape(heads * count // 8, 8, CHUNK), axis=0
             )
-
-        inverse = 1.0 / jnp.sum(total, axis=1, keepdims=True)
-        value = folded(mixed) * inverse
-        out = mm(value, w_v, NT, HIGHEST).astype(BF16)
-        out_ref[head] = out
-        delta = jnp.sum(cot.astype(F32) * out.astype(F32), axis=1, keepdims=True)
-
-        mixed = [jnp.zeros((count, 4 * FEAT), F32) for _ in range(2)]
-        for part in range(2):
-            for c in range(0, pairs, CHUNK):
-                at = part * pairs + c
-                dp = mm(cot, keys[(2 + part) * FEAT : (3 + part) * FEAT, c : c + CHUNK])
-                p = probs[:, at : at + CHUNK] * inverse
-                ds = p * (dp - delta)
-                mixed[part] = mixed[part] + mm(ds.astype(BF16), both[c : c + CHUNK, :])
-                both_sides = ds * scores[:, at : at + CHUNK] + p * dp
-                csum[:, at : at + CHUNK] += jnp.sum(both_sides.reshape(count // 8, 8, CHUNK), axis=0)
-        grad = folded(mixed)
-        dq = mm(grad, w_k, NT, HIGHEST) * factor
-        q32 = q.astype(F32)
-        qsum[...] += jnp.broadcast_to(jnp.sum(dq * q32, axis=1, keepdims=True), qsum.shape)
-        own = q_high.astype(F32) + q_low.astype(F32)
-        a_q = mm(dq, own, TN, HIGHEST)
-        a_k = mm(q_scaled.astype(F32), grad, TN, HIGHEST)
-        a_v = mm(cot.astype(F32), value, TN, HIGHEST)
-        for t, a in enumerate((a_q, a_k, a_v)):
-            at_ref[t * FEAT : (t + 1) * FEAT, head * FEAT : (head + 1) * FEAT] = a
+    grad = folded(mixed)
+    inner = 0.0
+    for head, side in enumerate(sides):
+        mine = slice(head * count, (head + 1) * count)
+        dq = mm(grad[mine], w_keys[head], NT, HIGHEST) * factor
+        inner = inner + jnp.sum(dq * queries[head].astype(F32), axis=1, keepdims=True)
+        at_ref[:FEAT, side] = mm(dq, own, TN, HIGHEST)
+        at_ref[FEAT : 2 * FEAT, side] = mm(scaled[head].astype(F32), grad[mine], TN, HIGHEST)
+        at_ref[2 * FEAT :, side] = mm(cots[head].astype(F32), value[mine], TN, HIGHEST)
 
     eye_i = lax.broadcasted_iota(jnp.int32, (2 * FEAT, 2 * FEAT), 0)
     eye_j = lax.broadcasted_iota(jnp.int32, (2 * FEAT, 2 * FEAT), 1)
@@ -242,7 +247,7 @@
         [turned[:FEAT] * c_all[:, :pairs], turned[FEAT:] * c_all[:, pairs:]], axis=0
     )
     full = mm(weighted.astype(BF16), high)
-    own_part = mm(own * qsum[:, :FEAT], own, TN, HIGHEST)
+    own_part = mm(own * inner, own, TN, HIGHEST)
     b_ref[...] = ((full[:FEAT, :FEAT] + full[FEAT:, FEAT:]) + own_part) * (1.0 / D)
 
 
@@ -258,11 +263,10 @@
         scratch_shapes=[
             pltpu.VMEM((pairs, 4 * FEAT), BF16),
             pltpu.VMEM((heads, 4 * FEAT, pairs), BF16),
-            pltpu.VMEM((heads, count, 2 * pairs), F32),
-            pltpu.VMEM((heads, count, 2 * pairs), F32),
+            pltpu.VMEM((heads * count, 2 * pairs), F32),
+            pltpu.VMEM((heads * count, 2 * pairs), F32),
             pltpu.VMEM((8, 2 * pairs), F32),
             pltpu.VMEM((count, 2 * FEAT), BF16),
-            pltpu.VMEM((count, 128), F32),
         ],
         compiler_params=pltpu.CompilerParams(
             vmem_limit_bytes=48 * 1024 * 1024
@@ -292,8 +296,6 @@
 
     w = qkv_weight.reshape(depth, 3, 2, 2, HEAD_DIM)
     w = jnp.transpose(w, (2, 1, 4, 3, 0)).reshape(2 * near_count, rows_each * 2, depth)
-    parts = taps(features[0, 0], conv_weight)
-    parts, w = lax.optimization_barrier((parts, w))
     w_slice = lax.all_to_all(w, SEQ, 0, 0, tiled=True)
     w_blocks = w_slice
     w_slice = jnp.transpose(w_slice, (1, 0, 2)).reshape(rows_each * 2, D)
@@ -314,13 +316,10 @@
         embed_weight, embed_weight, (((1,), (1,)), ((), ())), preferred_element_type=F32
     ) * (1.0 / D)
 
-    patch = latent_patches(parts, conv_bias)
-    token_order, m_slice, patch, gram = lax.optimization_barrier(
-        (token_order, m_slice, patch, gram)
-    )
+    patch = encode_tile(features[0, 0], conv_weight, conv_bias)
+    token_order, grad_out, patch = lax.optimization_barrier((token_order, grad_out, patch))
     own_rows = patch.shape[0]
     arrived = from_everyone(jnp.concatenate([patch, *two(m_slice)], axis=0), "seq_1")
-    grad_out, arrived = lax.optimization_barrier((grad_out, arrived))
     far_count, head_count = lax.axis_size("seq_0"), lax.axis_size(HEAD)
     plane = far_count * head_count
     mine = w_blocks.reshape(head_count, -1, far_count, rows_each * 2, depth)

time: 165 us -> 162 us (0.982)
  starting transfers between devices: 69.4 us -> 58 us
  waiting for transfers between devices: 48.8 us -> 57.3 us
  blocking collectives: 17.3 us -> 19.1 us
    all_to_all x1, waiting for transfers between devices: 1.3 us -> 11.8 us  [per_device(): w_slice = lax.all_to_all(w, SEQ, 0, 0, tiled=True)]
    all_to_all x1, waiting for transfers between devices: 1.66 us -> 11.1 us  [per_device(): lax.all_to_all(jnp.concatenate([latents, mine], axis=1), ('seq_0', *HEAD)...]
    ppermute x1, waiting for transfers between devices: 5.91 us -> 0.01 us  [swapped(): return (mine, lax.ppermute(given, 'seq_0', [(0, 1), (1, 0)]))]
    all_to_all x4, starting transfers between devices: 23.8 us -> 18.2 us  [from_everyone(): return lax.all_to_all(copies, axis, split_axis=0, concat_axis=0, tiled=True)]
    all_to_all x1, starting transfers between devices: 16.3 us -> 12.4 us  [per_device(): w_slice = lax.all_to_all(w, SEQ, 0, 0, tiled=True)]
    all_to_all x4, waiting for transfers between devices: 36.3 us -> 33.8 us  [from_everyone(): return lax.all_to_all(copies, axis, split_axis=0, concat_axis=0, tiled=True)]
    ppermute x1, waiting for transfers between devices: 1.95 us -> 0.01 us  [per_device(): lax.ppermute(token_order, 'seq_0', [(0, 1), (1, 0)])]
    all_to_all x1, blocking collectives: 17.3 us -> 19.1 us  [per_device(): at = jnp.sum(lax.all_to_all(at, 'seq_1', 0, 0, tiled=True), axis=0)]
  transfers between devices with their start and end apart: 13 -> 13, of which waited for: 10 -> 7; matrix products, arithmetic and copies ran while one was open for 3% -> 4% of each run, Pallas kernels for 0% -> 0%
where the time goes in v10:
time: 162 us; the launch traced here: 161 us
  starting transfers between devices  58 us (36%)
  waiting for transfers between devices  57.3 us (35%)
  blocking collectives  19.1 us (12%)
  Pallas kernels  14.1 us (9%)
  local copies, waits for them, and re-layouts  7.89 us (5%)
  other arithmetic  2.76 us (2%)
    all_to_all x4, waiting for transfers between devices, from_everyone(): return lax.all_to_all(copies, axis, split_axis=0, concat_axis=0, tiled=True)  33.8 us
    all_to_all x1, blocking collectives, per_device(): at = jnp.sum(lax.all_to_all(at, 'seq_1', 0, 0, tiled=True), axis=0)  19.1 us
    all_to_all x4, starting transfers between devices, from_everyone(): return lax.all_to_all(copies, axis, split_axis=0, concat_axis=0, tiled=True)  18.2 us
    ppermute x4, starting transfers between devices, shifted(): lax.ppermute(value, axis, [(source, source + steps) for source in range(l...  14.5 us
    all_to_all x1, starting transfers between devices, per_device(): w_slice = lax.all_to_all(w, SEQ, 0, 0, tiled=True)  12.4 us
    all_to_all x1, waiting for transfers between devices, per_device(): w_slice = lax.all_to_all(w, SEQ, 0, 0, tiled=True)  11.8 us
    pallas_call x1, Pallas kernels, attention(): pl.pallas_call(attention_kernel, out_shape=[jax.ShapeDtypeStruct(cot.shap...  11.8 us
    all_to_all x1, waiting for transfers between devices, per_device(): lax.all_to_all(jnp.concatenate([latents, mine], axis=1), ('seq_0', *HEAD)...  11.1 us
  transfers between devices with their start and end apart: 13, of which 7 were waited for; matrix products, arithmetic and copies ran while one was open for 4% of the time, Pallas kernels for 0%

profile of v10, /device:TPU:32, one launch (start us, length us, event | category | flops | bytes accessed | tf_op | source)
XLA Modules:
  0.0 161.3 jit_solution(799208384251800550)
XLA Ops:
  0.6 2.3 %taps.1 = f32[3,16,128]{2,1,0:T(8,128)} custom-call(bf16[64,512]{1,0:T(8,128)(2,1)} %bitcast.74, bf16[432,512]{1,0:T(8,128)(2,1)} %bitcast.67), custom_call_target="tpu_custom_call" | custom-call | tf_op jit(solution)/shard_map/taps/pallas_call | solution.py:94
  3.7 5.2 %collective-permute-start.1 = (f32[16,128]{1,0:T(8,128)S(1)}, f32[16,128]{1,0:T(8,128)S(1)}, u32[]{:S(2)}, u32[]{:S(2)}) collective-permute-start(f32[16,128]{1,0:T(8,128)S(1)} %get-tuple-element.45), channel_id=1, source_target_pairs={{0,16},{8,24},{16,32},{24,40},{32,48},{40,56},{48,64},{56,72},{64,... | collective-permute-start | bytes 24584 | tf_op jit(solution)/shard_map/ppermute | solution.py:23
  8.9 5.0 %collective-permute-start = (f32[16,128]{1,0:T(8,128)S(1)}, f32[16,128]{1,0:T(8,128)S(1)}, u32[]{:S(2)}, u32[]{:S(2)}) collective-permute-start(f32[16,128]{1,0:T(8,128)S(1)} %get-tuple-element.44), channel_id=1, source_target_pairs={{0,8},{8,16},{16,24},{24,32},{32,40},{40,48},{48,56},{56,64},{64,7... | collective-permute-start | bytes 24584 | tf_op jit(solution)/shard_map/ppermute | solution.py:23
  14.1 0.9 copy.105
  15.0 12.4 %all-to-all-start = ((bf16[32,24,96]{2,1,0:T(8,128)(2,1)}), bf16[32,24,96]{2,1,0:T(8,128)(2,1)S(1)}, u32[]{:S(2)}, u32[]{:S(2)}) async-start(bf16[32,24,96]{2,1,0:T(8,128)(2,1)} %bitcast.8), calls=%async_computation | async-start | bytes 393216 | tf_op jit(solution)/shard_map/all_to_all | solution.py:299
  28.2 1.3 collective-permute-start.3
  29.4 3.0 %collective-permute-start.2 = (f32[16,128]{1,0:T(8,128)S(1)}, f32[16,128]{1,0:T(8,128)S(1)}, u32[]{:S(2)}, u32[]{:S(2)}) collective-permute-start(f32[16,128]{1,0:T(8,128)S(1)} %fusion.30), channel_id=1, source_target_pairs={{0,1},{1,2},{2,3},{3,4},{4,5},{5,6},{6,7},{8,9},{9,10},{10,11},{11... | collective-permute-start | bytes 24584 | tf_op jit(solution)/shard_map/ppermute | solution.py:23
  33.5 11.8 %all-to-all-done = bf16[32,24,96]{2,1,0:T(8,128)(2,1)S(1)} async-done(((bf16[32,24,96]{2,1,0:T(8,128)(2,1)}), bf16[32,24,96]{2,1,0:T(8,128)(2,1)S(1)}, u32[]{:S(2)}, u32[]{:S(2)}) %all-to-all-start) | async-done | bytes 147488 | tf_op jit(solution)/shard_map/all_to_all | solution.py:299
  46.8 4.7 %all-to-all-start.1 = ((bf16[16,32,128]{2,1,0:T(8,128)(2,1)}), bf16[16,32,128]{2,1,0:T(8,128)(2,1)S(1)}, u32[]{:S(2)}, u32[]{:S(2)}) async-start(bf16[16,32,128]{2,1,0:T(8,128)(2,1)} %broadcast_in_dim.22), calls=%async_computation.1 | async-start | bytes 262144 | tf_op jit(solution)/shard_map/all_to_all | solution.py:28
  51.8 2.4 %collective-permute-start.4 = (s32[128]{0:T(128)S(1)}, s32[128]{0:T(128)S(1)}, u32[]{:S(2)}, u32[]{:S(2)}) collective-permute-start(s32[128]{0:T(128)S(1)} %copy-done.5), channel_id=1, source_target_pairs={{0,128},{128,0},{1,129},{129,1},{2,130},{130,2},{3,131},{131,3},{4... | collective-permute-start | bytes 1544 | tf_op jit(solution)/shard_map/ppermute | solution.py:340
  54.2 3.5 %collective-permute-start.5 = (bf16[128,128]{1,0:T(8,128)(2,1)S(1)}, bf16[128,128]{1,0:T(8,128)(2,1)S(1)}, u32[]{:S(2)}, u32[]{:S(2)}) collective-permute-start(bf16[128,128]{1,0:T(8,128)(2,1)S(1)} %get-tuple-element.41), channel_id=1, source_target_pairs={{0,128},{128,0},{1,129},{129,1},{2,130},{130,2},{3,131},{131,3},{4... | collective-permute-start | bytes 98312 | tf_op jit(solution)/shard_map/ppermute | solution.py:292
  57.7 6.4 %all-to-all-done.1 = bf16[16,32,128]{2,1,0:T(8,128)(2,1)S(1)} async-done(((bf16[16,32,128]{2,1,0:T(8,128)(2,1)}), bf16[16,32,128]{2,1,0:T(8,128)(2,1)S(1)}, u32[]{:S(2)}, u32[]{:S(2)}) %all-to-all-start.1) | async-done | bytes 131104 | tf_op jit(solution)/shard_map/all_to_all | solution.py:28
  64.2 0.9 fusion.5
  65.2 4.6 %all-to-all-start.2 = ((bf16[16,152,128]{2,1,0:T(8,128)(2,1)}), bf16[16,152,128]{2,1,0:T(8,128)(2,1)S(1)}, u32[]{:S(2)}, u32[]{:S(2)}) async-start(bf16[16,152,128]{2,1,0:T(8,128)(2,1)} %fusion.5), calls=%async_computation.2 | async-start | bytes 1245184 | tf_op jit(solution)/shard_map/all_to_all | solution.py:332
  70.6 11.1 %all-to-all-done.2.x_ref = bf16[16,152,128]{2,1,0:T(8,128)(2,1)S(1)} async-done(((bf16[16,152,128]{2,1,0:T(8,128)(2,1)}), bf16[16,152,128]{2,1,0:T(8,128)(2,1)S(1)}, u32[]{:S(2)}, u32[]{:S(2)}) %all-to-all-start.2) | async-done | bytes 622624 | tf_op jit(solution)/shard_map/all_to_all | solution.py:332
  81.7 11.8 %attention.1 = (bf16[2,256,64]{2,1,0:T(8,128)(2,1)S(1)}, f32[192,128]{1,0:T(8,128)S(1)}, f32[64,64]{1,0:T(8,128)S(1)}) custom-call(bf16[16,152,128]{2,1,0:T(8,128)(2,1)S(1)} %all-to-all-done.2.x_ref, bf16[192,128]{1,0:T(8,128)(2,1)S(1)} %reshape.621.high_ref, bf16[192,128]{1,0:T(8,128)(2,1)S(1)} %reshape.622.low_ref, ...), custom_call_target="tpu_custom_call" | custom-call | tf_op jit(solution)/shard_map/attention/pallas_call | solution.py:256
  93.6 19.1 %all_to_all.35 = f32[16,14,128]{2,1,0:T(8,128)S(1)} all-to-all(f32[16,14,128]{2,1,0:T(8,128)S(1)} %pad_maximum_fusion), channel_id=1, replica_groups=mesh['grp'=2,'seq_0'=2,'seq_1'=16,'head_0'=4,'head_1'=2] {'seq_1'}, dimensions={0} | all-to-all | bytes 229376 | tf_op jit(solution)/shard_map/all_to_all | solution.py:371
  113.4 5.1 %all-to-all-start.4 = ((f32[32,14,128]{2,1,0:T(8,128)}), f32[32,14,128]{2,1,0:T(8,128)S(1)}, u32[]{:S(2)}, u32[]{:S(2)}) async-start(f32[32,14,128]{2,1,0:T(8,128)} %broadcast_in_dim.25), calls=%async_computation.4 | async-start | bytes 524288 | tf_op jit(solution)/shard_map/all_to_all | solution.py:28
  118.7 8.7 %all-to-all-done.4 = f32[32,14,128]{2,1,0:T(8,128)S(1)} async-done(((f32[32,14,128]{2,1,0:T(8,128)}), f32[32,14,128]{2,1,0:T(8,128)S(1)}, u32[]{:S(2)}, u32[]{:S(2)}) %all-to-all-start.4) | async-done | bytes 229408 | tf_op jit(solution)/shard_map/all_to_all | solution.py:28
  129.1 5.1 %all-to-all-start.5 = ((bf16[16,16,384]{2,1,0:T(8,128)(2,1)}), bf16[16,16,384]{2,1,0:T(8,128)(2,1)S(1)}, u32[]{:S(2)}, u32[]{:S(2)}) async-start(bf16[16,16,384]{2,1,0:T(8,128)(2,1)} %broadcast_in_dim.26), calls=%async_computation.5 | async-start | bytes 393216 | tf_op jit(solution)/shard_map/all_to_all | solution.py:28
  134.3 2.5 %collective-permute-start.6 = (bf16[128,128]{0,1:T(8,128)(2,1)S(1)}, bf16[128,128]{0,1:T(8,128)(2,1)S(1)}, u32[]{:S(2)}, u32[]{:S(2)}) collective-permute-start(bf16[128,128]{0,1:T(8,128)(2,1)S(1)} %bitcast.75), channel_id=1, source_target_pairs={{0,128},{128,0},{1,129},{129,1},{2,130},{130,2},{3,131},{131,3},{4... | collective-permute-start | bytes 98312 | tf_op jit(solution)/shard_map/ppermute | solution.py:355
  136.9 13.7 %all-to-all-done.5 = bf16[16,16,384]{2,1,0:T(8,128)(2,1)S(1)} async-done(((bf16[16,16,384]{2,1,0:T(8,128)(2,1)}), bf16[16,16,384]{2,1,0:T(8,128)(2,1)S(1)}, u32[]{:S(2)}, u32[]{:S(2)}) %all-to-all-start.5) | async-done | bytes 196640 | tf_op jit(solution)/shard_map/all_to_all | solution.py:28
  151.3 3.3 %all-to-all-start.6 = ((f32[4,16,384]{2,1,0:T(8,128)}), f32[4,16,384]{2,1,0:T(8,128)S(1)}, u32[]{:S(2)}, u32[]{:S(2)}) async-start(f32[4,16,384]{2,1,0:T(8,128)} %broadcast_in_dim.27), calls=%async_computation.6 | async-start | bytes 196608 | tf_op jit(solution)/shard_map/all_to_all | solution.py:28
  155.4 5.0 %all-to-all-done.6 = f32[4,16,384]{2,1,0:T(8,128)S(1)} async-done(((f32[4,16,384]{2,1,0:T(8,128)}), f32[4,16,384]{2,1,0:T(8,128)S(1)}, u32[]{:S(2)}, u32[]{:S(2)}) %all-to-all-start.6) | async-done | bytes 98336 | tf_op jit(solution)/shard_map/all_to_all | solution.py:28
  (82 shorter events, 10.5 us)
Async XLA Ops:
  0.6 13.3 %copy-start.1 = (bf16[96,3,256]{2,0,1:T(8,128)(2,1)S(1)}, bf16[96,3,256]{2,0,1:T(8,128)(2,1)}, u32[]{:S(2)}) copy-start(bf16[96,3,256]{2,0,1:T(8,128)(2,1)} %param.14) | copy-start | bytes 442372
  3.0 29.5 %copy-start = (bf16[64,3072]{1,0:T(8,128)(2,1)S(1)}, bf16[64,3072]{1,0:T(8,128)(2,1)}, u32[]{:S(2)}) copy-start(bf16[64,3072]{1,0:T(8,128)(2,1)} %param.12) | copy-start | bytes 1179652
  3.0 29.5 %copy-start.3 = (f32[3072]{0:T(1024)S(1)}, f32[3072]{0:T(1024)}, u32[]{:S(2)}) copy-start(f32[3072]{0:T(1024)} %param.13) | copy-start | bytes 36868
  3.7 23.7 %collective-permute-start.1 = (f32[16,128]{1,0:T(8,128)S(1)}, f32[16,128]{1,0:T(8,128)S(1)}, u32[]{:S(2)}, u32[]{:S(2)}) collective-permute-start(f32[16,128]{1,0:T(8,128)S(1)} %get-tuple-element.45), channel_id=1, source_target_pairs={{0,16},{8,24},{16,32},{24,40},{32,48},{40,56},{48,64},{56,72},{64,... | collective-permute-start | bytes 24584 | tf_op jit(solution)/shard_map/ppermute | solution.py:23
  8.9 18.5 %collective-permute-start = (f32[16,128]{1,0:T(8,128)S(1)}, f32[16,128]{1,0:T(8,128)S(1)}, u32[]{:S(2)}, u32[]{:S(2)}) collective-permute-start(f32[16,128]{1,0:T(8,128)S(1)} %get-tuple-element.44), channel_id=1, source_target_pairs={{0,8},{8,16},{16,24},{24,32},{32,40},{40,48},{48,56},{56,64},{64,7... | collective-permute-start | bytes 24584 | tf_op jit(solution)/shard_map/ppermute | solution.py:23
  15.0 30.3 %all-to-all-start = ((bf16[32,24,96]{2,1,0:T(8,128)(2,1)}), bf16[32,24,96]{2,1,0:T(8,128)(2,1)S(1)}, u32[]{:S(2)}, u32[]{:S(2)}) async-start(bf16[32,24,96]{2,1,0:T(8,128)(2,1)} %bitcast.8), calls=%async_computation | async-start | bytes 393216 | tf_op jit(solution)/shard_map/all_to_all | solution.py:299
  27.4 5.2 %copy-start.4 = (f32[16]{0:T(128)S(1)}, f32[16]{0:T(128)}, u32[]{:S(2)}) copy-start(f32[16]{0:T(128)} %param.10) | copy-start | bytes 196
  28.2 5.2 %collective-permute-start.3 = (f32[16,128]{1,0:T(8,128)S(1)}, f32[16,128]{1,0:T(8,128)S(1)}, u32[]{:S(2)}, u32[]{:S(2)}) collective-permute-start(f32[16,128]{1,0:T(8,128)S(1)} %fusion.30), channel_id=1, source_target_pairs={{1,0},{2,1},{3,2},{4,3},{5,4},{6,5},{7,6},{9,8},{10,9},{11,10},{12... | collective-permute-start | bytes 24584 | tf_op jit(solution)/shard_map/ppermute | solution.py:23
  29.4 3.8 %collective-permute-start.2 = (f32[16,128]{1,0:T(8,128)S(1)}, f32[16,128]{1,0:T(8,128)S(1)}, u32[]{:S(2)}, u32[]{:S(2)}) collective-permute-start(f32[16,128]{1,0:T(8,128)S(1)} %fusion.30), channel_id=1, source_target_pairs={{0,1},{1,2},{2,3},{3,4},{4,5},{5,6},{6,7},{8,9},{9,10},{10,11},{11... | collective-permute-start | bytes 24584 | tf_op jit(solution)/shard_map/ppermute | solution.py:23
  46.1 5.7 %copy-start.5 = (s32[128]{0:T(128)S(1)}, s32[128]{0:T(128)}, u32[]{:S(2)}) copy-start(s32[128]{0:T(128)} %param.11) | copy-start | bytes 1540
  46.1 8.0 %copy-start.2 = (bf16[1,128,256]{2,1,0:T(8,128)(2,1)S(1)}, bf16[1,128,256]{2,1,0:T(8,128)(2,1)}, u32[]{:S(2)}) copy-start(bf16[1,128,256]{2,1,0:T(8,128)(2,1)} %param.15) | copy-start | bytes 196612
  46.8 17.3 %all-to-all-start.1 = ((bf16[16,32,128]{2,1,0:T(8,128)(2,1)}), bf16[16,32,128]{2,1,0:T(8,128)(2,1)S(1)}, u32[]{:S(2)}, u32[]{:S(2)}) async-start(bf16[16,32,128]{2,1,0:T(8,128)(2,1)} %broadcast_in_dim.22), calls=%async_computation.1 | async-start | bytes 262144 | tf_op jit(solution)/shard_map/all_to_all | solution.py:28
  51.8 17.9 %collective-permute-start.4 = (s32[128]{0:T(128)S(1)}, s32[128]{0:T(128)S(1)}, u32[]{:S(2)}, u32[]{:S(2)}) collective-permute-start(s32[128]{0:T(128)S(1)} %copy-done.5), channel_id=1, source_target_pairs={{0,128},{128,0},{1,129},{129,1},{2,130},{130,2},{3,131},{131,3},{4... | collective-permute-start | bytes 1544 | tf_op jit(solution)/shard_map/ppermute | solution.py:340
  54.2 16.2 %collective-permute-start.5 = (bf16[128,128]{1,0:T(8,128)(2,1)S(1)}, bf16[128,128]{1,0:T(8,128)(2,1)S(1)}, u32[]{:S(2)}, u32[]{:S(2)}) collective-permute-start(bf16[128,128]{1,0:T(8,128)(2,1)S(1)} %get-tuple-element.41), channel_id=1, source_target_pairs={{0,128},{128,0},{1,129},{129,1},{2,130},{130,2},{3,131},{131,3},{4... | collective-permute-start | bytes 98312 | tf_op jit(solution)/shard_map/ppermute | solution.py:292
  65.2 16.5 %all-to-all-start.2 = ((bf16[16,152,128]{2,1,0:T(8,128)(2,1)}), bf16[16,152,128]{2,1,0:T(8,128)(2,1)S(1)}, u32[]{:S(2)}, u32[]{:S(2)}) async-start(bf16[16,152,128]{2,1,0:T(8,128)(2,1)} %fusion.5), calls=%async_computation.2 | async-start | bytes 1245184 | tf_op jit(solution)/shard_map/all_to_all | solution.py:332
  113.4 14.1 %all-to-all-start.4 = ((f32[32,14,128]{2,1,0:T(8,128)}), f32[32,14,128]{2,1,0:T(8,128)S(1)}, u32[]{:S(2)}, u32[]{:S(2)}) async-start(f32[32,14,128]{2,1,0:T(8,128)} %broadcast_in_dim.25), calls=%async_computation.4 | async-start | bytes 524288 | tf_op jit(solution)/shard_map/all_to_all | solution.py:28
  129.1 21.5 %all-to-all-start.5 = ((bf16[16,16,384]{2,1,0:T(8,128)(2,1)}), bf16[16,16,384]{2,1,0:T(8,128)(2,1)S(1)}, u32[]{:S(2)}, u32[]{:S(2)}) async-start(bf16[16,16,384]{2,1,0:T(8,128)(2,1)} %broadcast_in_dim.26), calls=%async_computation.5 | async-start | bytes 393216 | tf_op jit(solution)/shard_map/all_to_all | solution.py:28
  134.3 20.3 %collective-permute-start.6 = (bf16[128,128]{0,1:T(8,128)(2,1)S(1)}, bf16[128,128]{0,1:T(8,128)(2,1)S(1)}, u32[]{:S(2)}, u32[]{:S(2)}) collective-permute-start(bf16[128,128]{0,1:T(8,128)(2,1)S(1)} %bitcast.75), channel_id=1, source_target_pairs={{0,128},{128,0},{1,129},{129,1},{2,130},{130,2},{3,131},{131,3},{4... | collective-permute-start | bytes 98312 | tf_op jit(solution)/shard_map/ppermute | solution.py:355
  151.3 9.1 %all-to-all-start.6 = ((f32[4,16,384]{2,1,0:T(8,128)}), f32[4,16,384]{2,1,0:T(8,128)S(1)}, u32[]{:S(2)}, u32[]{:S(2)}) async-start(f32[4,16,384]{2,1,0:T(8,128)} %broadcast_in_dim.27), calls=%async_computation.6 | async-start | bytes 196608 | tf_op jit(solution)/shard_map/all_to_all | solution.py:28

commit v11 on v10

--- a/solution.py
+++ b/solution.py
@@ -87,7 +87,7 @@
         out_ref[a] = sums[a]
 
 
-def encode_tile(tile, conv_weight, conv_bias):
+def taps(tile, conv_weight):
     rows, columns, channels = tile.shape
     lat = conv_weight.shape[-1]
     weight = jnp.moveaxis(conv_weight, 4, 3).reshape(27 * lat, channels)
@@ -96,6 +96,11 @@
         out_shape=jax.ShapeDtypeStruct((3, columns // 2, 8 * lat), F32),
         name="taps",
     )(tile.reshape(rows * columns, channels), weight)
+    return parts
+
+
+def latent_patches(parts, conv_bias):
+    lat = conv_bias.shape[0]
     total = (parts[2] + shifted(parts[1], SEQ, 1)) + shifted(parts[0], SEQ, 2)
     above, below = shifted(total, HEAD, 1), shifted(total, HEAD, -1)
     own = total[:, 2 * lat : 6 * lat]
@@ -294,15 +299,29 @@
     def in_order(mine, other):
         return jnp.where(far == 0, jnp.stack([mine, other]), jnp.stack([other, mine]))
 
+    clip = lax.axis_index("grp")
+    half_rows = rows_each // 2
+
+    def both_halves(mine, given, axis):
+        other = lax.ppermute(given, "grp", [(0, 1), (1, 0)])
+        return jnp.where(
+            clip == 0, jnp.stack([mine, other], axis), jnp.stack([other, mine], axis)
+        )
+
     w = qkv_weight.reshape(depth, 3, 2, 2, HEAD_DIM)
-    w = jnp.transpose(w, (2, 1, 4, 3, 0)).reshape(2 * near_count, rows_each * 2, depth)
-    w_slice = lax.all_to_all(w, SEQ, 0, 0, tiled=True)
-    w_blocks = w_slice
-    w_slice = jnp.transpose(w_slice, (1, 0, 2)).reshape(rows_each * 2, D)
+    w = jnp.transpose(w, (2, 1, 4, 3, 0)).reshape(2, near_count, 2, rows_each, depth)
+    w = jnp.where(clip == 0, w[:, :, 0], w[:, :, 1])
+    w = jnp.swapaxes(in_order(*swapped(w, 0))[:, 0], 0, 1).reshape(near_count, 2 * rows_each, depth)
+    parts = taps(features[0, 0], conv_weight)
+    parts, w = lax.optimization_barrier((parts, w))
+    w_blocks = lax.all_to_all(w, "seq_1", 0, 0, tiled=True)
+    w_blocks = w_blocks.reshape(near_count, 2, rows_each, depth)
+    w_blocks = jnp.swapaxes(w_blocks, 0, 1).reshape(2 * near_count, rows_each, depth)
+    w_slice = jnp.transpose(w_blocks, (1, 0, 2)).reshape(rows_each, D)
     embed32 = embed_weight.astype(F32)
     gained = jnp.concatenate(two(embed32 * norm_gain), axis=0)
     m_slice = mm(w_slice, gained, NT)
-    m_slice = (m_slice[:, :FEAT] + m_slice[:, FEAT:]).reshape(rows_each, 2 * FEAT)
+    m_slice = (m_slice[:, :FEAT] + m_slice[:, FEAT:]).reshape(half_rows, 2 * FEAT)
     columns = lax.axis_index(HEAD) * lax.axis_size(("grp", "seq_0"))
     columns = (columns + lax.axis_index(("grp", "seq_0"))) * depth
     gain_own = lax.dynamic_slice_in_dim(norm_gain, columns, depth, 0)
@@ -312,19 +331,20 @@
     embed_own = jnp.concatenate(
         [lax.dynamic_slice_in_dim(embed_own, b_at + k, b_each, 0) for k in (0, FEAT // 2)], axis=0
     )
+
+    patch = latent_patches(parts, conv_bias)
+    token_order, m_slice, patch, embed_late = lax.optimization_barrier(
+        (token_order, m_slice, patch, embed_weight)
+    )
     gram = lax.dot_general(
-        embed_weight, embed_weight, (((1,), (1,)), ((), ())), preferred_element_type=F32
+        embed_late, embed_late, (((1,), (1,)), ((), ())), preferred_element_type=F32
     ) * (1.0 / D)
-
-    patch = encode_tile(features[0, 0], conv_weight, conv_bias)
-    token_order, grad_out, patch = lax.optimization_barrier((token_order, grad_out, patch))
     own_rows = patch.shape[0]
     arrived = from_everyone(jnp.concatenate([patch, *two(m_slice)], axis=0), "seq_1")
     far_count, head_count = lax.axis_size("seq_0"), lax.axis_size(HEAD)
     plane = far_count * head_count
-    mine = w_blocks.reshape(head_count, -1, far_count, rows_each * 2, depth)
-    mine = jnp.swapaxes(lax.dynamic_index_in_dim(mine, lax.axis_index("grp"), 1, False), 0, 1)
-    mine = mine.reshape(plane, rows_each * 2, depth)
+    mine = w_blocks.reshape(head_count, -1, far_count, rows_each, depth)
+    mine = jnp.transpose(mine, (2, 0, 1, 3, 4)).reshape(plane, rows_each * 2, depth)
     mine = jnp.pad(mine, ((0, 0), (0, 0), (0, 2 * FEAT - depth)))
     latents = arrived[:, :own_rows].reshape(1, -1, 2 * FEAT)
     pairs_each = latents.shape[1]
@@ -332,9 +352,11 @@
     every = lax.all_to_all(
         jnp.concatenate([latents, mine], axis=1), ("seq_0", *HEAD), 0, 0, tiled=True
     )
-    w_own = every[:, pairs_each:, :depth].reshape(-1, depth)
-    m_high = arrived[:, own_rows : own_rows + rows_each].reshape(rows, 2 * FEAT)
-    m_low = arrived[:, own_rows + rows_each :].reshape(rows, 2 * FEAT)
+    m_half = arrived[:, own_rows:]
+    grad_out, m_half = lax.optimization_barrier((grad_out, m_half))
+    m_both = both_halves(m_half, m_half, 1).reshape(near_count, 2, 2, half_rows, 2 * FEAT)
+    m_high = m_both[:, :, 0].reshape(rows, 2 * FEAT)
+    m_low = m_both[:, :, 1].reshape(rows, 2 * FEAT)
 
     per_patch_row = own_rows
     order = in_order(token_order, lax.ppermute(token_order, "seq_0", [(0, 1), (1, 0)]))
@@ -359,6 +381,14 @@
         jnp.concatenate([other, mine], axis=1),
     )[None]
 
+    w_own, at = lax.optimization_barrier((every, at))
+    w_own = w_own[:, pairs_each:].reshape(plane, 2, rows_each, 2 * FEAT)
+    w_own = both_halves(
+        lax.dynamic_index_in_dim(w_own, clip, 1, False),
+        lax.dynamic_index_in_dim(w_own, 1 - clip, 1, False),
+        1,
+    )
+    w_own = w_own.reshape(-1, 2 * FEAT)[:, :depth]
     first, second = jnp.split(b, 2, axis=0)
     b = jnp.concatenate([first, second], axis=1)
     at = jnp.concatenate(

time: 162 us -> 174 us (1.074)
  starting transfers between devices: 58 us -> 78.7 us
  blocking collectives: 19.1 us -> 0 us
  waiting for transfers between devices: 57.3 us -> 64.9 us
    all_to_all x1 -> x0, blocking collectives: 19.1 us -> none  [per_device(): at = jnp.sum(lax.all_to_all(at, 'seq_1', 0, 0, tiled=True), axis=0)]
    all_to_all x1, waiting for transfers between devices: 11.1 us -> 0.01 us  [per_device(): lax.all_to_all(jnp.concatenate([latents, mine], axis=1), ('seq_0', *HEAD)...]
    all_to_all x1 -> x2, waiting for transfers between devices: 11.8 us -> 22.9 us  [the longest x1 12.8 us: per_device(): w_blocks = lax.all_to_all(w, 'seq_1', 0, 0, tiled=True)]
    ppermute x0 -> x2, starting transfers between devices: none -> 8.64 us  [both_halves(): other = lax.ppermute(given, 'grp', [(0, 1), (1, 0)])]
    all_to_all x1 -> x2, starting transfers between devices: 12.4 us -> 18.3 us  [the longest x1 13.8 us: per_device(): w_blocks = lax.all_to_all(w, 'seq_1', 0, 0, tiled=True)]
    ppermute x1 -> x2, starting transfers between devices: 3.48 us -> 7.36 us  [swapped(): return (mine, lax.ppermute(given, 'seq_0', [(0, 1), (1, 0)]))]
    ppermute x1 -> x2, waiting for transfers between devices: 0.01 us -> 2.03 us  [swapped(): return (mine, lax.ppermute(given, 'seq_0', [(0, 1), (1, 0)]))]
    ppermute x0 -> x2, waiting for transfers between devices: none -> 1.94 us  [both_halves(): other = lax.ppermute(given, 'grp', [(0, 1), (1, 0)])]
  transfers between devices with their start and end apart: 13 -> 17, of which waited for: 7 -> 11; matrix products, arithmetic and copies ran while one was open for 4% -> 3% of each run, Pallas kernels for 0% -> 1%
where the time goes in v11:
time: 174 us; the launch traced here: 173 us
  starting transfers between devices  78.7 us (45%)
  waiting for transfers between devices  64.9 us (37%)
  Pallas kernels  14.1 us (8%)
  local copies, waits for them, and re-layouts  8.89 us (5%)
  other arithmetic  3.77 us (2%)
    all_to_all x4, waiting for transfers between devices, from_everyone(): return lax.all_to_all(copies, axis, split_axis=0, concat_axis=0, tiled=True)  35 us
    all_to_all x4, starting transfers between devices, from_everyone(): return lax.all_to_all(copies, axis, split_axis=0, concat_axis=0, tiled=True)  18.7 us
    ppermute x4, starting transfers between devices, shifted(): lax.ppermute(value, axis, [(source, source + steps) for source in range(l...  14.5 us
    all_to_all x1, starting transfers between devices, per_device(): w_blocks = lax.all_to_all(w, 'seq_1', 0, 0, tiled=True)  13.8 us
    all_to_all x1, waiting for transfers between devices, per_device(): w_blocks = lax.all_to_all(w, 'seq_1', 0, 0, tiled=True)  12.8 us
    pallas_call x1, Pallas kernels, attention(): pl.pallas_call(attention_kernel, out_shape=[jax.ShapeDtypeStruct(cot.shap...  11.8 us
    all_to_all x1, waiting for transfers between devices, per_device(): at = jnp.sum(lax.all_to_all(at, 'seq_1', 0, 0, tiled=True), axis=0)  10.1 us
    ppermute x2, starting transfers between devices, both_halves(): other = lax.ppermute(given, 'grp', [(0, 1), (1, 0)])  8.64 us
  transfers between devices with their start and end apart: 17, of which 11 were waited for; matrix products, arithmetic and copies ran while one was open for 3% of the time, Pallas kernels for 1%

profile of v11, /device:TPU:32, one launch (start us, length us, event | category | flops | bytes accessed | tf_op | source)
XLA Modules:
  0.0 172.6 jit_solution(15525089525435993468)
XLA Ops:
  2.3 3.5 %collective-permute-start = (bf16[1,16,12,96]{3,1,2,0:T(8,128)(2,1)S(1)}, bf16[1,16,12,96]{3,1,2,0:T(8,128)(2,1)S(1)}, u32[]{:S(2)}, u32[]{:S(2)}) collective-permute-start(bf16[1,16,12,96]{3,1,2,0:T(8,128)(2,1)S(1)} %bitcast.98), channel_id=1, source_target_pairs={{0,128},{128,0},{1,129},{129,1},{2,130},{130,2},{3,131},{131,3},{4... | collective-permute-start | bytes 110600 | tf_op jit(solution)/shard_map/ppermute | solution.py:297
  5.9 2.3 %taps.1 = f32[3,16,128]{2,1,0:T(8,128)} custom-call(bf16[64,512]{1,0:T(8,128)(2,1)} %bitcast.96, bf16[432,512]{1,0:T(8,128)(2,1)} %bitcast.84), custom_call_target="tpu_custom_call" | custom-call | tf_op jit(solution)/shard_map/taps/pallas_call | solution.py:94
  9.2 5.2 %collective-permute-start.2 = (f32[16,128]{1,0:T(8,128)S(1)}, f32[16,128]{1,0:T(8,128)S(1)}, u32[]{:S(2)}, u32[]{:S(2)}) collective-permute-start(f32[16,128]{1,0:T(8,128)S(1)} %get-tuple-element.67), channel_id=1, source_target_pairs={{0,16},{8,24},{16,32},{24,40},{32,48},{40,56},{48,64},{56,72},{64,... | collective-permute-start | bytes 24584 | tf_op jit(solution)/shard_map/ppermute | solution.py:23
  14.4 5.0 %collective-permute-start.1 = (f32[16,128]{1,0:T(8,128)S(1)}, f32[16,128]{1,0:T(8,128)S(1)}, u32[]{:S(2)}, u32[]{:S(2)}) collective-permute-start(f32[16,128]{1,0:T(8,128)S(1)} %get-tuple-element.66), channel_id=1, source_target_pairs={{0,8},{8,16},{16,24},{24,32},{32,40},{40,48},{48,56},{56,64},{64,7... | collective-permute-start | bytes 24584 | tf_op jit(solution)/shard_map/ppermute | solution.py:23
  22.8 3.0 %collective-permute-start.3 = (f32[16,128]{1,0:T(8,128)S(1)}, f32[16,128]{1,0:T(8,128)S(1)}, u32[]{:S(2)}, u32[]{:S(2)}) collective-permute-start(f32[16,128]{1,0:T(8,128)S(1)} %fusion.31), channel_id=1, source_target_pairs={{0,1},{1,2},{2,3},{3,4},{4,5},{5,6},{6,7},{8,9},{9,10},{10,11},{11... | collective-permute-start | bytes 24584 | tf_op jit(solution)/shard_map/ppermute | solution.py:23
  26.7 13.8 %all-to-all-start = ((bf16[16,24,96]{2,1,0:T(8,128)(2,1)}), bf16[16,24,96]{2,1,0:T(8,128)(2,1)S(1)}, u32[]{:S(2)}, u32[]{:S(2)}) async-start(bf16[16,24,96]{2,1,0:T(8,128)(2,1)} %copy.225), calls=%async_computation | async-start | bytes 196608 | tf_op jit(solution)/shard_map/all_to_all | solution.py:317
  40.8 12.8 %all-to-all-done = bf16[16,24,96]{2,1,0:T(8,128)(2,1)S(1)} async-done(((bf16[16,24,96]{2,1,0:T(8,128)(2,1)}), bf16[16,24,96]{2,1,0:T(8,128)(2,1)S(1)}, u32[]{:S(2)}, u32[]{:S(2)}) %all-to-all-start) | async-done | bytes 73760 | tf_op jit(solution)/shard_map/all_to_all | solution.py:317
  54.9 5.4 %all-to-all-start.1 = ((bf16[16,20,128]{2,1,0:T(8,128)(2,1)}), bf16[16,20,128]{2,1,0:T(8,128)(2,1)S(1)}, u32[]{:S(2)}, u32[]{:S(2)}) async-start(bf16[16,20,128]{2,1,0:T(8,128)(2,1)} %broadcast_in_dim.22), calls=%async_computation.1 | async-start | bytes 196608 | tf_op jit(solution)/shard_map/all_to_all | solution.py:28
  60.4 3.4 %collective-permute-start.6 = (s32[128]{0:T(128)S(1)}, s32[128]{0:T(128)S(1)}, u32[]{:S(2)}, u32[]{:S(2)}) collective-permute-start(s32[128]{0:T(128)S(1)} %copy-done.4), channel_id=1, source_target_pairs={{0,128},{128,0},{1,129},{129,1},{2,130},{130,2},{3,131},{131,3},{4... | collective-permute-start | bytes 1544 | tf_op jit(solution)/shard_map/ppermute | solution.py:362
  66.0 7.6 %all-to-all-done.1 = bf16[16,20,128]{2,1,0:T(8,128)(2,1)S(1)} async-done(((bf16[16,20,128]{2,1,0:T(8,128)(2,1)}), bf16[16,20,128]{2,1,0:T(8,128)(2,1)S(1)}, u32[]{:S(2)}, u32[]{:S(2)}) %all-to-all-start.1) | async-done | bytes 81952 | tf_op jit(solution)/shard_map/all_to_all | solution.py:28
  74.6 5.3 %all-to-all-start.2 = ((bf16[16,152,128]{2,1,0:T(8,128)(2,1)}), bf16[16,152,128]{2,1,0:T(8,128)(2,1)S(1)}, u32[]{:S(2)}, u32[]{:S(2)}) async-start(bf16[16,152,128]{2,1,0:T(8,128)(2,1)} %fusion.6), calls=%async_computation.2 | async-start | bytes 1245184 | tf_op jit(solution)/shard_map/all_to_all | solution.py:352
  79.9 3.8 %collective-permute-start.7 = (bf16[128,128]{1,0:T(8,128)(2,1)S(1)}, bf16[128,128]{1,0:T(8,128)(2,1)S(1)}, u32[]{:S(2)}, u32[]{:S(2)}) collective-permute-start(bf16[128,128]{1,0:T(8,128)(2,1)S(1)} %get-tuple-element.63), channel_id=1, source_target_pairs={{0,128},{128,0},{1,129},{129,1},{2,130},{130,2},{3,131},{131,3},{4... | collective-permute-start | bytes 98312 | tf_op jit(solution)/shard_map/ppermute | solution.py:297
  84.2 4.8 %collective-permute-start.5 = (bf16[16,12,128]{2,1,0:T(8,128)(2,1)S(1)}, bf16[16,12,128]{2,1,0:T(8,128)(2,1)S(1)}, u32[]{:S(2)}, u32[]{:S(2)}) collective-permute-start(bf16[16,12,128]{2,1,0:T(8,128)(2,1)S(1)} %slice.102), channel_id=1, source_target_pairs={{0,256},{256,0},{1,257},{257,1},{2,258},{258,2},{3,259},{259,3},{4... | collective-permute-start | bytes 147464 | tf_op jit(solution)/shard_map/ppermute | solution.py:306
  93.1 11.8 %attention.1 = (bf16[2,256,64]{2,1,0:T(8,128)(2,1)S(1)}, f32[192,128]{1,0:T(8,128)S(1)}, f32[64,64]{1,0:T(8,128)S(1)}) custom-call(bf16[16,152,128]{2,1,0:T(8,128)(2,1)S(1)} %all-to-all-done.2.x_ref, bf16[192,128]{1,0:T(8,128)(2,1)S(1)} %reshape_squeeze.10.high_ref, bf16[192,128]{1,0:T(8,128)(2,1)S(1)} %reshape_squeeze.11.low_ref, ...), custom_call_target="tpu_custom_call" | custom-call | tf_op jit(solution)/shard_map/attention/pallas_call | solution.py:261
  105.7 4.5 %all-to-all-start.3 = ((f32[16,14,128]{2,1,0:T(8,128)}), f32[16,14,128]{2,1,0:T(8,128)S(1)}, u32[]{:S(2)}, u32[]{:S(2)}) async-start(f32[16,14,128]{2,1,0:T(8,128)} %pad_maximum_fusion), calls=%async_computation.3 | async-start | bytes 262144 | tf_op jit(solution)/shard_map/all_to_all | solution.py:401
  110.2 3.8 %collective-permute-start.9 = (bf16[16,12,128]{2,0,1:T(8,128)(2,1)S(1)}, bf16[16,12,128]{2,0,1:T(8,128)(2,1)S(1)}, u32[]{:S(2)}, u32[]{:S(2)}) collective-permute-start(bf16[16,12,128]{2,0,1:T(8,128)(2,1)S(1)} %get-tuple-element.57), channel_id=1, source_target_pairs={{0,256},{256,0},{1,257},{257,1},{2,258},{258,2},{3,259},{259,3},{4... | collective-permute-start | bytes 147464 | tf_op jit(solution)/shard_map/ppermute | solution.py:306
  114.1 10.1 %all-to-all-done.3 = f32[16,14,128]{2,1,0:T(8,128)S(1)} async-done(((f32[16,14,128]{2,1,0:T(8,128)}), f32[16,14,128]{2,1,0:T(8,128)S(1)}, u32[]{:S(2)}, u32[]{:S(2)}) %all-to-all-start.3) | async-done | bytes 114720 | tf_op jit(solution)/shard_map/all_to_all | solution.py:401
  124.9 5.5 %all-to-all-start.4 = ((f32[32,14,128]{2,1,0:T(8,128)}), f32[32,14,128]{2,1,0:T(8,128)S(1)}, u32[]{:S(2)}, u32[]{:S(2)}) async-start(f32[32,14,128]{2,1,0:T(8,128)} %broadcast_in_dim.25), calls=%async_computation.4 | async-start | bytes 524288 | tf_op jit(solution)/shard_map/all_to_all | solution.py:28
  130.7 8.7 %all-to-all-done.4 = f32[32,14,128]{2,1,0:T(8,128)S(1)} async-done(((f32[32,14,128]{2,1,0:T(8,128)}), f32[32,14,128]{2,1,0:T(8,128)S(1)}, u32[]{:S(2)}, u32[]{:S(2)}) %all-to-all-start.4) | async-done | bytes 229408 | tf_op jit(solution)/shard_map/all_to_all | solution.py:28
  140.9 4.5 %all-to-all-start.5 = ((bf16[16,16,384]{2,1,0:T(8,128)(2,1)}), bf16[16,16,384]{2,1,0:T(8,128)(2,1)S(1)}, u32[]{:S(2)}, u32[]{:S(2)}) async-start(bf16[16,16,384]{2,1,0:T(8,128)(2,1)} %broadcast_in_dim.26), calls=%async_computation.5 | async-start | bytes 393216 | tf_op jit(solution)/shard_map/all_to_all | solution.py:28
  145.5 2.5 %collective-permute-start.8 = (bf16[128,128]{0,1:T(8,128)(2,1)S(1)}, bf16[128,128]{0,1:T(8,128)(2,1)S(1)}, u32[]{:S(2)}, u32[]{:S(2)}) collective-permute-start(bf16[128,128]{0,1:T(8,128)(2,1)S(1)} %bitcast.99), channel_id=1, source_target_pairs={{0,128},{128,0},{1,129},{129,1},{2,130},{130,2},{3,131},{131,3},{4... | collective-permute-start | bytes 98312 | tf_op jit(solution)/shard_map/ppermute | solution.py:377
  148.1 13.7 %all-to-all-done.5 = bf16[16,16,384]{2,1,0:T(8,128)(2,1)S(1)} async-done(((bf16[16,16,384]{2,1,0:T(8,128)(2,1)}), bf16[16,16,384]{2,1,0:T(8,128)(2,1)S(1)}, u32[]{:S(2)}, u32[]{:S(2)}) %all-to-all-start.5) | async-done | bytes 196640 | tf_op jit(solution)/shard_map/all_to_all | solution.py:28
  162.5 3.3 %all-to-all-start.6 = ((f32[4,16,384]{2,1,0:T(8,128)}), f32[4,16,384]{2,1,0:T(8,128)S(1)}, u32[]{:S(2)}, u32[]{:S(2)}) async-start(f32[4,16,384]{2,1,0:T(8,128)} %broadcast_in_dim.27), calls=%async_computation.6 | async-start | bytes 196608 | tf_op jit(solution)/shard_map/all_to_all | solution.py:28
  166.6 5.0 %all-to-all-done.6 = f32[4,16,384]{2,1,0:T(8,128)S(1)} async-done(((f32[4,16,384]{2,1,0:T(8,128)}), f32[4,16,384]{2,1,0:T(8,128)S(1)}, u32[]{:S(2)}, u32[]{:S(2)}) %all-to-all-start.6) | async-done | bytes 98336 | tf_op jit(solution)/shard_map/all_to_all | solution.py:28
  (105 shorter events, 22.0 us)
Async XLA Ops:
  2.3 23.5 %copy-start = (bf16[64,3072]{1,0:T(8,128)(2,1)S(1)}, bf16[64,3072]{1,0:T(8,128)(2,1)}, u32[]{:S(2)}) copy-start(bf16[64,3072]{1,0:T(8,128)(2,1)} %param.12) | copy-start | bytes 1179652
  2.3 23.5 %copy-start.2 = (f32[3072]{0:T(1024)S(1)}, f32[3072]{0:T(1024)}, u32[]{:S(2)}) copy-start(f32[3072]{0:T(1024)} %param.13) | copy-start | bytes 36868
  2.3 6.1 %collective-permute-start = (bf16[1,16,12,96]{3,1,2,0:T(8,128)(2,1)S(1)}, bf16[1,16,12,96]{3,1,2,0:T(8,128)(2,1)S(1)}, u32[]{:S(2)}, u32[]{:S(2)}) collective-permute-start(bf16[1,16,12,96]{3,1,2,0:T(8,128)(2,1)S(1)} %bitcast.98), channel_id=1, source_target_pairs={{0,128},{128,0},{1,129},{129,1},{2,130},{130,2},{3,131},{131,3},{4... | collective-permute-start | bytes 110600 | tf_op jit(solution)/shard_map/ppermute | solution.py:297
  8.5 17.5 %copy-start.3 = (f32[16]{0:T(128)S(1)}, f32[16]{0:T(128)}, u32[]{:S(2)}) copy-start(f32[16]{0:T(128)} %param.10) | copy-start | bytes 196
  9.2 10.2 %collective-permute-start.2 = (f32[16,128]{1,0:T(8,128)S(1)}, f32[16,128]{1,0:T(8,128)S(1)}, u32[]{:S(2)}, u32[]{:S(2)}) collective-permute-start(f32[16,128]{1,0:T(8,128)S(1)} %get-tuple-element.67), channel_id=1, source_target_pairs={{0,16},{8,24},{16,32},{24,40},{32,48},{40,56},{48,64},{56,72},{64,... | collective-permute-start | bytes 24584 | tf_op jit(solution)/shard_map/ppermute | solution.py:23
  14.4 6.4 %collective-permute-start.1 = (f32[16,128]{1,0:T(8,128)S(1)}, f32[16,128]{1,0:T(8,128)S(1)}, u32[]{:S(2)}, u32[]{:S(2)}) collective-permute-start(f32[16,128]{1,0:T(8,128)S(1)} %get-tuple-element.66), channel_id=1, source_target_pairs={{0,8},{8,16},{16,24},{24,32},{32,40},{40,48},{48,56},{56,64},{64,7... | collective-permute-start | bytes 24584 | tf_op jit(solution)/shard_map/ppermute | solution.py:23
  21.5 19.1 %collective-permute-start.4 = (f32[16,128]{1,0:T(8,128)S(1)}, f32[16,128]{1,0:T(8,128)S(1)}, u32[]{:S(2)}, u32[]{:S(2)}) collective-permute-start(f32[16,128]{1,0:T(8,128)S(1)} %fusion.31), channel_id=1, source_target_pairs={{1,0},{2,1},{3,2},{4,3},{5,4},{6,5},{7,6},{9,8},{10,9},{11,10},{12... | collective-permute-start | bytes 24584 | tf_op jit(solution)/shard_map/ppermute | solution.py:23
  22.8 17.7 %collective-permute-start.3 = (f32[16,128]{1,0:T(8,128)S(1)}, f32[16,128]{1,0:T(8,128)S(1)}, u32[]{:S(2)}, u32[]{:S(2)}) collective-permute-start(f32[16,128]{1,0:T(8,128)S(1)} %fusion.31), channel_id=1, source_target_pairs={{0,1},{1,2},{2,3},{3,4},{4,5},{5,6},{6,7},{8,9},{9,10},{10,11},{11... | collective-permute-start | bytes 24584 | tf_op jit(solution)/shard_map/ppermute | solution.py:23
  26.7 26.8 %all-to-all-start = ((bf16[16,24,96]{2,1,0:T(8,128)(2,1)}), bf16[16,24,96]{2,1,0:T(8,128)(2,1)S(1)}, u32[]{:S(2)}, u32[]{:S(2)}) async-start(bf16[16,24,96]{2,1,0:T(8,128)(2,1)} %copy.225), calls=%async_computation | async-start | bytes 196608 | tf_op jit(solution)/shard_map/all_to_all | solution.py:317
  53.8 6.6 %copy-start.4 = (s32[128]{0:T(128)S(1)}, s32[128]{0:T(128)}, u32[]{:S(2)}) copy-start(s32[128]{0:T(128)} %param.11) | copy-start | bytes 1540
  54.9 18.7 %all-to-all-start.1 = ((bf16[16,20,128]{2,1,0:T(8,128)(2,1)}), bf16[16,20,128]{2,1,0:T(8,128)(2,1)S(1)}, u32[]{:S(2)}, u32[]{:S(2)}) async-start(bf16[16,20,128]{2,1,0:T(8,128)(2,1)} %broadcast_in_dim.22), calls=%async_computation.1 | async-start | bytes 196608 | tf_op jit(solution)/shard_map/all_to_all | solution.py:28
  60.4 5.4 %collective-permute-start.6 = (s32[128]{0:T(128)S(1)}, s32[128]{0:T(128)S(1)}, u32[]{:S(2)}, u32[]{:S(2)}) collective-permute-start(s32[128]{0:T(128)S(1)} %copy-done.4), channel_id=1, source_target_pairs={{0,128},{128,0},{1,129},{129,1},{2,130},{130,2},{3,131},{131,3},{4... | collective-permute-start | bytes 1544 | tf_op jit(solution)/shard_map/ppermute | solution.py:362
  74.6 5.3 %copy-start.1 = (bf16[1,128,256]{2,1,0:T(8,128)(2,1)S(1)}, bf16[1,128,256]{2,1,0:T(8,128)(2,1)}, u32[]{:S(2)}) copy-start(bf16[1,128,256]{2,1,0:T(8,128)(2,1)} %param.15) | copy-start | bytes 196612
  74.6 18.5 %all-to-all-start.2 = ((bf16[16,152,128]{2,1,0:T(8,128)(2,1)}), bf16[16,152,128]{2,1,0:T(8,128)(2,1)S(1)}, u32[]{:S(2)}, u32[]{:S(2)}) async-start(bf16[16,152,128]{2,1,0:T(8,128)(2,1)} %fusion.6), calls=%async_computation.2 | async-start | bytes 1245184 | tf_op jit(solution)/shard_map/all_to_all | solution.py:352
  79.9 10.9 %collective-permute-start.7 = (bf16[128,128]{1,0:T(8,128)(2,1)S(1)}, bf16[128,128]{1,0:T(8,128)(2,1)S(1)}, u32[]{:S(2)}, u32[]{:S(2)}) collective-permute-start(bf16[128,128]{1,0:T(8,128)(2,1)S(1)} %get-tuple-element.63), channel_id=1, source_target_pairs={{0,128},{128,0},{1,129},{129,1},{2,130},{130,2},{3,131},{131,3},{4... | collective-permute-start | bytes 98312 | tf_op jit(solution)/shard_map/ppermute | solution.py:297
  84.2 8.7 %collective-permute-start.5 = (bf16[16,12,128]{2,1,0:T(8,128)(2,1)S(1)}, bf16[16,12,128]{2,1,0:T(8,128)(2,1)S(1)}, u32[]{:S(2)}, u32[]{:S(2)}) collective-permute-start(bf16[16,12,128]{2,1,0:T(8,128)(2,1)S(1)} %slice.102), channel_id=1, source_target_pairs={{0,256},{256,0},{1,257},{257,1},{2,258},{258,2},{3,259},{259,3},{4... | collective-permute-start | bytes 147464 | tf_op jit(solution)/shard_map/ppermute | solution.py:306
  105.7 18.4 %all-to-all-start.3 = ((f32[16,14,128]{2,1,0:T(8,128)}), f32[16,14,128]{2,1,0:T(8,128)S(1)}, u32[]{:S(2)}, u32[]{:S(2)}) async-start(f32[16,14,128]{2,1,0:T(8,128)} %pad_maximum_fusion), calls=%async_computation.3 | async-start | bytes 262144 | tf_op jit(solution)/shard_map/all_to_all | solution.py:401
  110.2 20.4 %collective-permute-start.9 = (bf16[16,12,128]{2,0,1:T(8,128)(2,1)S(1)}, bf16[16,12,128]{2,0,1:T(8,128)(2,1)S(1)}, u32[]{:S(2)}, u32[]{:S(2)}) collective-permute-start(bf16[16,12,128]{2,0,1:T(8,128)(2,1)S(1)} %get-tuple-element.57), channel_id=1, source_target_pairs={{0,256},{256,0},{1,257},{257,1},{2,258},{258,2},{3,259},{259,3},{4... | collective-permute-start | bytes 147464 | tf_op jit(solution)/shard_map/ppermute | solution.py:306
  124.9 14.5 %all-to-all-start.4 = ((f32[32,14,128]{2,1,0:T(8,128)}), f32[32,14,128]{2,1,0:T(8,128)S(1)}, u32[]{:S(2)}, u32[]{:S(2)}) async-start(f32[32,14,128]{2,1,0:T(8,128)} %broadcast_in_dim.25), calls=%async_computation.4 | async-start | bytes 524288 | tf_op jit(solution)/shard_map/all_to_all | solution.py:28
  140.9 20.9 %all-to-all-start.5 = ((bf16[16,16,384]{2,1,0:T(8,128)(2,1)}), bf16[16,16,384]{2,1,0:T(8,128)(2,1)S(1)}, u32[]{:S(2)}, u32[]{:S(2)}) async-start(bf16[16,16,384]{2,1,0:T(8,128)(2,1)} %broadcast_in_dim.26), calls=%async_computation.5 | async-start | bytes 393216 | tf_op jit(solution)/shard_map/all_to_all | solution.py:28
  145.5 20.3 %collective-permute-start.8 = (bf16[128,128]{0,1:T(8,128)(2,1)S(1)}, bf16[128,128]{0,1:T(8,128)(2,1)S(1)}, u32[]{:S(2)}, u32[]{:S(2)}) collective-permute-start(bf16[128,128]{0,1:T(8,128)(2,1)S(1)} %bitcast.99), channel_id=1, source_target_pairs={{0,128},{128,0},{1,129},{129,1},{2,130},{130,2},{3,131},{131,3},{4... | collective-permute-start | bytes 98312 | tf_op jit(solution)/shard_map/ppermute | solution.py:377
  162.5 9.1 %all-to-all-start.6 = ((f32[4,16,384]{2,1,0:T(8,128)}), f32[4,16,384]{2,1,0:T(8,128)S(1)}, u32[]{:S(2)}, u32[]{:S(2)}) async-start(f32[4,16,384]{2,1,0:T(8,128)} %broadcast_in_dim.27), calls=%async_computation.6 | async-start | bytes 196608 | tf_op jit(solution)/shard_map/all_to_all | solution.py:28
